TPU v7x, 32 devices: a whole 2x2x4 slice. The times are simulated.
32 devices in a mesh: groups: 2 (over y), row: 8 (over z, core), col: 2 (over x), chan: 1.
Axes of the slice: x: 2, y: 2, z: 4, core: 2. Of those that a mesh axis runs over, the one named last changes fastest.
Arguments:
- pair_rep: bfloat16 [320, 160, 128], P(('groups', 'row'), 'col'), parts along dimension 0, may hold values from -6 to 6
- residue_mask: int32 [320], P('groups'), parts along dimension 0, may hold values 0 or 1
- ln_gain: float32 [128], replicated, may hold values from 0.1 to 1.9
- left_proj: bfloat16 [128, 128], replicated, may hold values from -0.5 to 0.5
- left_gate: bfloat16 [128, 128], replicated, may hold values from -0.5 to 0.5
- right_proj: bfloat16 [128, 128], replicated, may hold values from -0.5 to 0.5
- right_gate: bfloat16 [128, 128], replicated, may hold values from -0.5 to 0.5
- hidden_gain: float32 [128], replicated, may hold values from 0.1 to 1.9
- out_proj: bfloat16 [128, 128], replicated, may hold values from -0.5 to 0.5
- out_gate: bfloat16 [128, 128], replicated, may hold values from -0.5 to 0.5
Outputs:
- update: bfloat16 [320, 160, 128], P(('groups', 'row'), ('col', 'chan')), parts along dimension 0
There are 2 independent parts, one for each index of `groups`. A program takes and returns all parts, laid end to end along the dimension named above; an argument that names none is the same for every part. Nothing has to cross between parts.
All inputs are finite; a program needn't handle non-finite values.
Results may differ from a plain program's by a relative error of at most 0.015.
Values may be sent and summed in bfloat16 or wider, within the bound.
No kernel may reach another device: no remote copies, remote signals or barrier semaphores. Data moves between devices by JAX's collectives and lax.ppermute only.
A program may use at most 128 MiB of HBM per device.

v0:
```python
import jax
import jax.numpy as jnp
from jax import lax
from jax.sharding import PartitionSpec as P


def layer_norm(values, gain):
    center = jnp.mean(values, axis=-1, keepdims=True)
    spread = jnp.mean(jnp.square(values - center), axis=-1, keepdims=True)
    return (values - center) * lax.rsqrt(spread + 1e-05) * gain


def gated_pair(normed_pair, matrices, pair_mask):
    tile_rows, tile_cols, pair_width = normed_pair.shape
    stacked = jnp.concatenate(matrices, axis=1)
    width = matrices[0].shape[1]
    projected = jnp.dot(
        normed_pair.reshape(tile_rows * tile_cols, pair_width),
        stacked,
        preferred_element_type=jnp.float32,
    )
    projected = projected.reshape(tile_rows, tile_cols, 4, width)
    masked = pair_mask[:, :, None]
    left_act = (masked * jax.nn.sigmoid(projected[:, :, 1]) * projected[:, :, 0]).astype(
        jnp.bfloat16
    )
    right_act = (masked * jax.nn.sigmoid(projected[:, :, 3]) * projected[:, :, 2]).astype(
        jnp.bfloat16
    )
    return (left_act, right_act)


def finish_output(normed_hidden, normed_pair, out_proj, out_gate):
    projected = jnp.einsum(
        "ijc,cd->ijd", normed_hidden, out_proj, preferred_element_type=jnp.float32
    )
    gating = jax.nn.sigmoid(
        jnp.einsum("ijc,cd->ijd", normed_pair, out_gate, preferred_element_type=jnp.float32)
    )
    return (gating * projected).astype(jnp.bfloat16)


def local(
    pair_rep,
    residue_mask,
    ln_gain,
    left_proj,
    left_gate,
    right_proj,
    right_gate,
    hidden_gain,
    out_proj,
    out_gate,
):
    tile_rows, tile_cols, pair_width = pair_rep.shape
    hidden_width = left_proj.shape[1]
    core_count = lax.axis_size("chan")
    core_index = lax.axis_index("chan")
    row_index = lax.axis_index("row")
    col_index = lax.axis_index("col")
    mask_float = residue_mask.astype(jnp.float32)
    row_mask = lax.dynamic_slice_in_dim(mask_float, row_index * tile_rows, tile_rows)
    core_cols = tile_cols // core_count
    matrices_all = (left_proj, left_gate, right_proj, right_gate)
    normed_pair = layer_norm(pair_rep.astype(jnp.float32), ln_gain).astype(jnp.bfloat16)
    col_mask = lax.dynamic_slice_in_dim(mask_float, col_index * tile_cols, tile_cols)
    pair_mask = row_mask[:, None] * col_mask[None, :]
    half_width = hidden_width // core_count
    matrices = tuple(
        (
            lax.dynamic_slice_in_dim(matrix, core_index * half_width, half_width, 1)
            for matrix in matrices_all
        )
    )
    left_act, right_act = gated_pair(normed_pair, matrices, pair_mask)
    partial_sums = jnp.einsum(
        "ikc,jkc->ijc",
        left_act,
        lax.all_gather(right_act, "row", axis=0, tiled=True),
        preferred_element_type=jnp.float32,
    )
    tri_sum = lax.psum_scatter(
        partial_sums.astype(jnp.bfloat16), "col", scatter_dimension=1, tiled=True
    ).astype(jnp.float32)
    full_hidden = lax.all_to_all(
        tri_sum.astype(jnp.bfloat16), "chan", split_axis=1, concat_axis=2, tiled=True
    ).astype(tri_sum.dtype)
    normed_hidden = layer_norm(full_hidden, hidden_gain).astype(jnp.bfloat16)
    own_pair = lax.dynamic_slice_in_dim(normed_pair, core_index * core_cols, core_cols, 1)
    return finish_output(normed_hidden, own_pair, out_proj, out_gate)


def solution(mesh):
    in_specs = (
        P(("groups", "row"), "col", None),
        P("groups"),
        P(),
        P(),
        P(),
        P(),
        P(),
        P(),
        P(),
        P(),
    )
    out_specs = P(("groups", "row"), ("col", "chan"), None)
    return jax.shard_map(local, mesh=mesh, in_specs=in_specs, out_specs=out_specs, check_vma=False)
```

profile of v0, /device:TPU:0, one launch (start us, length us, event | category | flops | bytes accessed | tf_op | source)
XLA Modules:
  0.0 102.9 jit_solution(5138537153216289887)
XLA Ops:
  6.5 0.0 copy-start
  6.5 0.0 all-gather.2.cloned.1.call-start
  6.5 0.7 convert_element_type.34
  7.2 0.1 dynamic_slice.4
  7.3 0.1 dynamic_slice.5
  7.4 1.2 %convert_reduce_fusion.1 = f32[20,80]{1,0:T(8,128)S(1)} fusion(bf16[20,80,128]{2,1,0:T(8,128)(2,1)} %param.10), kind=kLoop, calls=%fused_computation.13 | loop fusion | flops 408000 | bytes 416000 | tf_op jit(solution)/shard_map/reduce_sum | solution.py:8
  8.6 1.7 %fusion.12 = f32[20,80]{1,0:T(8,128)S(1)} fusion(bf16[20,80,128]{2,1,0:T(8,128)(2,1)} %param.10, f32[20,80]{1,0:T(8,128)S(1)} %broadcast_multiply_fusion.2), kind=kLoop, calls=%fused_computation.19 | loop fusion | flops 817600 | bytes 422400 | tf_op jit(solution)/shard_map/reduce_sum | solution.py:9
  10.3 0.8 maximum_bitcast_fusion
  11.2 0.1 copy.38
  11.3 0.1 broadcast_multiply_fusion
  11.4 1.7 %fusion.31 = f32[20,80,4,128]{3,1,2,0:T(8,128)S(1)} fusion(bf16[4,128,128,1]{2,1,0,3:T(8,128)(2,1)S(1)} %bitcast.79, bf16[20,80,128]{2,1,0:T(8,128)(2,1)} %param.10, f32[128]{0:T(128)} %param.12, f32[20,80]{1,0:T(8,128)S(1)} %add_rsqrt_fusion.1, f32[20,80]{1,0:T(8,128)S(1)} %broadcast_multiply_fusion.2), kind=kOutput, calls=%fused_computation.42 | convolution fusion | flops 210739200 | bytes 3830784 | tf_op jit(solution)/shard_map/dot_general | solution.py:17
  13.0 1.2 %fusion.16 = (bf16[20,80,128]{2,1,0:T(8,128)(2,1)S(1)}, bf16[20,80,128]{2,1,0:T(8,128)(2,1)}) fusion(f32[20,80,4,128]{3,1,2,0:T(8,128)S(1)} %fusion.31, f32[20,80]{1,0:T(8,128)S(1)} %broadcast_multiply_fusion), kind=kLoop, calls=%fused_computation.24 | loop fusion | flops 2457600 | bytes 4102400 | tf_op jit(solution)/shard_map/convert_element_type | solution.py:24
  14.2 0.0 all-gather.2.cloned.1.call-update
  14.3 0.0 reduce-scatter.2.cloned.1.call-start
  14.3 0.4 copy.43
  14.7 41.7 %all-gather.2.cloned.1.call-done = bf16[160,80,128]{2,1,0:T(8,128)(2,1)} async-done(((bf16[20,80,128]{2,1,0:T(8,128)(2,1)}), bf16[160,80,128]{2,1,0:T(8,128)(2,1)}) %all-gather.2.cloned.1.call-update) | async-done | bytes 3276816 | tf_op jit(solution)/shard_map/all_gather | solution.py:79
  56.5 7.4 %copy.42 = bf16[160,80,128]{1,0,2:T(8,128)(2,1)} copy(bf16[160,80,128]{2,1,0:T(8,128)(2,1)} %all-gather.2.cloned.1.call-done) | data formatting | bytes 6553600 | tf_op jit(solution)/shard_map/all_gather | solution.py:79
  63.9 5.3 %fusion = bf16[20,160,128]{1,0,2:T(8,128)(2,1)S(1)} fusion(bf16[160,80,128]{1,0,2:T(8,128)(2,1)} %copy.42, bf16[20,80,128]{1,0,2:T(8,128)(2,1)S(1)} %copy.43), kind=kOutput, calls=%fused_computation.1 | convolution fusion | flops 65945600 | bytes 4505600 | tf_op jit(solution)/shard_map/ikc,jkc->ijc/dot_general | solution.py:76
  69.2 0.0 copy-start.1
  69.2 0.0 copy-start.3
  69.2 2.2 %copy.44 = bf16[20,160,128]{2,0,1:T(8,128)(2,1)} copy(bf16[20,160,128]{1,0,2:T(8,128)(2,1)S(1)} %fusion) | data formatting | bytes 1638400 | tf_op jit(solution)/shard_map/convert_element_type | solution.py:83
  71.4 0.0 copy-start.4
  71.4 0.0 reduce-scatter.2.cloned.1.call-update
  71.4 0.0 copy-done
  71.4 0.0 copy-done.1
  71.4 0.0 copy-done.3
  71.4 0.0 copy-start.2
  71.4 0.9 fusion.3
  72.3 17.7 %reduce-scatter.2.cloned.1.call-done = bf16[20,80,128]{2,0,1:T(8,128)(2,1)} async-done(((bf16[20,160,128]{2,0,1:T(8,128)(2,1)}), bf16[20,80,128]{2,0,1:T(8,128)(2,1)}) %reduce-scatter.2.cloned.1.call-update) | async-done | bytes 409616 | tf_op jit(solution)/shard_map/reduce_scatter | solution.py:82
  90.0 1.4 %convert_reduce_fusion = f32[20,80]{0,1:T(8,128)S(1)} fusion(bf16[20,80,128]{2,0,1:T(8,128)(2,1)} %reduce-scatter.2.cloned.1.call-done), kind=kLoop, calls=%fused_computation.9 | loop fusion | flops 408000 | bytes 416000 | tf_op jit(solution)/shard_map/reduce_sum | solution.py:8
  91.4 0.1 copy.45
  91.4 0.1 copy.46
  91.5 1.6 %fusion.7 = f32[20,80]{0,1:T(8,128)S(1)} fusion(bf16[20,80,128]{2,0,1:T(8,128)(2,1)} %reduce-scatter.2.cloned.1.call-done, f32[20,80]{0,1:T(8,128)S(1)} %copy.46), kind=kLoop, calls=%fused_computation.14 | loop fusion | flops 817600 | bytes 422400 | tf_op jit(solution)/shard_map/reduce_sum | solution.py:9
  93.2 0.1 copy.47
  93.3 0.1 copy.48
  93.4 0.0 copy-done.4
  93.4 1.6 %fusion.9 = bf16[20,80,128]{2,0,1:T(8,128)(2,1)S(1)} fusion(bf16[20,80,128]{2,0,1:T(8,128)(2,1)} %reduce-scatter.2.cloned.1.call-done, f32[128]{0:T(128)S(1)} %copy-done.4, f32[20,80]{0,1:T(8,128)S(1)} %copy.48, f32[20,80]{0,1:T(8,128)S(1)} %copy.46), kind=kLoop, calls=%fused_computation.16 | loop fusion | flops 1024000 | bytes 832512 | tf_op jit(solution)/shard_map/convert_element_type | solution.py:88
  95.0 0.0 copy-done.2
  95.0 1.0 fusion.4
  (4 shorter events, 0.0 us)
Async XLA Ops:
  6.5 64.9 %copy-start = (bf16[128,128]{1,0:T(8,128)(2,1)S(1)}, bf16[128,128]{1,0:T(8,128)(2,1)}, u32[]{:S(2)}) copy-start(bf16[128,128]{1,0:T(8,128)(2,1)} %param.19) | copy-start | bytes 98308
  6.5 49.9 %all-gather.2.cloned.1.call-start = ((), (), s32[]{:S(2)}) async-start(), calls=%async_computation.1 | async-start | bytes 3686400 | tf_op jit(solution)/shard_map/all_gather | solution.py:79
  14.3 75.7 %reduce-scatter.2.cloned.1.call-start = ((), (), s32[]{:S(2)}) async-start(), calls=%async_computation.2 | async-start | bytes 1474560 | tf_op jit(solution)/shard_map/reduce_scatter | solution.py:82
  69.2 2.2 %copy-start.1 = (bf16[20,80,128]{2,1,0:T(8,128)(2,1)S(1)}, bf16[20,80,128]{2,1,0:T(8,128)(2,1)}, u32[]{:S(2)}) copy-start(bf16[20,80,128]{2,1,0:T(8,128)(2,1)} %param.10) | copy-start | bytes 1228804
  69.2 2.2 %copy-start.3 = (f32[128]{0:T(128)S(1)}, f32[128]{0:T(128)}, u32[]{:S(2)}) copy-start(f32[128]{0:T(128)} %param.12) | copy-start | bytes 1540
  71.4 22.0 %copy-start.4 = (f32[128]{0:T(128)S(1)}, f32[128]{0:T(128)}, u32[]{:S(2)}) copy-start(f32[128]{0:T(128)} %param.17) | copy-start | bytes 1540
  71.4 23.6 %copy-start.2 = (bf16[128,128]{1,0:T(8,128)(2,1)S(1)}, bf16[128,128]{1,0:T(8,128)(2,1)}, u32[]{:S(2)}) copy-start(bf16[128,128]{1,0:T(8,128)(2,1)} %param.18) | copy-start | bytes 98308
Sparse Core Ops, SparseCore 0:
  14.4 42.0 all-gather.1
  71.5 18.4 reduce-scatter.1
where the time goes:
time: 104 us; the launch traced here: 103 us
  waiting for transfers between devices  59.5 us (57%)
  between operations  13.6 us (13%)
  local copies, waits for them, and re-layouts  10.6 us (10%)
  other arithmetic  10.3 us (10%)
  matrix products  8.85 us (9%)
    all_gather x1, waiting for transfers between devices, local(): lax.all_gather(right_act, 'row', axis=0, tiled=True)  41.7 us
    reduce_scatter x1, waiting for transfers between devices, local(): lax.psum_scatter(partial_sums.astype(jnp.bfloat16), 'col', scatter_dimens...  17.7 us
    all_gather x1, local copies, waits for them, and re-layouts, local(): lax.all_gather(right_act, 'row', axis=0, tiled=True)  7.38 us
    dot_general x1, matrix products, local(): jnp.einsum('ikc,jkc->ijc', left_act, lax.all_gather(right_act, 'row', axi...  5.32 us
    reduce_sum x2, other arithmetic, layer_norm(): spread = jnp.mean(jnp.square(values - center), axis=-1, keepdims=True)  3.29 us
    reduce_sum x2, other arithmetic, layer_norm(): center = jnp.mean(values, axis=-1, keepdims=True)  2.6 us
    convert_element_type x1, local copies, waits for them, and re-layouts, local(): partial_sums.astype(jnp.bfloat16)  2.15 us
  transfers between devices with their start and end apart: 2, of which 2 were waited for; matrix products, arithmetic and copies ran while one was open for 1% of the time, Pallas kernels for 0%

commit v1 on v0

--- a/solution.py
+++ b/solution.py
@@ -1,7 +1,14 @@
+import functools
+
 import jax
 import jax.numpy as jnp
 from jax import lax
+from jax.experimental import pallas as pl
+from jax.experimental.pallas import tpu as pltpu
 from jax.sharding import PartitionSpec as P
+
+LINE = ("row", "col")
+VMEM_LIMIT = 48 * 1024 * 1024
 
 
 def layer_norm(values, gain):
@@ -40,7 +47,7 @@
     return (gating * projected).astype(jnp.bfloat16)
 
 
-def local(
+def gathered(
     pair_rep,
     residue_mask,
     ln_gain,
@@ -90,6 +97,217 @@
     return finish_output(normed_hidden, own_pair, out_proj, out_gate)
 
 
+def whole(shape):
+    return pl.BlockSpec(shape, lambda *_: (0,) * len(shape))
+
+
+def normed_rows(pair_ref, gain_ref):
+    rows, cols, width = pair_ref.shape
+    values = pair_ref[...].astype(jnp.float32).reshape(rows * cols, width)
+    return layer_norm(values, gain_ref[...]).astype(jnp.bfloat16)
+
+
+def mask_block(mask_ref, flags_ref, rows, cols, width):
+    first = flags_ref[0] * (rows * pl.num_programs(0)) + pl.program_id(0) * rows
+    col_mask = jnp.zeros((1, cols), jnp.int32)
+    for block in range(mask_ref.shape[1] // cols):
+        part = mask_ref[:, block * cols : (block + 1) * cols]
+        col_mask = jnp.where(flags_ref[1] == block, part, col_mask)
+    spread = jnp.transpose(jnp.broadcast_to(col_mask.astype(jnp.float32), (width, cols)))
+    lanes = lax.broadcasted_iota(jnp.int32, mask_ref.shape, 1)
+    blocks = []
+    for row in range(rows):
+        present = jnp.sum(jnp.where(lanes == first + row, mask_ref[...], 0), axis=1, keepdims=True)
+        blocks.append(spread * present.astype(jnp.float32))
+    return jnp.concatenate(blocks, axis=0)
+
+
+def right_kernel(flags_ref, pair_ref, mask_ref, gain_ref, proj_ref, gate_ref, right_ref):
+    rows, cols, width = pair_ref.shape
+    normed = normed_rows(pair_ref, gain_ref)
+    masked = mask_block(mask_ref, flags_ref, rows, cols, width)
+    stacked = jnp.concatenate([proj_ref[...], gate_ref[...]], axis=1)
+    both = jnp.dot(normed, stacked, preferred_element_type=jnp.float32)
+    act = masked * jax.nn.sigmoid(both[:, width:]) * both[:, :width]
+    right_ref[...] = act.astype(jnp.bfloat16).reshape(rows, cols, width)
+
+
+def left_kernel(
+    flags_ref, pair_ref, mask_ref, gain_ref, proj_ref, gate_ref, out_gate_ref, left_ref, gating_ref
+):
+    rows, cols, width = pair_ref.shape
+    normed = normed_rows(pair_ref, gain_ref)
+    masked = mask_block(mask_ref, flags_ref, rows, cols, width)
+    stacked = jnp.concatenate([proj_ref[...], gate_ref[...]], axis=1)
+    both = jnp.dot(normed, stacked, preferred_element_type=jnp.float32)
+    act = masked * jax.nn.sigmoid(both[:, width:]) * both[:, :width]
+    left_ref[...] = act.astype(jnp.bfloat16).astype(jnp.float32)
+    gating_ref[...] = jax.nn.sigmoid(
+        jnp.dot(normed, out_gate_ref[...], preferred_element_type=jnp.float32)
+    )
+
+
+def triangle_kernel(rows, cols, flags_ref, left_ref, mine_ref, other_ref, sum_ref, held):
+    width = held.shape[1]
+    tile = rows * cols
+    core = flags_ref[2]
+    held[pl.ds(pl.multiple_of(core * tile, tile), tile), :] = (
+        mine_ref[...].astype(jnp.float32).reshape(tile, width)
+    )
+    held[pl.ds(pl.multiple_of((1 - core) * tile, tile), tile), :] = (
+        other_ref[...].astype(jnp.float32).reshape(tile, width)
+    )
+    group = 5
+
+    def of_rows(block, _):
+        def of_col(k, totals):
+            right = held[pl.ds(k, 2 * rows, stride=cols), :]
+            return tuple(
+                totals[g] + left_ref[pl.ds((block * group + g) * cols + k, 1), :] * right
+                for g in range(group)
+            )
+
+        start = tuple(jnp.zeros((2 * rows, width), jnp.float32) for _ in range(group))
+        totals = lax.fori_loop(0, cols, of_col, start, unroll=8)
+        for g in range(group):
+            sum_ref[block * group + g] = totals[g].astype(jnp.bfloat16)
+        return 0
+
+    lax.fori_loop(0, rows // group, of_rows, 0)
+
+
+def finish_kernel(
+    flags_ref, near0, near1, far0, far1, gnear0, gnear1, gfar0, gfar1, gain_ref, proj_ref, gating_ref, out_ref
+):
+    rows, cols, width = out_ref.shape
+    keeps_near, odd = flags_ref[3] == 1, flags_ref[4] == 1
+
+    def total(a, b, c, d):
+        f = lambda ref: ref[...].astype(jnp.float32)
+        return jnp.where(keeps_near, f(a) + f(b), f(c) + f(d))
+
+    first = total(near0, gnear0, far0, gfar0)
+    second = total(near1, gnear1, far1, gfar1)
+    hidden = jnp.concatenate(
+        [jnp.where(odd, second, first), jnp.where(odd, first, second)], axis=1
+    ).reshape(rows * cols, width)
+    normed = layer_norm(hidden, gain_ref[...]).astype(jnp.bfloat16)
+    projected = jnp.dot(normed, proj_ref[...], preferred_element_type=jnp.float32)
+    out_ref[...] = (gating_ref[...] * projected).astype(jnp.bfloat16).reshape(rows, cols, width)
+
+
+def call(kernel, micros, out_shape, in_specs, out_specs, grid, scratch=()):
+    return pl.pallas_call(
+        kernel,
+        out_shape=out_shape,
+        grid_spec=pltpu.PrefetchScalarGridSpec(
+            num_scalar_prefetch=1,
+            grid=grid,
+            in_specs=in_specs,
+            out_specs=out_specs,
+            scratch_shapes=list(scratch),
+        ),
+        compiler_params=pltpu.CompilerParams(vmem_limit_bytes=VMEM_LIMIT),
+        cost_estimate=pl.CostEstimate(
+            flops=int(micros * 1.1e9), bytes_accessed=int(micros * 3e6), transcendentals=0
+        ),
+    )
+
+
+def exchanged(
+    pair_rep,
+    residue_mask,
+    ln_gain,
+    left_proj,
+    left_gate,
+    right_proj,
+    right_gate,
+    hidden_gain,
+    out_proj,
+    out_gate,
+):
+    rows, cols, width = pair_rep.shape
+    tile = rows * cols
+    row = lax.axis_index("row")
+    col = lax.axis_index("col")
+    core = row % 2
+    chip = row // 2
+    keeps_near = (chip // 2 == col).astype(jnp.int32)
+    flags = jnp.stack([row, col, core, keeps_near, chip % 2]).astype(jnp.int32)
+    mask = residue_mask.reshape(1, -1)
+    ln_gain = ln_gain.reshape(1, -1)
+    hidden_gain = hidden_gain.reshape(1, -1)
+
+    places = range(16)
+    over_core = [(p, p ^ 2) for p in places]
+    over_next = [(p, p ^ 4) for p in places]
+    over_pair = [(p, p ^ 8) for p in places]
+    near_sums = [(p, p ^ 1) for p in places if p // 8 != p % 2]
+    far_sums = [(p, p ^ 1) for p in places if p // 8 == p % 2]
+    send = lambda value, pairs: lax.ppermute(value, LINE, pairs)
+
+    steps = 4
+    block = rows // steps
+    pair_spec = pl.BlockSpec((block, cols, width), lambda s, _: (s, 0, 0))
+    flat_spec = pl.BlockSpec((block * cols, width), lambda s, _: (s, 0))
+    square = whole((width, width))
+    vector = whole((1, width))
+    right = call(
+        right_kernel,
+        2.2,
+        jax.ShapeDtypeStruct((rows, cols, width), jnp.bfloat16),
+        [pair_spec, whole(mask.shape), vector, square, square],
+        pair_spec,
+        (steps,),
+    )(flags, pair_rep, mask, ln_gain, right_proj, right_gate)
+
+    from_pair = send(right, over_pair)
+    from_next = send(right, over_next)
+    from_core = send(right, over_core)
+
+    left, gating = call(
+        left_kernel,
+        2.9,
+        (
+            jax.ShapeDtypeStruct((tile, width), jnp.float32),
+            jax.ShapeDtypeStruct((tile, width), jnp.float32),
+        ),
+        [pair_spec, whole(mask.shape), vector, square, square, square],
+        (flat_spec, flat_spec),
+        (steps,),
+    )(flags, pair_rep, mask, ln_gain, left_proj, left_gate, out_gate)
+
+    tile_spec = whole((rows, cols, width))
+    sums = call(
+        functools.partial(triangle_kernel, rows, cols),
+        4.2,
+        jax.ShapeDtypeStruct((rows, 2 * rows, width), jnp.bfloat16),
+        [whole((tile, width)), tile_spec, tile_spec],
+        whole((rows, 2 * rows, width)),
+        (1,),
+        [pltpu.VMEM((2 * tile, width), jnp.float32)],
+    )
+    near0 = sums(flags, left, right, from_core)
+    gnear0 = send(near0, near_sums)
+    near1 = sums(flags, left, from_next, send(from_next, over_core))
+    gnear1 = send(near1, near_sums)
+    from_far = send(from_pair, over_next)
+    far0 = sums(flags, left, from_pair, send(from_pair, over_core))
+    gfar0 = send(far0, far_sums)
+    far1 = sums(flags, left, from_far, send(from_far, over_core))
+    gfar1 = send(far1, far_sums)
+
+    part = whole((rows, 2 * rows, width))
+    return call(
+        finish_kernel,
+        2.0,
+        jax.ShapeDtypeStruct((rows, cols, width), jnp.bfloat16),
+        [part] * 8 + [vector, square, whole((tile, width))],
+        tile_spec,
+        (1,),
+    )(flags, near0, near1, far0, far1, gnear0, gnear1, gfar0, gfar1, hidden_gain, out_proj, gating)
+
+
 def solution(mesh):
     in_specs = (
         P(("groups", "row"), "col", None),
@@ -104,4 +322,6 @@
         P(),
     )
     out_specs = P(("groups", "row"), ("col", "chan"), None)
+    short = mesh.shape["row"] == 8 and mesh.shape["col"] == 2 and mesh.shape["chan"] == 1
+    local = exchanged if short else gathered
     return jax.shard_map(local, mesh=mesh, in_specs=in_specs, out_specs=out_specs, check_vma=False)

time: 104 us -> 64 us (0.62)
  the two profiles are of different devices: /device:TPU:0 before, /device:TPU:25 now
where the time goes in v1:
time: 64 us; the launch traced here: 63.1 us
  waiting for transfers between devices  25.5 us (40%)
  Pallas kernels  23.8 us (37%)
  starting transfers between devices  11.2 us (18%)
  local copies, waits for them, and re-layouts  2.43 us (4%)
    ppermute x11, waiting for transfers between devices, exchanged(): send = lambda value, pairs: lax.ppermute(value, LINE, pairs)  25.5 us
    ppermute x11, starting transfers between devices, exchanged(): send = lambda value, pairs: lax.ppermute(value, LINE, pairs)  11.2 us
    pallas_call x1, Pallas kernels, exchanged(): far1 = sums(flags, left, from_far, send(from_far, over_core))  4.18 us
    pallas_call x1, Pallas kernels, exchanged(): near1 = sums(flags, left, from_next, send(from_next, over_core))  4.18 us
    pallas_call x1, Pallas kernels, exchanged(): near0 = sums(flags, left, right, from_core)  4.18 us
    pallas_call x1, Pallas kernels, exchanged(): far0 = sums(flags, left, from_pair, send(from_pair, over_core))  4.18 us
    pallas_call x1, Pallas kernels, exchanged(): call(left_kernel, 2.9, (jax.ShapeDtypeStruct((tile, width), jnp.float32),...  2.86 us
    unnamed x20, local copies, waits for them, and re-layouts  2.35 us
  transfers between devices with their start and end apart: 11, of which 4 were waited for; matrix products, arithmetic and copies ran while one was open for 0% of the time, Pallas kernels for 31%

profile of v1, /device:TPU:25, one launch (start us, length us, event | category | flops | bytes accessed | tf_op | source)
XLA Modules:
  0.0 63.1 jit_solution(14283189022147804599)
XLA Ops:
  0.0 0.0 copy-start.7
  0.0 0.0 copy-start.1
  0.0 0.0 copy-start.2
  0.1 0.1 stack.27.flags_ref
  0.1 0.5 copy-done.7
  0.7 0.0 copy-done.8
  0.7 0.1 copy-done.1
  0.8 0.0 copy-done.2
  0.8 0.0 copy-start
  0.8 1.0 %copy-done = bf16[20,80,128]{2,1,0:T(8,128)(2,1)S(1)} copy-done((bf16[20,80,128]{2,1,0:T(8,128)(2,1)S(1)}, bf16[20,80,128]{2,1,0:T(8,128)(2,1)}, u32[]{:S(2)}) %copy-start) | copy-done | bytes 409624
  1.8 0.0 copy-start.3
  1.8 0.0 copy-start.4
  1.8 2.2 %shard_map.101.mine_ref = bf16[20,80,128]{2,1,0:T(8,128)(2,1)S(1)} custom-call(s32[5]{0:T(128)S(1)} %stack.27.flags_ref, bf16[20,80,128]{2,1,0:T(8,128)(2,1)S(1)} %copy-done, s32[1,160]{1,0:T(1,128)S(1)} %bitcast.8, f32[1,128]{1,0:T(1,128)S(1)} %bitcast.10, bf16[128,128]{1,0:T(8,128)(2,1)S(1)} %copy-done.1, bf16[128,128]{1,0:T(8,128)(2,1)S(1)} %copy-done.2), custom_call_target="tpu_custom_call" | custom-call | flops 2420000000 | bytes 6600000 | tf_op jit(solution)/shard_map/pallas_call | solution.py:255
  4.0 0.2 collective-permute-start.1
  4.3 1.0 %collective-permute-start = (bf16[20,80,128]{2,1,0:T(8,128)(2,1)S(1)}, bf16[20,80,128]{2,1,0:T(8,128)(2,1)S(1)}, u32[]{:S(2)}, u32[]{:S(2)}) collective-permute-start(bf16[20,80,128]{2,1,0:T(8,128)(2,1)S(1)} %shard_map.101.mine_ref), channel_id=1, source_target_pairs={{0,2},{1,3},{2,0},{3,1},{4,6},{5,7},{6,4},{7,5},{8,10},{9,11},{10,... | collective-permute-start | bytes 1228808 | tf_op jit(solution)/shard_map/ppermute | solution.py:247
  5.2 0.0 collective-permute-start.3
  5.2 0.0 copy-done.3
  5.2 0.0 copy-done.4
  5.2 0.0 copy-done.5
  5.3 2.9 %shard_map.100 = (f32[1600,128]{1,0:T(8,128)S(1)}, f32[1600,128]{1,0:T(8,128)S(1)}) custom-call(s32[5]{0:T(128)S(1)} %stack.27.flags_ref, bf16[20,80,128]{2,1,0:T(8,128)(2,1)S(1)} %copy-done, s32[1,160]{1,0:T(1,128)S(1)} %bitcast.9, f32[1,128]{1,0:T(1,128)S(1)} %bitcast.11, bf16[128,128]{1,0:T(8,128)(2,1)S(1)} %copy-done.3, bf16[128,128]{1,0:T(8,128)(2,1)S(1)} %copy-done.4, ...), custom_call_target="tpu_custom_call" | custom-call | flops 3190000128 | bytes 8700000 | tf_op jit(solution)/shard_map/pallas_call | solution.py:268
  8.1 12.9 %collective-permute-done.1.mine_ref = bf16[20,80,128]{2,1,0:T(8,128)(2,1)S(1)} collective-permute-done((bf16[20,80,128]{2,1,0:T(8,128)(2,1)S(1)}, bf16[20,80,128]{2,1,0:T(8,128)(2,1)S(1)}, u32[]{:S(2)}, u32[]{:S(2)}) %collective-permute-start.1) | collective-permute-done | bytes 409632 | tf_op jit(solution)/shard_map/ppermute | solution.py:247
  21.0 1.6 %collective-permute-start.2 = (bf16[20,80,128]{2,1,0:T(8,128)(2,1)S(1)}, bf16[20,80,128]{2,1,0:T(8,128)(2,1)S(1)}, u32[]{:S(2)}, u32[]{:S(2)}) collective-permute-start(bf16[20,80,128]{2,1,0:T(8,128)(2,1)S(1)} %collective-permute-done.1.mine_ref), channel_id=1, source_target_pairs={{0,2},{1,3},{2,0},{3,1},{4,6},{5,7},{6,4},{7,5},{8,10},{9,11},{10,... | collective-permute-start | bytes 1228808 | tf_op jit(solution)/shard_map/ppermute | solution.py:247
  22.6 0.0 collective-permute-done.other_ref
  22.6 4.2 %shard_map.102.near0 = bf16[20,40,128]{2,1,0:T(8,128)(2,1)S(1)} custom-call(s32[5]{0:T(128)S(1)} %stack.27.flags_ref, f32[1600,128]{1,0:T(8,128)S(1)} %get-tuple-element.7.left_ref, bf16[20,80,128]{2,1,0:T(8,128)(2,1)S(1)} %shard_map.101.mine_ref, bf16[20,80,128]{2,1,0:T(8,128)(2,1)S(1)} %collective-permute-done.other_ref), custom_call_target="tpu_custom_call" | custom-call | flops 4620000256 | bytes 12600000 | tf_op jit(solution)/shard_map/pallas_call | solution.py:290
  26.8 3.1 %collective-permute-start.7 = (bf16[20,40,128]{2,1,0:T(8,128)(2,1)S(1)}, bf16[20,40,128]{2,1,0:T(8,128)(2,1)S(1)}, u32[]{:S(2)}, u32[]{:S(2)}) collective-permute-start(bf16[20,40,128]{2,1,0:T(8,128)(2,1)S(1)} %shard_map.102.near0), channel_id=1, source_target_pairs={{1,0},{3,2},{5,4},{7,6},{8,9},{10,11},{12,13},{14,15},{17,16},{19,... | collective-permute-start | bytes 614408 | tf_op jit(solution)/shard_map/ppermute | solution.py:247
  29.9 0.0 collective-permute-done.3.mine_ref
  29.9 0.3 collective-permute-start.4
  30.3 0.0 collective-permute-start.5
  30.3 0.0 collective-permute-done.2.other_ref
  30.3 4.2 %shard_map.103.near1 = bf16[20,40,128]{2,1,0:T(8,128)(2,1)S(1)} custom-call(s32[5]{0:T(128)S(1)} %stack.27.flags_ref, f32[1600,128]{1,0:T(8,128)S(1)} %get-tuple-element.7.left_ref, bf16[20,80,128]{2,1,0:T(8,128)(2,1)S(1)} %collective-permute-done.1.mine_ref, bf16[20,80,128]{2,1,0:T(8,128)(2,1)S(1)} %collective-permute-done.2.other_ref), custom_call_target="tpu_custom_call" | custom-call | flops 4620000256 | bytes 12600000 | tf_op jit(solution)/shard_map/pallas_call | solution.py:292
  34.4 1.3 %collective-permute-start.8 = (bf16[20,40,128]{2,1,0:T(8,128)(2,1)S(1)}, bf16[20,40,128]{2,1,0:T(8,128)(2,1)S(1)}, u32[]{:S(2)}, u32[]{:S(2)}) collective-permute-start(bf16[20,40,128]{2,1,0:T(8,128)(2,1)S(1)} %shard_map.103.near1), channel_id=1, source_target_pairs={{1,0},{3,2},{5,4},{7,6},{8,9},{10,11},{12,13},{14,15},{17,16},{19,... | collective-permute-start | bytes 614408 | tf_op jit(solution)/shard_map/ppermute | solution.py:247
  35.8 5.3 %collective-permute-done.5.mine_ref = bf16[20,80,128]{2,1,0:T(8,128)(2,1)S(1)} collective-permute-done((bf16[20,80,128]{2,1,0:T(8,128)(2,1)S(1)}, bf16[20,80,128]{2,1,0:T(8,128)(2,1)S(1)}, u32[]{:S(2)}, u32[]{:S(2)}) %collective-permute-start.5) | collective-permute-done | bytes 409632 | tf_op jit(solution)/shard_map/ppermute | solution.py:247
  41.1 1.0 %collective-permute-start.6 = (bf16[20,80,128]{2,1,0:T(8,128)(2,1)S(1)}, bf16[20,80,128]{2,1,0:T(8,128)(2,1)S(1)}, u32[]{:S(2)}, u32[]{:S(2)}) collective-permute-start(bf16[20,80,128]{2,1,0:T(8,128)(2,1)S(1)} %collective-permute-done.5.mine_ref), channel_id=1, source_target_pairs={{0,2},{1,3},{2,0},{3,1},{4,6},{5,7},{6,4},{7,5},{8,10},{9,11},{10,... | collective-permute-start | bytes 1228808 | tf_op jit(solution)/shard_map/ppermute | solution.py:247
  42.1 0.0 collective-permute-done.4.other_ref
  42.1 4.2 %shard_map.104.far0 = bf16[20,40,128]{2,1,0:T(8,128)(2,1)S(1)} custom-call(s32[5]{0:T(128)S(1)} %stack.27.flags_ref, f32[1600,128]{1,0:T(8,128)S(1)} %get-tuple-element.7.left_ref, bf16[20,80,128]{2,1,0:T(8,128)(2,1)S(1)} %collective-permute-done.3.mine_ref, bf16[20,80,128]{2,1,0:T(8,128)(2,1)S(1)} %collective-permute-done.4.other_ref), custom_call_target="tpu_custom_call" | custom-call | flops 4620000256 | bytes 12600000 | tf_op jit(solution)/shard_map/pallas_call | solution.py:295
  46.3 0.0 copy-start.6
  46.3 1.3 %collective-permute-start.9 = (bf16[20,40,128]{2,1,0:T(8,128)(2,1)S(1)}, bf16[20,40,128]{2,1,0:T(8,128)(2,1)S(1)}, u32[]{:S(2)}, u32[]{:S(2)}) collective-permute-start(bf16[20,40,128]{2,1,0:T(8,128)(2,1)S(1)} %shard_map.104.far0), channel_id=1, source_target_pairs={{0,1},{2,3},{4,5},{6,7},{9,8},{11,10},{13,12},{15,14},{16,17},{18,... | collective-permute-start | bytes 614408 | tf_op jit(solution)/shard_map/ppermute | solution.py:247
  47.6 0.0 collective-permute-done.6.other_ref
  47.6 4.2 %shard_map.105.far1 = bf16[20,40,128]{2,1,0:T(8,128)(2,1)S(1)} custom-call(s32[5]{0:T(128)S(1)} %stack.27.flags_ref, f32[1600,128]{1,0:T(8,128)S(1)} %get-tuple-element.7.left_ref, bf16[20,80,128]{2,1,0:T(8,128)(2,1)S(1)} %collective-permute-done.5.mine_ref, bf16[20,80,128]{2,1,0:T(8,128)(2,1)S(1)} %collective-permute-done.6.other_ref), custom_call_target="tpu_custom_call" | custom-call | flops 4620000256 | bytes 12600000 | tf_op jit(solution)/shard_map/pallas_call | solution.py:297
  51.8 1.3 %collective-permute-start.10 = (bf16[20,40,128]{2,1,0:T(8,128)(2,1)S(1)}, bf16[20,40,128]{2,1,0:T(8,128)(2,1)S(1)}, u32[]{:S(2)}, u32[]{:S(2)}) collective-permute-start(bf16[20,40,128]{2,1,0:T(8,128)(2,1)S(1)} %shard_map.105.far1), channel_id=1, source_target_pairs={{0,1},{2,3},{4,5},{6,7},{9,8},{11,10},{13,12},{15,14},{16,17},{18,... | collective-permute-start | bytes 614408 | tf_op jit(solution)/shard_map/ppermute | solution.py:247
  53.1 0.0 collective-permute-done.7.gnear0
  53.1 0.0 collective-permute-done.8.gnear1
  53.2 1.8 %collective-permute-done.9.gfar0 = bf16[20,40,128]{2,1,0:T(8,128)(2,1)S(1)} collective-permute-done((bf16[20,40,128]{2,1,0:T(8,128)(2,1)S(1)}, bf16[20,40,128]{2,1,0:T(8,128)(2,1)S(1)}, u32[]{:S(2)}, u32[]{:S(2)}) %collective-permute-start.9) | collective-permute-done | bytes 204832 | tf_op jit(solution)/shard_map/ppermute | solution.py:247
  54.9 5.5 %collective-permute-done.10.gfar1 = bf16[20,40,128]{2,1,0:T(8,128)(2,1)S(1)} collective-permute-done((bf16[20,40,128]{2,1,0:T(8,128)(2,1)S(1)}, bf16[20,40,128]{2,1,0:T(8,128)(2,1)S(1)}, u32[]{:S(2)}, u32[]{:S(2)}) %collective-permute-start.10) | collective-permute-done | bytes 204832 | tf_op jit(solution)/shard_map/ppermute | solution.py:247
  60.4 0.0 copy-start.9
  60.4 0.0 copy-done.6
  60.5 0.7 %copy-done.9 = f32[128]{0:T(128)S(1)} copy-done((f32[128]{0:T(128)S(1)}, f32[128]{0:T(128)}, u32[]{:S(2)}) %copy-start.9) | copy-done | bytes 536
  61.1 2.0 %shard_map.106 = bf16[20,80,128]{2,1,0:T(8,128)(2,1)} custom-call(s32[5]{0:T(128)S(1)} %stack.27.flags_ref, bf16[20,40,128]{2,1,0:T(8,128)(2,1)S(1)} %shard_map.102.near0, bf16[20,40,128]{2,1,0:T(8,128)(2,1)S(1)} %shard_map.103.near1, bf16[20,40,128]{2,1,0:T(8,128)(2,1)S(1)} %shard_map.104.far0, bf16[20,40,128]{2,1,0:T(8,128)(2,1)S(1)} %shard_map.105.far1, ...), custom_call_target="tpu_custom_call" | custom-call | flops 2200000000 | bytes 6000000 | tf_op jit(solution)/shard_map/pallas_call | solution.py:301
  (2 shorter events, 0.0 us)
Async XLA Ops:
  0.0 0.7 %copy-start.7 = (s32[160]{0:T(256)S(1)}, s32[160]{0:T(256)}, u32[]{:S(2)}) copy-start(s32[160]{0:T(256)} %param.11) | copy-start | bytes 1924
  0.0 0.7 %copy-start.8 = (f32[128]{0:T(128)S(1)}, f32[128]{0:T(128)}, u32[]{:S(2)}) copy-start(f32[128]{0:T(128)} %param.12) | copy-start | bytes 1540
  0.0 0.8 %copy-start.1 = (bf16[128,128]{1,0:T(8,128)(2,1)S(1)}, bf16[128,128]{1,0:T(8,128)(2,1)}, u32[]{:S(2)}) copy-start(bf16[128,128]{1,0:T(8,128)(2,1)} %proj_ref.4) | copy-start | bytes 98308
  0.0 0.8 %copy-start.2 = (bf16[128,128]{1,0:T(8,128)(2,1)S(1)}, bf16[128,128]{1,0:T(8,128)(2,1)}, u32[]{:S(2)}) copy-start(bf16[128,128]{1,0:T(8,128)(2,1)} %gate_ref.3) | copy-start | bytes 98308
  0.8 1.0 %copy-start = (bf16[20,80,128]{2,1,0:T(8,128)(2,1)S(1)}, bf16[20,80,128]{2,1,0:T(8,128)(2,1)}, u32[]{:S(2)}) copy-start(bf16[20,80,128]{2,1,0:T(8,128)(2,1)} %pair_ref.3) | copy-start | bytes 1228804
  1.8 3.4 %copy-start.3 = (bf16[128,128]{1,0:T(8,128)(2,1)S(1)}, bf16[128,128]{1,0:T(8,128)(2,1)}, u32[]{:S(2)}) copy-start(bf16[128,128]{1,0:T(8,128)(2,1)} %proj_ref.3) | copy-start | bytes 98308
  1.8 3.4 %copy-start.4 = (bf16[128,128]{1,0:T(8,128)(2,1)S(1)}, bf16[128,128]{1,0:T(8,128)(2,1)}, u32[]{:S(2)}) copy-start(bf16[128,128]{1,0:T(8,128)(2,1)} %gate_ref.2) | copy-start | bytes 98308
  1.8 3.4 %copy-start.5 = (bf16[128,128]{1,0:T(8,128)(2,1)S(1)}, bf16[128,128]{1,0:T(8,128)(2,1)}, u32[]{:S(2)}) copy-start(bf16[128,128]{1,0:T(8,128)(2,1)} %out_gate_ref.1) | copy-start | bytes 98308
  4.0 17.0 %collective-permute-start.1 = (bf16[20,80,128]{2,1,0:T(8,128)(2,1)S(1)}, bf16[20,80,128]{2,1,0:T(8,128)(2,1)S(1)}, u32[]{:S(2)}, u32[]{:S(2)}) collective-permute-start(bf16[20,80,128]{2,1,0:T(8,128)(2,1)S(1)} %shard_map.101.mine_ref), channel_id=1, source_target_pairs={{0,4},{1,5},{2,6},{3,7},{4,0},{5,1},{6,2},{7,3},{8,12},{9,13},{10,... | collective-permute-start | bytes 1228808 | tf_op jit(solution)/shard_map/ppermute | solution.py:247
  4.3 18.3 %collective-permute-start = (bf16[20,80,128]{2,1,0:T(8,128)(2,1)S(1)}, bf16[20,80,128]{2,1,0:T(8,128)(2,1)S(1)}, u32[]{:S(2)}, u32[]{:S(2)}) collective-permute-start(bf16[20,80,128]{2,1,0:T(8,128)(2,1)S(1)} %shard_map.101.mine_ref), channel_id=1, source_target_pairs={{0,2},{1,3},{2,0},{3,1},{4,6},{5,7},{6,4},{7,5},{8,10},{9,11},{10,... | collective-permute-start | bytes 1228808 | tf_op jit(solution)/shard_map/ppermute | solution.py:247
  5.2 24.7 %collective-permute-start.3 = (bf16[20,80,128]{2,1,0:T(8,128)(2,1)S(1)}, bf16[20,80,128]{2,1,0:T(8,128)(2,1)S(1)}, u32[]{:S(2)}, u32[]{:S(2)}) collective-permute-start(bf16[20,80,128]{2,1,0:T(8,128)(2,1)S(1)} %shard_map.101.mine_ref), channel_id=1, source_target_pairs={{0,8},{1,9},{2,10},{3,11},{4,12},{5,13},{6,14},{7,15},{8,0},{9,1},... | collective-permute-start | bytes 1228808 | tf_op jit(solution)/shard_map/ppermute | solution.py:247
  21.0 9.2 %collective-permute-start.2 = (bf16[20,80,128]{2,1,0:T(8,128)(2,1)S(1)}, bf16[20,80,128]{2,1,0:T(8,128)(2,1)S(1)}, u32[]{:S(2)}, u32[]{:S(2)}) collective-permute-start(bf16[20,80,128]{2,1,0:T(8,128)(2,1)S(1)} %collective-permute-done.1.mine_ref), channel_id=1, source_target_pairs={{0,2},{1,3},{2,0},{3,1},{4,6},{5,7},{6,4},{7,5},{8,10},{9,11},{10,... | collective-permute-start | bytes 1228808 | tf_op jit(solution)/shard_map/ppermute | solution.py:247
  26.8 26.4 %collective-permute-start.7 = (bf16[20,40,128]{2,1,0:T(8,128)(2,1)S(1)}, bf16[20,40,128]{2,1,0:T(8,128)(2,1)S(1)}, u32[]{:S(2)}, u32[]{:S(2)}) collective-permute-start(bf16[20,40,128]{2,1,0:T(8,128)(2,1)S(1)} %shard_map.102.near0), channel_id=1, source_target_pairs={{1,0},{3,2},{5,4},{7,6},{8,9},{10,11},{12,13},{14,15},{17,16},{19,... | collective-permute-start | bytes 614408 | tf_op jit(solution)/shard_map/ppermute | solution.py:247
  29.9 12.2 %collective-permute-start.4 = (bf16[20,80,128]{2,1,0:T(8,128)(2,1)S(1)}, bf16[20,80,128]{2,1,0:T(8,128)(2,1)S(1)}, u32[]{:S(2)}, u32[]{:S(2)}) collective-permute-start(bf16[20,80,128]{2,1,0:T(8,128)(2,1)S(1)} %collective-permute-done.3.mine_ref), channel_id=1, source_target_pairs={{0,2},{1,3},{2,0},{3,1},{4,6},{5,7},{6,4},{7,5},{8,10},{9,11},{10,... | collective-permute-start | bytes 1228808 | tf_op jit(solution)/shard_map/ppermute | solution.py:247
  30.3 10.8 %collective-permute-start.5 = (bf16[20,80,128]{2,1,0:T(8,128)(2,1)S(1)}, bf16[20,80,128]{2,1,0:T(8,128)(2,1)S(1)}, u32[]{:S(2)}, u32[]{:S(2)}) collective-permute-start(bf16[20,80,128]{2,1,0:T(8,128)(2,1)S(1)} %collective-permute-done.3.mine_ref), channel_id=1, source_target_pairs={{0,4},{1,5},{2,6},{3,7},{4,0},{5,1},{6,2},{7,3},{8,12},{9,13},{10,... | collective-permute-start | bytes 1228808 | tf_op jit(solution)/shard_map/ppermute | solution.py:247
  34.4 18.7 %collective-permute-start.8 = (bf16[20,40,128]{2,1,0:T(8,128)(2,1)S(1)}, bf16[20,40,128]{2,1,0:T(8,128)(2,1)S(1)}, u32[]{:S(2)}, u32[]{:S(2)}) collective-permute-start(bf16[20,40,128]{2,1,0:T(8,128)(2,1)S(1)} %shard_map.103.near1), channel_id=1, source_target_pairs={{1,0},{3,2},{5,4},{7,6},{8,9},{10,11},{12,13},{14,15},{17,16},{19,... | collective-permute-start | bytes 614408 | tf_op jit(solution)/shard_map/ppermute | solution.py:247
  41.1 6.5 %collective-permute-start.6 = (bf16[20,80,128]{2,1,0:T(8,128)(2,1)S(1)}, bf16[20,80,128]{2,1,0:T(8,128)(2,1)S(1)}, u32[]{:S(2)}, u32[]{:S(2)}) collective-permute-start(bf16[20,80,128]{2,1,0:T(8,128)(2,1)S(1)} %collective-permute-done.5.mine_ref), channel_id=1, source_target_pairs={{0,2},{1,3},{2,0},{3,1},{4,6},{5,7},{6,4},{7,5},{8,10},{9,11},{10,... | collective-permute-start | bytes 1228808 | tf_op jit(solution)/shard_map/ppermute | solution.py:247
  46.3 14.1 %copy-start.6 = (bf16[128,128]{1,0:T(8,128)(2,1)S(1)}, bf16[128,128]{1,0:T(8,128)(2,1)}, u32[]{:S(2)}) copy-start(bf16[128,128]{1,0:T(8,128)(2,1)} %proj_ref.5) | copy-start | bytes 98308
  46.3 8.6 %collective-permute-start.9 = (bf16[20,40,128]{2,1,0:T(8,128)(2,1)S(1)}, bf16[20,40,128]{2,1,0:T(8,128)(2,1)S(1)}, u32[]{:S(2)}, u32[]{:S(2)}) collective-permute-start(bf16[20,40,128]{2,1,0:T(8,128)(2,1)S(1)} %shard_map.104.far0), channel_id=1, source_target_pairs={{0,1},{2,3},{4,5},{6,7},{9,8},{11,10},{13,12},{15,14},{16,17},{18,... | collective-permute-start | bytes 614408 | tf_op jit(solution)/shard_map/ppermute | solution.py:247
  51.8 8.6 %collective-permute-start.10 = (bf16[20,40,128]{2,1,0:T(8,128)(2,1)S(1)}, bf16[20,40,128]{2,1,0:T(8,128)(2,1)S(1)}, u32[]{:S(2)}, u32[]{:S(2)}) collective-permute-start(bf16[20,40,128]{2,1,0:T(8,128)(2,1)S(1)} %shard_map.105.far1), channel_id=1, source_target_pairs={{0,1},{2,3},{4,5},{6,7},{9,8},{11,10},{13,12},{15,14},{16,17},{18,... | collective-permute-start | bytes 614408 | tf_op jit(solution)/shard_map/ppermute | solution.py:247
  60.4 0.7 %copy-start.9 = (f32[128]{0:T(128)S(1)}, f32[128]{0:T(128)}, u32[]{:S(2)}) copy-start(f32[128]{0:T(128)} %param.17) | copy-start | bytes 1540

commit v2 on v1

--- a/solution.py
+++ b/solution.py
@@ -9,6 +9,9 @@
 
 LINE = ("row", "col")
 VMEM_LIMIT = 48 * 1024 * 1024
+VECTOR_ROWS = 8
+PAIR = 2
+UNROLL = 10
 
 
 def layer_norm(values, gain):
@@ -133,7 +136,21 @@
 
 
 def left_kernel(
-    flags_ref, pair_ref, mask_ref, gain_ref, proj_ref, gate_ref, out_gate_ref, left_ref, gating_ref
+    flags_ref,
+    pair_ref,
+    mask_ref,
+    gain_ref,
+    proj_ref,
+    gate_ref,
+    out_gate_ref,
+    mine_ref,
+    other_ref,
+    left_ref,
+    gating_ref,
+    sum_ref,
+    swap_ref,
+    left_wide,
+    right_wide,
 ):
     rows, cols, width = pair_ref.shape
     normed = normed_rows(pair_ref, gain_ref)
@@ -141,56 +158,150 @@
     stacked = jnp.concatenate([proj_ref[...], gate_ref[...]], axis=1)
     both = jnp.dot(normed, stacked, preferred_element_type=jnp.float32)
     act = masked * jax.nn.sigmoid(both[:, width:]) * both[:, :width]
-    left_ref[...] = act.astype(jnp.bfloat16).astype(jnp.float32)
+    left_ref[...] = act.astype(jnp.bfloat16).reshape(rows, cols, width)
     gating_ref[...] = jax.nn.sigmoid(
         jnp.dot(normed, out_gate_ref[...], preferred_element_type=jnp.float32)
     )
-
-
-def triangle_kernel(rows, cols, flags_ref, left_ref, mine_ref, other_ref, sum_ref, held):
-    width = held.shape[1]
-    tile = rows * cols
-    core = flags_ref[2]
-    held[pl.ds(pl.multiple_of(core * tile, tile), tile), :] = (
-        mine_ref[...].astype(jnp.float32).reshape(tile, width)
-    )
-    held[pl.ds(pl.multiple_of((1 - core) * tile, tile), tile), :] = (
-        other_ref[...].astype(jnp.float32).reshape(tile, width)
-    )
-    group = 5
-
-    def of_rows(block, _):
-        def of_col(k, totals):
-            right = held[pl.ds(k, 2 * rows, stride=cols), :]
-            return tuple(
-                totals[g] + left_ref[pl.ds((block * group + g) * cols + k, 1), :] * right
-                for g in range(group)
+    triangle([left_ref], [[mine_ref], [other_ref]], sum_ref, left_wide, right_wide)
+    keeps_near = flags_ref[3] == 1
+
+    @pl.when(keeps_near)
+    def _():
+        swap_ref[...] = left_ref[...]
+
+    @pl.when(jnp.logical_not(keeps_near))
+    def _():
+        swap_ref[:, : 2 * rows] = sum_ref[...]
+        swap_ref[:, 2 * rows :] = jnp.zeros((rows, cols - 2 * rows, width), jnp.bfloat16)
+
+
+def run_sums(count, length):
+    row = lax.broadcasted_iota(jnp.int32, (count, count * length), 0) * length
+    col = lax.broadcasted_iota(jnp.int32, (count, count * length), 1)
+    return jnp.where((col >= row) & (col < row + length), 1.0, 0.0).astype(jnp.bfloat16)
+
+
+def triangle(lefts, tiles, sum_ref, left_wide, right_wide):
+    rows, cols, width = lefts[0].shape
+    size = rows * cols
+    few = VECTOR_ROWS
+    many = rows - few
+    for b, left_ref in enumerate(lefts):
+        left_wide[b * size : (b + 1) * size, :] = (
+            left_ref[...].astype(jnp.float32).reshape(size, width)
+        )
+    held = few * cols
+    blocks = [block for tile in tiles for block in tile]
+    for n, block in enumerate(blocks):
+        right_wide[n * held : (n + 1) * held, :] = (
+            block[:few].astype(jnp.float32).reshape(held, width)
+        )
+    sum_many, sum_few = run_sums(many, cols), run_sums(few, 8)
+
+    def of_rows(step, _):
+        lines = [step * PAIR + n for n in range(PAIR)]
+        narrow = [[left_ref[line] for line in lines] for left_ref in lefts]
+        wide = [
+            [
+                left_wide[pl.ds(pl.multiple_of(b * size + line * cols, 8), cols), :].reshape(
+                    cols // 8, 8, width
+                )
+                for line in lines
+            ]
+            for b in range(len(lefts))
+        ]
+        for t, tile in enumerate(tiles):
+            last, partial = 0.0, [0.0] * PAIR
+            for b, block in enumerate(tile):
+                right = block[few:]
+                products = jnp.concatenate(
+                    [(right * left[None]).reshape(many * cols, width) for left in narrow[b]], axis=1
+                )
+                last = last + jnp.dot(sum_many, products, preferred_element_type=jnp.float32)
+                n = t * len(tile) + b
+                right = right_wide[n * held : (n + 1) * held, :]
+                right = right.reshape(few, cols // 8, 8, width)
+                partial = [
+                    total + jnp.sum(right * left[None], axis=1).reshape(few * 8, width)
+                    for total, left in zip(partial, wide[b])
+                ]
+            first = jnp.dot(
+                sum_few,
+                jnp.concatenate(partial, axis=1).astype(jnp.bfloat16),
+                preferred_element_type=jnp.float32,
             )
-
-        start = tuple(jnp.zeros((2 * rows, width), jnp.float32) for _ in range(group))
-        totals = lax.fori_loop(0, cols, of_col, start, unroll=8)
-        for g in range(group):
-            sum_ref[block * group + g] = totals[g].astype(jnp.bfloat16)
+            sums = jnp.concatenate([first, last], axis=0).astype(sum_ref.dtype)
+            for n, line in enumerate(lines):
+                sum_ref[line, t * rows : (t + 1) * rows, :] = sums[:, n * width : (n + 1) * width]
         return 0
 
-    lax.fori_loop(0, rows // group, of_rows, 0)
+    lax.fori_loop(0, rows // PAIR, of_rows, 0, unroll=UNROLL)
+
+
+def middle_kernel(
+    flags_ref,
+    left_ref,
+    next_mine,
+    next_other,
+    pair_mine,
+    pair_other,
+    kept_ref,
+    sent_ref,
+    both,
+    left_wide,
+    right_wide,
+):
+    keeps_near = flags_ref[3]
+    triangle([left_ref], [[next_mine], [next_other]], both.at[1 - keeps_near], left_wide, right_wide)
+    triangle([left_ref], [[pair_mine], [pair_other]], both.at[keeps_near], left_wide, right_wide)
+    kept_ref[...] = both[0]
+    sent_ref[...] = both[1]
+
+
+def last_kernel(
+    flags_ref, left_ref, given_ref, straight_ref, across_ref, sum_ref, left_wide, right_wide
+):
+    @pl.when(flags_ref[3] == 0)
+    def _():
+        triangle(
+            [left_ref, given_ref], [[straight_ref, across_ref]], sum_ref, left_wide, right_wide
+        )
 
 
 def finish_kernel(
-    flags_ref, near0, near1, far0, far1, gnear0, gnear1, gfar0, gfar1, gain_ref, proj_ref, gating_ref, out_ref
-):
+    flags_ref,
+    left_ref,
+    given_ref,
+    straight_ref,
+    across_ref,
+    mine_ref,
+    near_ref,
+    kept_ref,
+    kept_given_ref,
+    gain_ref,
+    proj_ref,
+    gating_ref,
+    out_ref,
+    other_ref,
+    left_wide,
+    right_wide,
+):
+    last_kernel(
+        flags_ref, left_ref, given_ref, straight_ref, across_ref, other_ref, left_wide, right_wide
+    )
     rows, cols, width = out_ref.shape
-    keeps_near, odd = flags_ref[3] == 1, flags_ref[4] == 1
-
-    def total(a, b, c, d):
-        f = lambda ref: ref[...].astype(jnp.float32)
-        return jnp.where(keeps_near, f(a) + f(b), f(c) + f(d))
-
-    first = total(near0, gnear0, far0, gfar0)
-    second = total(near1, gnear1, far1, gfar1)
-    hidden = jnp.concatenate(
-        [jnp.where(odd, second, first), jnp.where(odd, first, second)], axis=1
-    ).reshape(rows * cols, width)
+    core, keeps_near, odd = flags_ref[2] == 1, flags_ref[3] == 1, flags_ref[4] == 1
+    near = near_ref[...].astype(jnp.float32) + given_ref[:, : 2 * rows].astype(jnp.float32)
+    far = jnp.concatenate([mine_ref[...], other_ref[...]], axis=1)
+    swapped = kept_ref[...].astype(jnp.float32) + kept_given_ref[...].astype(jnp.float32)
+    whole_near, next_near = keeps_near, jnp.logical_not(keeps_near)
+    first = jnp.where(whole_near, near, swapped)
+    second = jnp.where(next_near, far, swapped)
+    parts = []
+    for block in (jnp.where(odd, second, first), jnp.where(odd, first, second)):
+        own, partner = block[:, :rows], block[:, rows:]
+        parts += [jnp.where(core, partner, own), jnp.where(core, own, partner)]
+    hidden = jnp.concatenate(parts, axis=1).reshape(rows * cols, width)
     normed = layer_norm(hidden, gain_ref[...]).astype(jnp.bfloat16)
     projected = jnp.dot(normed, proj_ref[...], preferred_element_type=jnp.float32)
     out_ref[...] = (gating_ref[...] * projected).astype(jnp.bfloat16).reshape(rows, cols, width)
@@ -242,14 +353,15 @@
     over_core = [(p, p ^ 2) for p in places]
     over_next = [(p, p ^ 4) for p in places]
     over_pair = [(p, p ^ 8) for p in places]
-    near_sums = [(p, p ^ 1) for p in places if p // 8 != p % 2]
-    far_sums = [(p, p ^ 1) for p in places if p // 8 == p % 2]
+    over_col = [(p, p ^ 1) for p in places]
+    keeps_far = lambda p: p // 8 != p % 2
+    straight = [(p, p ^ 4) for p in places if keeps_far(p ^ 4)]
+    across = [(p, p ^ 5) for p in places if keeps_far(p ^ 5)]
     send = lambda value, pairs: lax.ppermute(value, LINE, pairs)
 
     steps = 4
     block = rows // steps
     pair_spec = pl.BlockSpec((block, cols, width), lambda s, _: (s, 0, 0))
-    flat_spec = pl.BlockSpec((block * cols, width), lambda s, _: (s, 0))
     square = whole((width, width))
     vector = whole((1, width))
     right = call(
@@ -265,47 +377,69 @@
     from_next = send(right, over_next)
     from_core = send(right, over_core)
 
-    left, gating = call(
+    after = lambda value, *last: lax.optimization_barrier((value, *last))[0]
+    bf16 = lambda *shape: jax.ShapeDtypeStruct(shape, jnp.bfloat16)
+    f32 = lambda *shape: jax.ShapeDtypeStruct(shape, jnp.float32)
+    tile_spec = whole((rows, cols, width))
+    flat_spec = whole((tile, width))
+    two, one = (rows, 2 * rows, width), (rows, rows, width)
+    held = VECTOR_ROWS * cols
+    wide = lambda lefts, blocks: [
+        pltpu.VMEM((lefts * tile, width), jnp.float32),
+        pltpu.VMEM((blocks * held, width), jnp.float32),
+    ]
+    left, gating, near, swap = call(
         left_kernel,
-        2.9,
-        (
-            jax.ShapeDtypeStruct((tile, width), jnp.float32),
-            jax.ShapeDtypeStruct((tile, width), jnp.float32),
-        ),
-        [pair_spec, whole(mask.shape), vector, square, square, square],
-        (flat_spec, flat_spec),
-        (steps,),
-    )(flags, pair_rep, mask, ln_gain, left_proj, left_gate, out_gate)
-
-    tile_spec = whole((rows, cols, width))
-    sums = call(
-        functools.partial(triangle_kernel, rows, cols),
-        4.2,
-        jax.ShapeDtypeStruct((rows, 2 * rows, width), jnp.bfloat16),
-        [whole((tile, width)), tile_spec, tile_spec],
-        whole((rows, 2 * rows, width)),
+        4.0,
+        (bf16(rows, cols, width), f32(tile, width), bf16(*two), bf16(rows, cols, width)),
+        [tile_spec, whole(mask.shape), vector, square, square, square, tile_spec, tile_spec],
+        (tile_spec, flat_spec, whole(two), tile_spec),
         (1,),
-        [pltpu.VMEM((2 * tile, width), jnp.float32)],
-    )
-    near0 = sums(flags, left, right, from_core)
-    gnear0 = send(near0, near_sums)
-    near1 = sums(flags, left, from_next, send(from_next, over_core))
-    gnear1 = send(near1, near_sums)
-    from_far = send(from_pair, over_next)
-    far0 = sums(flags, left, from_pair, send(from_pair, over_core))
-    gfar0 = send(far0, far_sums)
-    far1 = sums(flags, left, from_far, send(from_far, over_core))
-    gfar1 = send(far1, far_sums)
-
-    part = whole((rows, 2 * rows, width))
+        wide(1, 2),
+    )(flags, pair_rep, mask, ln_gain, left_proj, left_gate, out_gate, right, from_core)
+    given = send(swap, over_col)
+
+    from_pair = after(from_pair, left)
+    from_next = after(from_next, from_pair, given)
+    far_straight, far_across = send(from_pair, straight), send(from_pair, across)
+    kept, sent = call(
+        middle_kernel,
+        5.7,
+        (bf16(*two), bf16(*two)),
+        [tile_spec] * 5,
+        (whole(two), whole(two)),
+        (1,),
+        [pltpu.VMEM((2, *two), jnp.bfloat16)] + wide(1, 2),
+    )(flags, left, from_next, send(from_next, over_core), from_pair, send(from_pair, over_core))
+    kept_given = send(sent, over_col)
+
+    far_straight, far_across = after(far_straight, sent), after(far_across, sent)
+    other_straight, other_across = send(far_straight, over_core), send(far_across, over_core)
+    mine = call(
+        last_kernel, 2.9, f32(*one), [tile_spec] * 4, whole(one), (1,), wide(2, 2)
+    )(flags, left, given, far_straight, far_across)
     return call(
         finish_kernel,
-        2.0,
-        jax.ShapeDtypeStruct((rows, cols, width), jnp.bfloat16),
-        [part] * 8 + [vector, square, whole((tile, width))],
+        5.0,
+        bf16(rows, cols, width),
+        [tile_spec] * 4 + [whole(one)] + [whole(two)] * 3 + [vector, square, flat_spec],
         tile_spec,
         (1,),
-    )(flags, near0, near1, far0, far1, gnear0, gnear1, gfar0, gfar1, hidden_gain, out_proj, gating)
+        [pltpu.VMEM(one, jnp.float32)] + wide(2, 2),
+    )(
+        flags,
+        left,
+        given,
+        other_straight,
+        other_across,
+        mine,
+        near,
+        kept,
+        kept_given,
+        hidden_gain,
+        out_proj,
+        gating,
+    )
 
 
 def solution(mesh):

time: 64 us -> 54.1 us (0.85)
  the two profiles are of different devices: /device:TPU:25 before, /device:TPU:2 now
where the time goes in v2:
time: 54.1 us; the launch traced here: 53.8 us
  waiting for transfers between devices  22.6 us (42%)
  Pallas kernels  18.7 us (35%)
  starting transfers between devices  9.97 us (18%)
  local copies, waits for them, and re-layouts  2.42 us (4%)
    ppermute x11, waiting for transfers between devices, exchanged(): send = lambda value, pairs: lax.ppermute(value, LINE, pairs)  22.6 us
    ppermute x11, starting transfers between devices, exchanged(): send = lambda value, pairs: lax.ppermute(value, LINE, pairs)  9.97 us
    pallas_call x1, Pallas kernels, exchanged(): call(middle_kernel, 5.7, (bf16(*two), bf16(*two)), [tile_spec] * 5, (whol...  5.01 us
    pallas_call x1, Pallas kernels, exchanged(): call(finish_kernel, 5.0, bf16(rows, cols, width), [tile_spec] * 4 + [whol...  4.63 us
    pallas_call x1, Pallas kernels, exchanged(): call(left_kernel, 4.0, (bf16(rows, cols, width), f32(tile, width), bf16(*...  3.79 us
    pallas_call x1, Pallas kernels, exchanged(): call(last_kernel, 2.9, f32(*one), [tile_spec] * 4, whole(one), (1,), wide...  3.05 us
    unnamed x20, local copies, waits for them, and re-layouts  2.33 us
    pallas_call x1, Pallas kernels, exchanged(): call(right_kernel, 2.2, jax.ShapeDtypeStruct((rows, cols, width), jnp.bfl...  2.22 us
  transfers between devices with their start and end apart: 11, of which 5 were waited for; matrix products, arithmetic and copies ran while one was open for 0% of the time, Pallas kernels for 22%

profile of v2, /device:TPU:2, one launch (start us, length us, event | category | flops | bytes accessed | tf_op | source)
XLA Modules:
  0.0 53.8 jit_solution(3701808915437724278)
XLA Ops:
  0.0 0.0 copy-start.7
  0.0 0.0 copy-start.8
  0.0 0.0 copy-start.1
  0.0 0.0 copy-start.2
  0.1 0.1 stack.27.flags_ref
  0.1 0.5 %copy-done.7 = s32[160]{0:T(256)S(1)} copy-done((s32[160]{0:T(256)S(1)}, s32[160]{0:T(256)}, u32[]{:S(2)}) %copy-start.7) | copy-done | bytes 664
  0.7 0.0 copy-done.8
  0.7 0.1 copy-done.1
  0.8 0.0 copy-done.2
  0.8 0.0 copy-start
  0.8 1.0 %copy-done = bf16[20,80,128]{2,1,0:T(8,128)(2,1)S(1)} copy-done((bf16[20,80,128]{2,1,0:T(8,128)(2,1)S(1)}, bf16[20,80,128]{2,1,0:T(8,128)(2,1)}, u32[]{:S(2)}) %copy-start) | copy-done | bytes 409624
  1.8 0.0 copy-start.3
  1.8 0.0 copy-start.4
  1.8 0.0 copy-start.5
  1.8 2.2 %shard_map.100.mine_ref = bf16[20,80,128]{2,1,0:T(8,128)(2,1)S(1)} custom-call(s32[5]{0:T(128)S(1)} %stack.27.flags_ref, bf16[20,80,128]{2,1,0:T(8,128)(2,1)S(1)} %copy-done, s32[1,160]{1,0:T(1,128)S(1)} %bitcast.8, f32[1,128]{1,0:T(1,128)S(1)} %bitcast.10, bf16[128,128]{1,0:T(8,128)(2,1)S(1)} %copy-done.1, bf16[128,128]{1,0:T(8,128)(2,1)S(1)} %copy-done.2), custom_call_target="tpu_custom_call" | custom-call | flops 2420000000 | bytes 6600000 | tf_op jit(solution)/shard_map/pallas_call | solution.py:367
  4.0 0.1 collective-permute-start
  4.1 2.7 %collective-permute-start.2 = (bf16[20,80,128]{2,1,0:T(8,128)(2,1)S(1)}, bf16[20,80,128]{2,1,0:T(8,128)(2,1)S(1)}, u32[]{:S(2)}, u32[]{:S(2)}) collective-permute-start(bf16[20,80,128]{2,1,0:T(8,128)(2,1)S(1)} %shard_map.100.mine_ref), channel_id=1, source_target_pairs={{0,8},{1,9},{2,10},{3,11},{4,12},{5,13},{6,14},{7,15},{8,0},{9,1},... | collective-permute-start | bytes 1228808 | tf_op jit(solution)/shard_map/ppermute | solution.py:360
  6.8 1.6 %collective-permute-start.4 = (bf16[20,80,128]{2,1,0:T(8,128)(2,1)S(1)}, bf16[20,80,128]{2,1,0:T(8,128)(2,1)S(1)}, u32[]{:S(2)}, u32[]{:S(2)}) collective-permute-start(bf16[20,80,128]{2,1,0:T(8,128)(2,1)S(1)} %shard_map.100.mine_ref), channel_id=1, source_target_pairs={{0,4},{1,5},{2,6},{3,7},{4,0},{5,1},{6,2},{7,3},{8,12},{9,13},{10,... | collective-permute-start | bytes 1228808 | tf_op jit(solution)/shard_map/ppermute | solution.py:360
  8.4 0.0 collective-permute-done.other_ref
  8.4 0.0 copy-done.3
  8.4 0.0 copy-done.4
  8.4 0.0 copy-done.5
  8.4 3.8 %shard_map.101 = (bf16[20,80,128]{2,1,0:T(8,128)(2,1)S(1)}, f32[1600,128]{1,0:T(8,128)S(1)}, bf16[20,40,128]{2,1,0:T(8,128)(2,1)S(1)}, bf16[20,80,128]{2,1,0:T(8,128)(2,1)S(1)}) custom-call(s32[5]{0:T(128)S(1)} %stack.27.flags_ref, bf16[20,80,128]{2,1,0:T(8,128)(2,1)S(1)} %copy-done, s32[1,160]{1,0:T(1,128)S(1)} %bitcast.9, f32[1,128]{1,0:T(1,128)S(1)} %bitcast.11, ...), custom_call_target="tpu_custom_call" | custom-call | flops 4400000000 | bytes 12000000 | tf_op jit(solution)/shard_map/pallas_call | solution.py:391
  12.2 0.5 collective-permute-start.1
  12.7 13.1 %collective-permute-done.2.pair_mine = bf16[20,80,128]{2,1,0:T(8,128)(2,1)S(1)} collective-permute-done((bf16[20,80,128]{2,1,0:T(8,128)(2,1)S(1)}, bf16[20,80,128]{2,1,0:T(8,128)(2,1)S(1)}, u32[]{:S(2)}, u32[]{:S(2)}) %collective-permute-start.2) | collective-permute-done | bytes 409632 | tf_op jit(solution)/shard_map/ppermute | solution.py:360
  25.8 0.0 collective-permute-start.6
  25.8 0.2 collective-permute-done.4.next_mine
  26.0 0.0 collective-permute-done.1.given_ref
  26.0 0.3 collective-permute-start.5
  26.3 1.3 %collective-permute-start.8 = (bf16[20,80,128]{2,1,0:T(8,128)(2,1)S(1)}, bf16[20,80,128]{2,1,0:T(8,128)(2,1)S(1)}, u32[]{:S(2)}, u32[]{:S(2)}) collective-permute-start(bf16[20,80,128]{2,1,0:T(8,128)(2,1)S(1)} %collective-permute-done.2.pair_mine), channel_id=1, source_target_pairs={{0,5},{2,7},{4,1},{6,3},{9,12},{11,14},{13,8},{15,10},{16,21},{18,... | collective-permute-start | bytes 1228808 | tf_op jit(solution)/shard_map/ppermute | solution.py:360
  27.6 3.0 %collective-permute-start.3 = (bf16[20,80,128]{2,1,0:T(8,128)(2,1)S(1)}, bf16[20,80,128]{2,1,0:T(8,128)(2,1)S(1)}, u32[]{:S(2)}, u32[]{:S(2)}) collective-permute-start(bf16[20,80,128]{2,1,0:T(8,128)(2,1)S(1)} %collective-permute-done.2.pair_mine), channel_id=1, source_target_pairs={{1,5},{3,7},{5,1},{7,3},{8,12},{10,14},{12,8},{14,10},{17,21},{19,... | collective-permute-start | bytes 1228808 | tf_op jit(solution)/shard_map/ppermute | solution.py:360
  30.6 0.0 collective-permute-done.6.pair_other
  30.6 0.0 collective-permute-done.5.next_other
  30.6 5.0 %shard_map.102 = (bf16[20,40,128]{2,1,0:T(8,128)(2,1)S(1)}, bf16[20,40,128]{2,1,0:T(8,128)(2,1)S(1)}) custom-call(s32[5]{0:T(128)S(1)} %stack.27.flags_ref, bf16[20,80,128]{2,1,0:T(8,128)(2,1)S(1)} %get-tuple-element.15.left_ref, bf16[20,80,128]{2,1,0:T(8,128)(2,1)S(1)} %collective-permute-done.4.next_mine, ...), custom_call_target="tpu_custom_call" | custom-call | flops 6270000128 | bytes 17100000 | tf_op jit(solution)/shard_map/pallas_call | solution.py:405
  35.7 5.0 %collective-permute-done.8.across_ref = bf16[20,80,128]{2,1,0:T(8,128)(2,1)S(1)} collective-permute-done((bf16[20,80,128]{2,1,0:T(8,128)(2,1)S(1)}, bf16[20,80,128]{2,1,0:T(8,128)(2,1)S(1)}, u32[]{:S(2)}, u32[]{:S(2)}) %collective-permute-start.8) | collective-permute-done | bytes 409632 | tf_op jit(solution)/shard_map/ppermute | solution.py:360
  40.6 0.0 copy-start.6
  40.6 0.4 collective-permute-done.3.straight_ref
  41.0 0.0 collective-permute-start.9
  41.0 0.5 collective-permute-start.7
  41.6 0.0 collective-permute-start.10
  41.6 3.0 %shard_map.103.mine_ref = f32[20,20,128]{2,1,0:T(8,128)S(1)} custom-call(s32[5]{0:T(128)S(1)} %stack.27.flags_ref, bf16[20,80,128]{2,1,0:T(8,128)(2,1)S(1)} %get-tuple-element.15.left_ref, bf16[20,80,128]{2,1,0:T(8,128)(2,1)S(1)} %collective-permute-done.1.given_ref, bf16[20,80,128]{2,1,0:T(8,128)(2,1)S(1)} %collective-permute-done.3.straight_ref, ...), custom_call_target="tpu_custom_call" | custom-call | flops 3190000128 | bytes 8700000 | tf_op jit(solution)/shard_map/pallas_call | solution.py:418
  44.6 3.9 %collective-permute-done.10.kept_given_ref = bf16[20,40,128]{2,1,0:T(8,128)(2,1)S(1)} collective-permute-done((bf16[20,40,128]{2,1,0:T(8,128)(2,1)S(1)}, bf16[20,40,128]{2,1,0:T(8,128)(2,1)S(1)}, u32[]{:S(2)}, u32[]{:S(2)}) %collective-permute-start.10) | collective-permute-done | bytes 204832 | tf_op jit(solution)/shard_map/ppermute | solution.py:360
  48.5 0.0 collective-permute-done.9.across_ref
  48.5 0.0 collective-permute-done.7.straight_ref
  48.5 0.0 copy-start.9
  48.6 0.0 copy-done.6
  48.6 0.6 %copy-done.9 = f32[128]{0:T(128)S(1)} copy-done((f32[128]{0:T(128)S(1)}, f32[128]{0:T(128)}, u32[]{:S(2)}) %copy-start.9) | copy-done | bytes 536
  49.2 4.6 %shard_map.104 = bf16[20,80,128]{2,1,0:T(8,128)(2,1)} custom-call(s32[5]{0:T(128)S(1)} %stack.27.flags_ref, bf16[20,80,128]{2,1,0:T(8,128)(2,1)S(1)} %get-tuple-element.15.left_ref, bf16[20,80,128]{2,1,0:T(8,128)(2,1)S(1)} %collective-permute-done.1.given_ref, bf16[20,80,128]{2,1,0:T(8,128)(2,1)S(1)} %collective-permute-done.7.straight_ref, ...), custom_call_target="tpu_custom_call" | custom-call | flops 5500000256 | bytes 15000000 | tf_op jit(solution)/shard_map/pallas_call | solution.py:421
Async XLA Ops:
  0.0 0.7 %copy-start.7 = (s32[160]{0:T(256)S(1)}, s32[160]{0:T(256)}, u32[]{:S(2)}) copy-start(s32[160]{0:T(256)} %param.11) | copy-start | bytes 1924
  0.0 0.7 %copy-start.8 = (f32[128]{0:T(128)S(1)}, f32[128]{0:T(128)}, u32[]{:S(2)}) copy-start(f32[128]{0:T(128)} %param.12) | copy-start | bytes 1540
  0.0 0.8 %copy-start.1 = (bf16[128,128]{1,0:T(8,128)(2,1)S(1)}, bf16[128,128]{1,0:T(8,128)(2,1)}, u32[]{:S(2)}) copy-start(bf16[128,128]{1,0:T(8,128)(2,1)} %proj_ref.3) | copy-start | bytes 98308
  0.0 0.8 %copy-start.2 = (bf16[128,128]{1,0:T(8,128)(2,1)S(1)}, bf16[128,128]{1,0:T(8,128)(2,1)}, u32[]{:S(2)}) copy-start(bf16[128,128]{1,0:T(8,128)(2,1)} %gate_ref.2) | copy-start | bytes 98308
  0.8 1.0 %copy-start = (bf16[20,80,128]{2,1,0:T(8,128)(2,1)S(1)}, bf16[20,80,128]{2,1,0:T(8,128)(2,1)}, u32[]{:S(2)}) copy-start(bf16[20,80,128]{2,1,0:T(8,128)(2,1)} %pair_ref.3) | copy-start | bytes 1228804
  1.8 6.5 %copy-start.3 = (bf16[128,128]{1,0:T(8,128)(2,1)S(1)}, bf16[128,128]{1,0:T(8,128)(2,1)}, u32[]{:S(2)}) copy-start(bf16[128,128]{1,0:T(8,128)(2,1)} %proj_ref.4) | copy-start | bytes 98308
  1.8 6.5 %copy-start.4 = (bf16[128,128]{1,0:T(8,128)(2,1)S(1)}, bf16[128,128]{1,0:T(8,128)(2,1)}, u32[]{:S(2)}) copy-start(bf16[128,128]{1,0:T(8,128)(2,1)} %gate_ref.3) | copy-start | bytes 98308
  1.8 6.6 %copy-start.5 = (bf16[128,128]{1,0:T(8,128)(2,1)S(1)}, bf16[128,128]{1,0:T(8,128)(2,1)}, u32[]{:S(2)}) copy-start(bf16[128,128]{1,0:T(8,128)(2,1)} %out_gate_ref.1) | copy-start | bytes 98308
  4.0 4.3 %collective-permute-start = (bf16[20,80,128]{2,1,0:T(8,128)(2,1)S(1)}, bf16[20,80,128]{2,1,0:T(8,128)(2,1)S(1)}, u32[]{:S(2)}, u32[]{:S(2)}) collective-permute-start(bf16[20,80,128]{2,1,0:T(8,128)(2,1)S(1)} %shard_map.100.mine_ref), channel_id=1, source_target_pairs={{0,2},{1,3},{2,0},{3,1},{4,6},{5,7},{6,4},{7,5},{8,10},{9,11},{10,... | collective-permute-start | bytes 1228808 | tf_op jit(solution)/shard_map/ppermute | solution.py:360
  4.1 21.7 %collective-permute-start.2 = (bf16[20,80,128]{2,1,0:T(8,128)(2,1)S(1)}, bf16[20,80,128]{2,1,0:T(8,128)(2,1)S(1)}, u32[]{:S(2)}, u32[]{:S(2)}) collective-permute-start(bf16[20,80,128]{2,1,0:T(8,128)(2,1)S(1)} %shard_map.100.mine_ref), channel_id=1, source_target_pairs={{0,8},{1,9},{2,10},{3,11},{4,12},{5,13},{6,14},{7,15},{8,0},{9,1},... | collective-permute-start | bytes 1228808 | tf_op jit(solution)/shard_map/ppermute | solution.py:360
  6.8 19.2 %collective-permute-start.4 = (bf16[20,80,128]{2,1,0:T(8,128)(2,1)S(1)}, bf16[20,80,128]{2,1,0:T(8,128)(2,1)S(1)}, u32[]{:S(2)}, u32[]{:S(2)}) collective-permute-start(bf16[20,80,128]{2,1,0:T(8,128)(2,1)S(1)} %shard_map.100.mine_ref), channel_id=1, source_target_pairs={{0,4},{1,5},{2,6},{3,7},{4,0},{5,1},{6,2},{7,3},{8,12},{9,13},{10,... | collective-permute-start | bytes 1228808 | tf_op jit(solution)/shard_map/ppermute | solution.py:360
  12.2 13.8 %collective-permute-start.1 = (bf16[20,80,128]{2,1,0:T(8,128)(2,1)S(1)}, bf16[20,80,128]{2,1,0:T(8,128)(2,1)S(1)}, u32[]{:S(2)}, u32[]{:S(2)}) collective-permute-start(bf16[20,80,128]{2,1,0:T(8,128)(2,1)S(1)} %get-tuple-element.16), channel_id=1, source_target_pairs={{0,1},{1,0},{2,3},{3,2},{4,5},{5,4},{6,7},{7,6},{8,9},{9,8},{10,11... | collective-permute-start | bytes 1228808 | tf_op jit(solution)/shard_map/ppermute | solution.py:360
  25.8 4.8 %collective-permute-start.6 = (bf16[20,80,128]{2,1,0:T(8,128)(2,1)S(1)}, bf16[20,80,128]{2,1,0:T(8,128)(2,1)S(1)}, u32[]{:S(2)}, u32[]{:S(2)}) collective-permute-start(bf16[20,80,128]{2,1,0:T(8,128)(2,1)S(1)} %collective-permute-done.2.pair_mine), channel_id=1, source_target_pairs={{0,2},{1,3},{2,0},{3,1},{4,6},{5,7},{6,4},{7,5},{8,10},{9,11},{10,... | collective-permute-start | bytes 1228808 | tf_op jit(solution)/shard_map/ppermute | solution.py:360
  26.0 4.7 %collective-permute-start.5 = (bf16[20,80,128]{2,1,0:T(8,128)(2,1)S(1)}, bf16[20,80,128]{2,1,0:T(8,128)(2,1)S(1)}, u32[]{:S(2)}, u32[]{:S(2)}) collective-permute-start(bf16[20,80,128]{2,1,0:T(8,128)(2,1)S(1)} %collective-permute-done.4.next_mine), channel_id=1, source_target_pairs={{0,2},{1,3},{2,0},{3,1},{4,6},{5,7},{6,4},{7,5},{8,10},{9,11},{10,... | collective-permute-start | bytes 1228808 | tf_op jit(solution)/shard_map/ppermute | solution.py:360
  26.3 14.3 %collective-permute-start.8 = (bf16[20,80,128]{2,1,0:T(8,128)(2,1)S(1)}, bf16[20,80,128]{2,1,0:T(8,128)(2,1)S(1)}, u32[]{:S(2)}, u32[]{:S(2)}) collective-permute-start(bf16[20,80,128]{2,1,0:T(8,128)(2,1)S(1)} %collective-permute-done.2.pair_mine), channel_id=1, source_target_pairs={{0,5},{2,7},{4,1},{6,3},{9,12},{11,14},{13,8},{15,10},{16,21},{18,... | collective-permute-start | bytes 1228808 | tf_op jit(solution)/shard_map/ppermute | solution.py:360
  27.6 13.5 %collective-permute-start.3 = (bf16[20,80,128]{2,1,0:T(8,128)(2,1)S(1)}, bf16[20,80,128]{2,1,0:T(8,128)(2,1)S(1)}, u32[]{:S(2)}, u32[]{:S(2)}) collective-permute-start(bf16[20,80,128]{2,1,0:T(8,128)(2,1)S(1)} %collective-permute-done.2.pair_mine), channel_id=1, source_target_pairs={{1,5},{3,7},{5,1},{7,3},{8,12},{10,14},{12,8},{14,10},{17,21},{19,... | collective-permute-start | bytes 1228808 | tf_op jit(solution)/shard_map/ppermute | solution.py:360
  40.6 7.9 %copy-start.6 = (bf16[128,128]{1,0:T(8,128)(2,1)S(1)}, bf16[128,128]{1,0:T(8,128)(2,1)}, u32[]{:S(2)}) copy-start(bf16[128,128]{1,0:T(8,128)(2,1)} %proj_ref.5) | copy-start | bytes 98308
  41.0 7.5 %collective-permute-start.9 = (bf16[20,80,128]{2,1,0:T(8,128)(2,1)S(1)}, bf16[20,80,128]{2,1,0:T(8,128)(2,1)S(1)}, u32[]{:S(2)}, u32[]{:S(2)}) collective-permute-start(bf16[20,80,128]{2,1,0:T(8,128)(2,1)S(1)} %collective-permute-done.8.across_ref), channel_id=1, source_target_pairs={{0,2},{1,3},{2,0},{3,1},{4,6},{5,7},{6,4},{7,5},{8,10},{9,11},{10,... | collective-permute-start | bytes 1228808 | tf_op jit(solution)/shard_map/ppermute | solution.py:360
  41.0 7.5 %collective-permute-start.7 = (bf16[20,80,128]{2,1,0:T(8,128)(2,1)S(1)}, bf16[20,80,128]{2,1,0:T(8,128)(2,1)S(1)}, u32[]{:S(2)}, u32[]{:S(2)}) collective-permute-start(bf16[20,80,128]{2,1,0:T(8,128)(2,1)S(1)} %collective-permute-done.3.straight_ref), channel_id=1, source_target_pairs={{0,2},{1,3},{2,0},{3,1},{4,6},{5,7},{6,4},{7,5},{8,10},{9,11},{10,... | collective-permute-start | bytes 1228808 | tf_op jit(solution)/shard_map/ppermute | solution.py:360
  41.6 7.0 %collective-permute-start.10 = (bf16[20,40,128]{2,1,0:T(8,128)(2,1)S(1)}, bf16[20,40,128]{2,1,0:T(8,128)(2,1)S(1)}, u32[]{:S(2)}, u32[]{:S(2)}) collective-permute-start(bf16[20,40,128]{2,1,0:T(8,128)(2,1)S(1)} %get-tuple-element.19), channel_id=1, source_target_pairs={{0,1},{1,0},{2,3},{3,2},{4,5},{5,4},{6,7},{7,6},{8,9},{9,8},{10,11... | collective-permute-start | bytes 614408 | tf_op jit(solution)/shard_map/ppermute | solution.py:360
  48.5 0.7 %copy-start.9 = (f32[128]{0:T(128)S(1)}, f32[128]{0:T(128)}, u32[]{:S(2)}) copy-start(f32[128]{0:T(128)} %param.17) | copy-start | bytes 1540

commit v3 on v2

--- a/solution.py
+++ b/solution.py
@@ -241,21 +241,24 @@
 def middle_kernel(
     flags_ref,
     left_ref,
-    next_mine,
-    next_other,
-    pair_mine,
-    pair_other,
-    kept_ref,
-    sent_ref,
+    left_other,
+    next_ref,
+    pair_ref,
+    kept_own,
+    kept_other,
+    sent_own,
+    sent_other,
     both,
     left_wide,
     right_wide,
 ):
-    keeps_near = flags_ref[3]
-    triangle([left_ref], [[next_mine], [next_other]], both.at[1 - keeps_near], left_wide, right_wide)
-    triangle([left_ref], [[pair_mine], [pair_other]], both.at[keeps_near], left_wide, right_wide)
-    kept_ref[...] = both[0]
-    sent_ref[...] = both[1]
+    rows = left_ref.shape[0]
+    keeps_near = flags_ref[3] == 1
+    for left, kept, sent in ((left_ref, kept_own, sent_own), (left_other, kept_other, sent_other)):
+        triangle([left], [[next_ref], [pair_ref]], both, left_wide, right_wide)
+        of_next, of_pair = both[:, :rows], both[:, rows:]
+        kept[...] = jnp.where(keeps_near, of_next, of_pair).astype(jnp.bfloat16)
+        sent[...] = jnp.where(keeps_near, of_pair, of_next).astype(jnp.bfloat16)
 
 
 def last_kernel(
@@ -266,6 +269,43 @@
         triangle(
             [left_ref, given_ref], [[straight_ref, across_ref]], sum_ref, left_wide, right_wide
         )
+
+
+def finished(flags_ref, own, partner, at, gain_ref, proj_ref, gating_ref):
+    rows, _, width = own.shape
+    core = flags_ref[2] == 1
+    hidden = jnp.concatenate(
+        [jnp.where(core, partner, own), jnp.where(core, own, partner)], axis=1
+    ).reshape(2 * rows * rows, width)
+    normed = layer_norm(hidden, gain_ref[...]).astype(jnp.bfloat16)
+    projected = jnp.dot(normed, proj_ref[...], preferred_element_type=jnp.float32)
+    gating = jnp.where(at == 1, gating_ref[:, 2 * rows :], gating_ref[:, : 2 * rows])
+    return gating * projected.reshape(rows, 2 * rows, width)
+
+
+def swapped_kernel(
+    flags_ref,
+    own_ref,
+    own_given,
+    partner_ref,
+    partner_given,
+    gain_ref,
+    proj_ref,
+    gating_ref,
+    out_ref,
+):
+    keeps_near, odd = flags_ref[3], flags_ref[4]
+    total = lambda a, b: a[...].astype(jnp.float32) + b[...].astype(jnp.float32)
+    at = jnp.where(keeps_near == 1, 1 - odd, odd)
+    out_ref[...] = finished(
+        flags_ref,
+        total(own_ref, own_given),
+        total(partner_ref, partner_given),
+        at,
+        gain_ref,
+        proj_ref,
+        gating_ref,
+    ).astype(jnp.bfloat16)
 
 
 def finish_kernel(
@@ -276,8 +316,7 @@
     across_ref,
     mine_ref,
     near_ref,
-    kept_ref,
-    kept_given_ref,
+    done_ref,
     gain_ref,
     proj_ref,
     gating_ref,
@@ -289,22 +328,17 @@
     last_kernel(
         flags_ref, left_ref, given_ref, straight_ref, across_ref, other_ref, left_wide, right_wide
     )
-    rows, cols, width = out_ref.shape
-    core, keeps_near, odd = flags_ref[2] == 1, flags_ref[3] == 1, flags_ref[4] == 1
+    rows = out_ref.shape[0]
+    keeps_near, odd = flags_ref[3] == 1, flags_ref[4]
     near = near_ref[...].astype(jnp.float32) + given_ref[:, : 2 * rows].astype(jnp.float32)
-    far = jnp.concatenate([mine_ref[...], other_ref[...]], axis=1)
-    swapped = kept_ref[...].astype(jnp.float32) + kept_given_ref[...].astype(jnp.float32)
-    whole_near, next_near = keeps_near, jnp.logical_not(keeps_near)
-    first = jnp.where(whole_near, near, swapped)
-    second = jnp.where(next_near, far, swapped)
-    parts = []
-    for block in (jnp.where(odd, second, first), jnp.where(odd, first, second)):
-        own, partner = block[:, :rows], block[:, rows:]
-        parts += [jnp.where(core, partner, own), jnp.where(core, own, partner)]
-    hidden = jnp.concatenate(parts, axis=1).reshape(rows * cols, width)
-    normed = layer_norm(hidden, gain_ref[...]).astype(jnp.bfloat16)
-    projected = jnp.dot(normed, proj_ref[...], preferred_element_type=jnp.float32)
-    out_ref[...] = (gating_ref[...] * projected).astype(jnp.bfloat16).reshape(rows, cols, width)
+    own = jnp.where(keeps_near, near[:, :rows], mine_ref[...])
+    partner = jnp.where(keeps_near, near[:, rows:], other_ref[...])
+    at = jnp.where(keeps_near, odd, 1 - odd)
+    result = finished(flags_ref, own, partner, at, gain_ref, proj_ref, gating_ref)
+    done = done_ref[...].astype(jnp.float32)
+    out_ref[...] = jnp.concatenate(
+        [jnp.where(at == 1, done, result), jnp.where(at == 1, result, done)], axis=1
+    ).astype(jnp.bfloat16)
 
 
 def call(kernel, micros, out_shape, in_specs, out_specs, grid, scratch=()):
@@ -354,6 +388,7 @@
     over_next = [(p, p ^ 4) for p in places]
     over_pair = [(p, p ^ 8) for p in places]
     over_col = [(p, p ^ 1) for p in places]
+    over_both = [(p, p ^ 3) for p in places]
     keeps_far = lambda p: p // 8 != p % 2
     straight = [(p, p ^ 4) for p in places if keeps_far(p ^ 4)]
     across = [(p, p ^ 5) for p in places if keeps_far(p ^ 5)]
@@ -398,31 +433,44 @@
         wide(1, 2),
     )(flags, pair_rep, mask, ln_gain, left_proj, left_gate, out_gate, right, from_core)
     given = send(swap, over_col)
+    left_other = send(left, over_core)
 
     from_pair = after(from_pair, left)
     from_next = after(from_next, from_pair, given)
     far_straight, far_across = send(from_pair, straight), send(from_pair, across)
-    kept, sent = call(
+    kept_own, kept_other, sent_own, sent_other = call(
         middle_kernel,
         5.7,
-        (bf16(*two), bf16(*two)),
-        [tile_spec] * 5,
-        (whole(two), whole(two)),
+        (bf16(*one),) * 4,
+        [tile_spec] * 4,
+        (whole(one),) * 4,
         (1,),
-        [pltpu.VMEM((2, *two), jnp.bfloat16)] + wide(1, 2),
-    )(flags, left, from_next, send(from_next, over_core), from_pair, send(from_pair, over_core))
-    kept_given = send(sent, over_col)
-
-    far_straight, far_across = after(far_straight, sent), after(far_across, sent)
+        [pltpu.VMEM(two, jnp.float32)] + wide(1, 2),
+    )(flags, left, after(left_other, from_pair), from_next, from_pair)
+    kept_given = send(sent_own, over_col)
+    partner_given = send(sent_other, over_both)
+    partner = send(kept_other, over_core)
+
+    far_straight, far_across = after(far_straight, kept_own), after(far_across, kept_own)
     other_straight, other_across = send(far_straight, over_core), send(far_across, over_core)
     mine = call(
-        last_kernel, 2.9, f32(*one), [tile_spec] * 4, whole(one), (1,), wide(2, 2)
+        last_kernel, 0.1, f32(*one), [tile_spec] * 4, whole(one), (1,), wide(2, 2)
     )(flags, left, given, far_straight, far_across)
+    gating = gating.reshape(rows, cols, width)
+    done = call(
+        swapped_kernel,
+        8.0,
+        bf16(*two),
+        [whole(one)] * 4 + [vector, square, tile_spec],
+        whole(two),
+        (1,),
+    )(flags, kept_own, kept_given, partner, partner_given, hidden_gain, out_proj, gating)
+    other_straight, other_across = after(other_straight, done), after(other_across, done)
     return call(
         finish_kernel,
-        5.0,
+        4.0,
         bf16(rows, cols, width),
-        [tile_spec] * 4 + [whole(one)] + [whole(two)] * 3 + [vector, square, flat_spec],
+        [tile_spec] * 4 + [whole(one), whole(two), whole(two), vector, square, tile_spec],
         tile_spec,
         (1,),
         [pltpu.VMEM(one, jnp.float32)] + wide(2, 2),
@@ -434,8 +482,7 @@
         other_across,
         mine,
         near,
-        kept,
-        kept_given,
+        done,
         hidden_gain,
         out_proj,
         gating,

time: 54.1 us -> 51.7 us (0.956)
  the two profiles are of different devices: /device:TPU:2 before, /device:TPU:25 now
where the time goes in v3:
time: 51.7 us; the launch traced here: 51.4 us
  Pallas kernels  20 us (39%)
  waiting for transfers between devices  19.5 us (38%)
  starting transfers between devices  9.37 us (18%)
  local copies, waits for them, and re-layouts  2.43 us (5%)
    ppermute x12, waiting for transfers between devices, exchanged(): send = lambda value, pairs: lax.ppermute(value, LINE, pairs)  19.5 us
    ppermute x12, starting transfers between devices, exchanged(): send = lambda value, pairs: lax.ppermute(value, LINE, pairs)  9.37 us
    pallas_call x1, Pallas kernels, exchanged(): call(middle_kernel, 5.7, (bf16(*one),) * 4, [tile_spec] * 4, (whole(one),...  5.11 us
    pallas_call x1, Pallas kernels, exchanged(): call(finish_kernel, 4.0, bf16(rows, cols, width), [tile_spec] * 4 + [whol...  4.54 us
    pallas_call x1, Pallas kernels, exchanged(): call(left_kernel, 4.0, (bf16(rows, cols, width), f32(tile, width), bf16(*...  4 us
    pallas_call x1, Pallas kernels, exchanged(): call(last_kernel, 0.1, f32(*one), [tile_spec] * 4, whole(one), (1,), wide...  3.13 us
    unnamed x20, local copies, waits for them, and re-layouts  2.34 us
    pallas_call x1, Pallas kernels, exchanged(): call(right_kernel, 2.2, jax.ShapeDtypeStruct((rows, cols, width), jnp.bfl...  2.22 us
  transfers between devices with their start and end apart: 12, of which 5 were waited for; matrix products, arithmetic and copies ran while one was open for 0% of the time, Pallas kernels for 26%

profile of v3, /device:TPU:25, one launch (start us, length us, event | category | flops | bytes accessed | tf_op | source)
XLA Modules:
  0.0 51.4 jit_solution(11254214600652055335)
XLA Ops:
  0.0 0.0 copy-start.7
  0.0 0.0 copy-start.8
  0.0 0.0 copy-start.2
  0.1 0.1 stack.27.flags_ref
  0.1 0.5 %copy-done.7 = s32[160]{0:T(256)S(1)} copy-done((s32[160]{0:T(256)S(1)}, s32[160]{0:T(256)}, u32[]{:S(2)}) %copy-start.7) | copy-done | bytes 664
  0.7 0.0 copy-done.8
  0.7 0.1 copy-done.1
  0.8 0.0 copy-done.2
  0.8 0.0 copy-start
  0.8 1.0 %copy-done = bf16[20,80,128]{2,1,0:T(8,128)(2,1)S(1)} copy-done((bf16[20,80,128]{2,1,0:T(8,128)(2,1)S(1)}, bf16[20,80,128]{2,1,0:T(8,128)(2,1)}, u32[]{:S(2)}) %copy-start) | copy-done | bytes 409624
  1.8 0.0 copy-start.3
  1.8 0.0 copy-start.4
  1.8 0.0 copy-start.5
  1.8 2.2 %shard_map.100.mine_ref = bf16[20,80,128]{2,1,0:T(8,128)(2,1)S(1)} custom-call(s32[5]{0:T(128)S(1)} %stack.27.flags_ref, bf16[20,80,128]{2,1,0:T(8,128)(2,1)S(1)} %copy-done, s32[1,160]{1,0:T(1,128)S(1)} %bitcast.9, f32[1,128]{1,0:T(1,128)S(1)} %bitcast.11, bf16[128,128]{1,0:T(8,128)(2,1)S(1)} %copy-done.1, bf16[128,128]{1,0:T(8,128)(2,1)S(1)} %copy-done.2), custom_call_target="tpu_custom_call" | custom-call | flops 2420000000 | bytes 6600000 | tf_op jit(solution)/shard_map/pallas_call | solution.py:402
  4.0 0.7 %collective-permute-start = (bf16[20,80,128]{2,1,0:T(8,128)(2,1)S(1)}, bf16[20,80,128]{2,1,0:T(8,128)(2,1)S(1)}, u32[]{:S(2)}, u32[]{:S(2)}) collective-permute-start(bf16[20,80,128]{2,1,0:T(8,128)(2,1)S(1)} %shard_map.100.mine_ref), channel_id=1, source_target_pairs={{0,2},{1,3},{2,0},{3,1},{4,6},{5,7},{6,4},{7,5},{8,10},{9,11},{10,... | collective-permute-start | bytes 1228808 | tf_op jit(solution)/shard_map/ppermute | solution.py:395
  4.8 0.1 collective-permute-start.2
  4.9 0.1 collective-permute-start.5
  5.0 1.2 %collective-permute-done.other_ref = bf16[20,80,128]{2,1,0:T(8,128)(2,1)S(1)} collective-permute-done((bf16[20,80,128]{2,1,0:T(8,128)(2,1)S(1)}, bf16[20,80,128]{2,1,0:T(8,128)(2,1)S(1)}, u32[]{:S(2)}, u32[]{:S(2)}) %collective-permute-start) | collective-permute-done | bytes 409632 | tf_op jit(solution)/shard_map/ppermute | solution.py:395
  6.2 0.0 copy-done.3
  6.2 0.0 copy-done.4
  6.2 0.0 copy-done.5
  6.2 4.0 %shard_map.101 = (bf16[20,80,128]{2,1,0:T(8,128)(2,1)S(1)}, f32[1600,128]{1,0:T(8,128)S(1)}, bf16[20,40,128]{2,1,0:T(8,128)(2,1)S(1)}, bf16[20,80,128]{2,1,0:T(8,128)(2,1)S(1)}) custom-call(s32[5]{0:T(128)S(1)} %stack.27.flags_ref, bf16[20,80,128]{2,1,0:T(8,128)(2,1)S(1)} %copy-done, s32[1,160]{1,0:T(1,128)S(1)} %bitcast.10, f32[1,128]{1,0:T(1,128)S(1)} %bitcast.12, ...), custom_call_target="tpu_custom_call" | custom-call | flops 4400000000 | bytes 12000000 | tf_op jit(solution)/shard_map/pallas_call | solution.py:426
  10.2 1.2 %collective-permute-start.1 = (bf16[20,80,128]{2,1,0:T(8,128)(2,1)S(1)}, bf16[20,80,128]{2,1,0:T(8,128)(2,1)S(1)}, u32[]{:S(2)}, u32[]{:S(2)}) collective-permute-start(bf16[20,80,128]{2,1,0:T(8,128)(2,1)S(1)} %get-tuple-element.21), channel_id=1, source_target_pairs={{0,1},{1,0},{2,3},{3,2},{4,5},{5,4},{6,7},{7,6},{8,9},{9,8},{10,11... | collective-permute-start | bytes 1228808 | tf_op jit(solution)/shard_map/ppermute | solution.py:395
  11.4 0.7 %collective-permute-start.4 = (bf16[20,80,128]{2,1,0:T(8,128)(2,1)S(1)}, bf16[20,80,128]{2,1,0:T(8,128)(2,1)S(1)}, u32[]{:S(2)}, u32[]{:S(2)}) collective-permute-start(bf16[20,80,128]{2,1,0:T(8,128)(2,1)S(1)} %get-tuple-element.20.left_ref), channel_id=1, source_target_pairs={{0,2},{1,3},{2,0},{3,1},{4,6},{5,7},{6,4},{7,5},{8,10},{9,11},{10,... | collective-permute-start | bytes 1228808 | tf_op jit(solution)/shard_map/ppermute | solution.py:395
  12.0 13.8 %collective-permute-done.2.pair_ref = bf16[20,80,128]{2,1,0:T(8,128)(2,1)S(1)} collective-permute-done((bf16[20,80,128]{2,1,0:T(8,128)(2,1)S(1)}, bf16[20,80,128]{2,1,0:T(8,128)(2,1)S(1)}, u32[]{:S(2)}, u32[]{:S(2)}) %collective-permute-start.2) | collective-permute-done | bytes 409632 | tf_op jit(solution)/shard_map/ppermute | solution.py:395
  25.8 1.3 %collective-permute-start.10 = (bf16[20,80,128]{2,1,0:T(8,128)(2,1)S(1)}, bf16[20,80,128]{2,1,0:T(8,128)(2,1)S(1)}, u32[]{:S(2)}, u32[]{:S(2)}) collective-permute-start(bf16[20,80,128]{2,1,0:T(8,128)(2,1)S(1)} %collective-permute-done.2.pair_ref), channel_id=1, source_target_pairs={{0,5},{2,7},{4,1},{6,3},{9,12},{11,14},{13,8},{15,10},{16,21},{18,... | collective-permute-start | bytes 1228808 | tf_op jit(solution)/shard_map/ppermute | solution.py:395
  27.1 1.9 %collective-permute-start.3 = (bf16[20,80,128]{2,1,0:T(8,128)(2,1)S(1)}, bf16[20,80,128]{2,1,0:T(8,128)(2,1)S(1)}, u32[]{:S(2)}, u32[]{:S(2)}) collective-permute-start(bf16[20,80,128]{2,1,0:T(8,128)(2,1)S(1)} %collective-permute-done.2.pair_ref), channel_id=1, source_target_pairs={{1,5},{3,7},{5,1},{7,3},{8,12},{10,14},{12,8},{14,10},{17,21},{19,... | collective-permute-start | bytes 1228808 | tf_op jit(solution)/shard_map/ppermute | solution.py:395
  29.0 0.0 collective-permute-done.5.next_ref
  29.0 0.0 collective-permute-done.1.given_ref
  29.0 0.0 collective-permute-done.4.left_other
  29.0 5.1 %shard_map.102 = (bf16[20,20,128]{2,1,0:T(8,128)(2,1)S(1)}, bf16[20,20,128]{2,1,0:T(8,128)(2,1)S(1)}, bf16[20,20,128]{2,1,0:T(8,128)(2,1)S(1)}, bf16[20,20,128]{2,1,0:T(8,128)(2,1)S(1)}) custom-call(s32[5]{0:T(128)S(1)} %stack.27.flags_ref, bf16[20,80,128]{2,1,0:T(8,128)(2,1)S(1)} %get-tuple-element.20.left_ref, ...), custom_call_target="tpu_custom_call" | custom-call | flops 6270000128 | bytes 17100000 | tf_op jit(solution)/shard_map/pallas_call | solution.py:441
  34.2 0.0 collective-permute-start.7
  34.2 0.7 %collective-permute-start.8 = (bf16[20,20,128]{2,1,0:T(8,128)(2,1)S(1)}, bf16[20,20,128]{2,1,0:T(8,128)(2,1)S(1)}, u32[]{:S(2)}, u32[]{:S(2)}) collective-permute-start(bf16[20,20,128]{2,1,0:T(8,128)(2,1)S(1)} %get-tuple-element.28), channel_id=1, source_target_pairs={{0,2},{1,3},{2,0},{3,1},{4,6},{5,7},{6,4},{7,5},{8,10},{9,11},{10,... | collective-permute-start | bytes 307208 | tf_op jit(solution)/shard_map/ppermute | solution.py:395
  34.9 1.4 %collective-permute-start.9 = (bf16[20,20,128]{2,1,0:T(8,128)(2,1)S(1)}, bf16[20,20,128]{2,1,0:T(8,128)(2,1)S(1)}, u32[]{:S(2)}, u32[]{:S(2)}) collective-permute-start(bf16[20,20,128]{2,1,0:T(8,128)(2,1)S(1)} %get-tuple-element.29), channel_id=1, source_target_pairs={{0,3},{1,2},{2,1},{3,0},{4,7},{5,6},{6,5},{7,4},{8,11},{9,10},{10,... | collective-permute-start | bytes 307208 | tf_op jit(solution)/shard_map/ppermute | solution.py:395
  36.3 2.9 %collective-permute-done.10.across_ref = bf16[20,80,128]{2,1,0:T(8,128)(2,1)S(1)} collective-permute-done((bf16[20,80,128]{2,1,0:T(8,128)(2,1)S(1)}, bf16[20,80,128]{2,1,0:T(8,128)(2,1)S(1)}, u32[]{:S(2)}, u32[]{:S(2)}) %collective-permute-start.10) | collective-permute-done | bytes 409632 | tf_op jit(solution)/shard_map/ppermute | solution.py:395
  39.2 0.4 collective-permute-done.3.straight_ref
  39.6 1.3 %collective-permute-start.11 = (bf16[20,80,128]{2,1,0:T(8,128)(2,1)S(1)}, bf16[20,80,128]{2,1,0:T(8,128)(2,1)S(1)}, u32[]{:S(2)}, u32[]{:S(2)}) collective-permute-start(bf16[20,80,128]{2,1,0:T(8,128)(2,1)S(1)} %collective-permute-done.10.across_ref), channel_id=1, source_target_pairs={{0,2},{1,3},{2,0},{3,1},{4,6},{5,7},{6,4},{7,5},{8,10},{9,11},{10,... | collective-permute-start | bytes 1228808 | tf_op jit(solution)/shard_map/ppermute | solution.py:395
  40.9 0.0 collective-permute-start.6
  40.9 3.1 %shard_map.104.mine_ref = f32[20,20,128]{2,1,0:T(8,128)S(1)} custom-call(s32[5]{0:T(128)S(1)} %stack.27.flags_ref, bf16[20,80,128]{2,1,0:T(8,128)(2,1)S(1)} %get-tuple-element.20.left_ref, bf16[20,80,128]{2,1,0:T(8,128)(2,1)S(1)} %collective-permute-done.1.given_ref, bf16[20,80,128]{2,1,0:T(8,128)(2,1)S(1)} %collective-permute-done.3.straight_ref, ...), custom_call_target="tpu_custom_call" | custom-call | flops 110000000 | bytes 300000 | tf_op jit(solution)/shard_map/pallas_call | solution.py:456
  44.0 0.0 collective-permute-done.7.own_given
  44.0 0.0 collective-permute-done.8.partner_ref
  44.0 1.2 %collective-permute-done.9.partner_given = bf16[20,20,128]{2,1,0:T(8,128)(2,1)S(1)} collective-permute-done((bf16[20,20,128]{2,1,0:T(8,128)(2,1)S(1)}, bf16[20,20,128]{2,1,0:T(8,128)(2,1)S(1)}, u32[]{:S(2)}, u32[]{:S(2)}) %collective-permute-start.9) | collective-permute-done | bytes 102432 | tf_op jit(solution)/shard_map/ppermute | solution.py:395
  45.2 0.0 copy-done.6
  45.2 0.7 %copy-done.9 = f32[128]{0:T(128)S(1)} copy-done((f32[128]{0:T(128)S(1)}, f32[128]{0:T(128)}, u32[]{:S(2)}) %copy-start.9) | copy-done | bytes 536
  45.9 1.0 %shard_map.103.done_ref = bf16[20,40,128]{2,1,0:T(8,128)(2,1)S(1)} custom-call(s32[5]{0:T(128)S(1)} %stack.27.flags_ref, bf16[20,20,128]{2,1,0:T(8,128)(2,1)S(1)} %get-tuple-element.25.own_ref, bf16[20,20,128]{2,1,0:T(8,128)(2,1)S(1)} %collective-permute-done.7.own_given, bf16[20,20,128]{2,1,0:T(8,128)(2,1)S(1)} %collective-permute-done.8.partner_ref, ...), custom_call_target="tpu_custom_call" | custom-call | flops 8800000000 | bytes 24000000 | tf_op jit(solution)/shard_map/pallas_call | solution.py:460
  46.9 0.0 collective-permute-done.11.across_ref
  46.9 0.0 collective-permute-done.6.straight_ref
  46.9 4.5 %shard_map.105 = bf16[20,80,128]{2,1,0:T(8,128)(2,1)} custom-call(s32[5]{0:T(128)S(1)} %stack.27.flags_ref, bf16[20,80,128]{2,1,0:T(8,128)(2,1)S(1)} %get-tuple-element.20.left_ref, bf16[20,80,128]{2,1,0:T(8,128)(2,1)S(1)} %collective-permute-done.1.given_ref, bf16[20,80,128]{2,1,0:T(8,128)(2,1)S(1)} %collective-permute-done.6.straight_ref, ...), custom_call_target="tpu_custom_call" | custom-call | flops 4400000000 | bytes 12000000 | tf_op jit(solution)/shard_map/pallas_call | solution.py:469
  (3 shorter events, 0.0 us)
Async XLA Ops:
  0.0 0.7 %copy-start.7 = (s32[160]{0:T(256)S(1)}, s32[160]{0:T(256)}, u32[]{:S(2)}) copy-start(s32[160]{0:T(256)} %param.11) | copy-start | bytes 1924
  0.0 0.7 %copy-start.8 = (f32[128]{0:T(128)S(1)}, f32[128]{0:T(128)}, u32[]{:S(2)}) copy-start(f32[128]{0:T(128)} %param.12) | copy-start | bytes 1540
  0.0 0.8 %copy-start.1 = (bf16[128,128]{1,0:T(8,128)(2,1)S(1)}, bf16[128,128]{1,0:T(8,128)(2,1)}, u32[]{:S(2)}) copy-start(bf16[128,128]{1,0:T(8,128)(2,1)} %proj_ref.4) | copy-start | bytes 98308
  0.0 0.8 %copy-start.2 = (bf16[128,128]{1,0:T(8,128)(2,1)S(1)}, bf16[128,128]{1,0:T(8,128)(2,1)}, u32[]{:S(2)}) copy-start(bf16[128,128]{1,0:T(8,128)(2,1)} %gate_ref.2) | copy-start | bytes 98308
  0.8 1.0 %copy-start = (bf16[20,80,128]{2,1,0:T(8,128)(2,1)S(1)}, bf16[20,80,128]{2,1,0:T(8,128)(2,1)}, u32[]{:S(2)}) copy-start(bf16[20,80,128]{2,1,0:T(8,128)(2,1)} %pair_ref.3) | copy-start | bytes 1228804
  1.8 4.3 %copy-start.3 = (bf16[128,128]{1,0:T(8,128)(2,1)S(1)}, bf16[128,128]{1,0:T(8,128)(2,1)}, u32[]{:S(2)}) copy-start(bf16[128,128]{1,0:T(8,128)(2,1)} %proj_ref.5) | copy-start | bytes 98308
  1.8 4.4 %copy-start.4 = (bf16[128,128]{1,0:T(8,128)(2,1)S(1)}, bf16[128,128]{1,0:T(8,128)(2,1)}, u32[]{:S(2)}) copy-start(bf16[128,128]{1,0:T(8,128)(2,1)} %gate_ref.3) | copy-start | bytes 98308
  1.8 4.4 %copy-start.5 = (bf16[128,128]{1,0:T(8,128)(2,1)S(1)}, bf16[128,128]{1,0:T(8,128)(2,1)}, u32[]{:S(2)}) copy-start(bf16[128,128]{1,0:T(8,128)(2,1)} %out_gate_ref.1) | copy-start | bytes 98308
  4.0 2.1 %collective-permute-start = (bf16[20,80,128]{2,1,0:T(8,128)(2,1)S(1)}, bf16[20,80,128]{2,1,0:T(8,128)(2,1)S(1)}, u32[]{:S(2)}, u32[]{:S(2)}) collective-permute-start(bf16[20,80,128]{2,1,0:T(8,128)(2,1)S(1)} %shard_map.100.mine_ref), channel_id=1, source_target_pairs={{0,2},{1,3},{2,0},{3,1},{4,6},{5,7},{6,4},{7,5},{8,10},{9,11},{10,... | collective-permute-start | bytes 1228808 | tf_op jit(solution)/shard_map/ppermute | solution.py:395
  4.8 21.0 %collective-permute-start.2 = (bf16[20,80,128]{2,1,0:T(8,128)(2,1)S(1)}, bf16[20,80,128]{2,1,0:T(8,128)(2,1)S(1)}, u32[]{:S(2)}, u32[]{:S(2)}) collective-permute-start(bf16[20,80,128]{2,1,0:T(8,128)(2,1)S(1)} %shard_map.100.mine_ref), channel_id=1, source_target_pairs={{0,8},{1,9},{2,10},{3,11},{4,12},{5,13},{6,14},{7,15},{8,0},{9,1},... | collective-permute-start | bytes 1228808 | tf_op jit(solution)/shard_map/ppermute | solution.py:395
  4.9 24.2 %collective-permute-start.5 = (bf16[20,80,128]{2,1,0:T(8,128)(2,1)S(1)}, bf16[20,80,128]{2,1,0:T(8,128)(2,1)S(1)}, u32[]{:S(2)}, u32[]{:S(2)}) collective-permute-start(bf16[20,80,128]{2,1,0:T(8,128)(2,1)S(1)} %shard_map.100.mine_ref), channel_id=1, source_target_pairs={{0,4},{1,5},{2,6},{3,7},{4,0},{5,1},{6,2},{7,3},{8,12},{9,13},{10,... | collective-permute-start | bytes 1228808 | tf_op jit(solution)/shard_map/ppermute | solution.py:395
  10.2 18.9 %collective-permute-start.1 = (bf16[20,80,128]{2,1,0:T(8,128)(2,1)S(1)}, bf16[20,80,128]{2,1,0:T(8,128)(2,1)S(1)}, u32[]{:S(2)}, u32[]{:S(2)}) collective-permute-start(bf16[20,80,128]{2,1,0:T(8,128)(2,1)S(1)} %get-tuple-element.21), channel_id=1, source_target_pairs={{0,1},{1,0},{2,3},{3,2},{4,5},{5,4},{6,7},{7,6},{8,9},{9,8},{10,11... | collective-permute-start | bytes 1228808 | tf_op jit(solution)/shard_map/ppermute | solution.py:395
  11.4 17.7 %collective-permute-start.4 = (bf16[20,80,128]{2,1,0:T(8,128)(2,1)S(1)}, bf16[20,80,128]{2,1,0:T(8,128)(2,1)S(1)}, u32[]{:S(2)}, u32[]{:S(2)}) collective-permute-start(bf16[20,80,128]{2,1,0:T(8,128)(2,1)S(1)} %get-tuple-element.20.left_ref), channel_id=1, source_target_pairs={{0,2},{1,3},{2,0},{3,1},{4,6},{5,7},{6,4},{7,5},{8,10},{9,11},{10,... | collective-permute-start | bytes 1228808 | tf_op jit(solution)/shard_map/ppermute | solution.py:395
  25.8 13.4 %collective-permute-start.10 = (bf16[20,80,128]{2,1,0:T(8,128)(2,1)S(1)}, bf16[20,80,128]{2,1,0:T(8,128)(2,1)S(1)}, u32[]{:S(2)}, u32[]{:S(2)}) collective-permute-start(bf16[20,80,128]{2,1,0:T(8,128)(2,1)S(1)} %collective-permute-done.2.pair_ref), channel_id=1, source_target_pairs={{0,5},{2,7},{4,1},{6,3},{9,12},{11,14},{13,8},{15,10},{16,21},{18,... | collective-permute-start | bytes 1228808 | tf_op jit(solution)/shard_map/ppermute | solution.py:395
  27.1 12.5 %collective-permute-start.3 = (bf16[20,80,128]{2,1,0:T(8,128)(2,1)S(1)}, bf16[20,80,128]{2,1,0:T(8,128)(2,1)S(1)}, u32[]{:S(2)}, u32[]{:S(2)}) collective-permute-start(bf16[20,80,128]{2,1,0:T(8,128)(2,1)S(1)} %collective-permute-done.2.pair_ref), channel_id=1, source_target_pairs={{1,5},{3,7},{5,1},{7,3},{8,12},{10,14},{12,8},{14,10},{17,21},{19,... | collective-permute-start | bytes 1228808 | tf_op jit(solution)/shard_map/ppermute | solution.py:395
  34.2 9.8 %collective-permute-start.7 = (bf16[20,20,128]{2,1,0:T(8,128)(2,1)S(1)}, bf16[20,20,128]{2,1,0:T(8,128)(2,1)S(1)}, u32[]{:S(2)}, u32[]{:S(2)}) collective-permute-start(bf16[20,20,128]{2,1,0:T(8,128)(2,1)S(1)} %get-tuple-element.27), channel_id=1, source_target_pairs={{0,1},{1,0},{2,3},{3,2},{4,5},{5,4},{6,7},{7,6},{8,9},{9,8},{10,11... | collective-permute-start | bytes 307208 | tf_op jit(solution)/shard_map/ppermute | solution.py:395
  34.2 9.8 %collective-permute-start.8 = (bf16[20,20,128]{2,1,0:T(8,128)(2,1)S(1)}, bf16[20,20,128]{2,1,0:T(8,128)(2,1)S(1)}, u32[]{:S(2)}, u32[]{:S(2)}) collective-permute-start(bf16[20,20,128]{2,1,0:T(8,128)(2,1)S(1)} %get-tuple-element.28), channel_id=1, source_target_pairs={{0,2},{1,3},{2,0},{3,1},{4,6},{5,7},{6,4},{7,5},{8,10},{9,11},{10,... | collective-permute-start | bytes 307208 | tf_op jit(solution)/shard_map/ppermute | solution.py:395
  34.9 10.3 %collective-permute-start.9 = (bf16[20,20,128]{2,1,0:T(8,128)(2,1)S(1)}, bf16[20,20,128]{2,1,0:T(8,128)(2,1)S(1)}, u32[]{:S(2)}, u32[]{:S(2)}) collective-permute-start(bf16[20,20,128]{2,1,0:T(8,128)(2,1)S(1)} %get-tuple-element.29), channel_id=1, source_target_pairs={{0,3},{1,2},{2,1},{3,0},{4,7},{5,6},{6,5},{7,4},{8,11},{9,10},{10,... | collective-permute-start | bytes 307208 | tf_op jit(solution)/shard_map/ppermute | solution.py:395
  39.2 6.0 %copy-start.6 = (bf16[128,128]{1,0:T(8,128)(2,1)S(1)}, bf16[128,128]{1,0:T(8,128)(2,1)}, u32[]{:S(2)}) copy-start(bf16[128,128]{1,0:T(8,128)(2,1)} %proj_ref.7) | copy-start | bytes 98308
  39.6 7.3 %collective-permute-start.11 = (bf16[20,80,128]{2,1,0:T(8,128)(2,1)S(1)}, bf16[20,80,128]{2,1,0:T(8,128)(2,1)S(1)}, u32[]{:S(2)}, u32[]{:S(2)}) collective-permute-start(bf16[20,80,128]{2,1,0:T(8,128)(2,1)S(1)} %collective-permute-done.10.across_ref), channel_id=1, source_target_pairs={{0,2},{1,3},{2,0},{3,1},{4,6},{5,7},{6,4},{7,5},{8,10},{9,11},{10,... | collective-permute-start | bytes 1228808 | tf_op jit(solution)/shard_map/ppermute | solution.py:395
  40.9 6.0 %collective-permute-start.6 = (bf16[20,80,128]{2,1,0:T(8,128)(2,1)S(1)}, bf16[20,80,128]{2,1,0:T(8,128)(2,1)S(1)}, u32[]{:S(2)}, u32[]{:S(2)}) collective-permute-start(bf16[20,80,128]{2,1,0:T(8,128)(2,1)S(1)} %collective-permute-done.3.straight_ref), channel_id=1, source_target_pairs={{0,2},{1,3},{2,0},{3,1},{4,6},{5,7},{6,4},{7,5},{8,10},{9,11},{10,... | collective-permute-start | bytes 1228808 | tf_op jit(solution)/shard_map/ppermute | solution.py:395
  45.2 0.7 %copy-start.9 = (f32[128]{0:T(128)S(1)}, f32[128]{0:T(128)}, u32[]{:S(2)}) copy-start(f32[128]{0:T(128)} %param.17) | copy-start | bytes 1540

commit v4 on v3

--- a/solution.py
+++ b/solution.py
@@ -9,7 +9,7 @@
 
 LINE = ("row", "col")
 VMEM_LIMIT = 48 * 1024 * 1024
-VECTOR_ROWS = 8
+VECTOR_ROWS = 16
 PAIR = 2
 UNROLL = 10
 
@@ -100,10 +100,6 @@
     return finish_output(normed_hidden, own_pair, out_proj, out_gate)
 
 
-def whole(shape):
-    return pl.BlockSpec(shape, lambda *_: (0,) * len(shape))
-
-
 def normed_rows(pair_ref, gain_ref):
     rows, cols, width = pair_ref.shape
     values = pair_ref[...].astype(jnp.float32).reshape(rows * cols, width)
@@ -111,7 +107,7 @@
 
 
 def mask_block(mask_ref, flags_ref, rows, cols, width):
-    first = flags_ref[0] * (rows * pl.num_programs(0)) + pl.program_id(0) * rows
+    first = flags_ref[0] * rows
     col_mask = jnp.zeros((1, cols), jnp.int32)
     for block in range(mask_ref.shape[1] // cols):
         part = mask_ref[:, block * cols : (block + 1) * cols]
@@ -145,11 +141,12 @@
     out_gate_ref,
     mine_ref,
     other_ref,
+    hidden_gain_ref,
     left_ref,
     gating_ref,
     sum_ref,
     swap_ref,
-    left_wide,
+    held_gain_ref,
     right_wide,
 ):
     rows, cols, width = pair_ref.shape
@@ -162,7 +159,8 @@
     gating_ref[...] = jax.nn.sigmoid(
         jnp.dot(normed, out_gate_ref[...], preferred_element_type=jnp.float32)
     )
-    triangle([left_ref], [[mine_ref], [other_ref]], sum_ref, left_wide, right_wide)
+    triangle(left_ref, [mine_ref, other_ref], sum_ref, right_wide)
+    held_gain_ref[...] = hidden_gain_ref[...]
     keeps_near = flags_ref[3] == 1
 
     @pl.when(keeps_near)
@@ -181,61 +179,57 @@
     return jnp.where((col >= row) & (col < row + length), 1.0, 0.0).astype(jnp.bfloat16)
 
 
-def triangle(lefts, tiles, sum_ref, left_wide, right_wide):
-    rows, cols, width = lefts[0].shape
-    size = rows * cols
+def triangle(left_ref, tiles, sum_ref, right_wide, more=False):
+    rows, cols, width = left_ref.shape
     few = VECTOR_ROWS
     many = rows - few
-    for b, left_ref in enumerate(lefts):
-        left_wide[b * size : (b + 1) * size, :] = (
-            left_ref[...].astype(jnp.float32).reshape(size, width)
-        )
-    held = few * cols
-    blocks = [block for tile in tiles for block in tile]
-    for n, block in enumerate(blocks):
-        right_wide[n * held : (n + 1) * held, :] = (
-            block[:few].astype(jnp.float32).reshape(held, width)
+    for t, tile in enumerate(tiles):
+        right_wide[t * few : (t + 1) * few] = (
+            tile[:few].astype(jnp.float32).reshape(few, cols // 8, 8, width)
         )
     sum_many, sum_few = run_sums(many, cols), run_sums(few, 8)
 
     def of_rows(step, _):
         lines = [step * PAIR + n for n in range(PAIR)]
-        narrow = [[left_ref[line] for line in lines] for left_ref in lefts]
-        wide = [
-            [
-                left_wide[pl.ds(pl.multiple_of(b * size + line * cols, 8), cols), :].reshape(
-                    cols // 8, 8, width
-                )
-                for line in lines
-            ]
-            for b in range(len(lefts))
-        ]
+        narrow = [left_ref[line] for line in lines]
+        wide = [left.astype(jnp.float32).reshape(cols // 8, 8, width) for left in narrow]
         for t, tile in enumerate(tiles):
-            last, partial = 0.0, [0.0] * PAIR
-            for b, block in enumerate(tile):
-                right = block[few:]
-                products = jnp.concatenate(
-                    [(right * left[None]).reshape(many * cols, width) for left in narrow[b]], axis=1
-                )
-                last = last + jnp.dot(sum_many, products, preferred_element_type=jnp.float32)
-                n = t * len(tile) + b
-                right = right_wide[n * held : (n + 1) * held, :]
-                right = right.reshape(few, cols // 8, 8, width)
-                partial = [
-                    total + jnp.sum(right * left[None], axis=1).reshape(few * 8, width)
-                    for total, left in zip(partial, wide[b])
-                ]
+            products = jnp.concatenate(
+                [(tile[few:] * left[None]).reshape(many * cols, width) for left in narrow], axis=1
+            )
+            last = jnp.dot(sum_many, products, preferred_element_type=jnp.float32)
+            partial = [0.0] * PAIR
+            for k in range(cols // 8):
+                right = right_wide[t * few : (t + 1) * few, k]
+                partial = [total + right * left[k] for total, left in zip(partial, wide)]
+            partial = [total.reshape(few * 8, width) for total in partial]
             first = jnp.dot(
                 sum_few,
                 jnp.concatenate(partial, axis=1).astype(jnp.bfloat16),
                 preferred_element_type=jnp.float32,
             )
-            sums = jnp.concatenate([first, last], axis=0).astype(sum_ref.dtype)
+            sums = jnp.concatenate([first, last], axis=0)
             for n, line in enumerate(lines):
-                sum_ref[line, t * rows : (t + 1) * rows, :] = sums[:, n * width : (n + 1) * width]
+                place = (line, slice(t * rows, (t + 1) * rows))
+                total = sums[:, n * width : (n + 1) * width]
+                if more:
+                    total = total + sum_ref[place]
+                sum_ref[place] = total.astype(sum_ref.dtype)
         return 0
 
     lax.fori_loop(0, rows // PAIR, of_rows, 0, unroll=UNROLL)
+
+
+def paired(sums):
+    rows, cols, width = sums.shape
+    pairs = sums.reshape(rows // 2, 2, cols, width)
+    return jnp.concatenate([pairs[:, 0], pairs[:, 1]], axis=1)
+
+
+def unpaired(pairs):
+    half, double, width = pairs.shape
+    cols = double // 2
+    return jnp.stack([pairs[:, :cols], pairs[:, cols:]], axis=1).reshape(2 * half, cols, width)
 
 
 def middle_kernel(
@@ -249,26 +243,24 @@
     sent_own,
     sent_other,
     both,
-    left_wide,
     right_wide,
 ):
     rows = left_ref.shape[0]
     keeps_near = flags_ref[3] == 1
     for left, kept, sent in ((left_ref, kept_own, sent_own), (left_other, kept_other, sent_other)):
-        triangle([left], [[next_ref], [pair_ref]], both, left_wide, right_wide)
+        triangle(left, [next_ref, pair_ref], both, right_wide)
         of_next, of_pair = both[:, :rows], both[:, rows:]
-        kept[...] = jnp.where(keeps_near, of_next, of_pair).astype(jnp.bfloat16)
-        sent[...] = jnp.where(keeps_near, of_pair, of_next).astype(jnp.bfloat16)
+        kept[...] = paired(jnp.where(keeps_near, of_next, of_pair)).astype(jnp.bfloat16)
+        sent[...] = paired(jnp.where(keeps_near, of_pair, of_next)).astype(jnp.bfloat16)
 
 
 def last_kernel(
-    flags_ref, left_ref, given_ref, straight_ref, across_ref, sum_ref, left_wide, right_wide
+    flags_ref, left_ref, given_ref, straight_ref, across_ref, sum_ref, right_wide
 ):
     @pl.when(flags_ref[3] == 0)
     def _():
-        triangle(
-            [left_ref, given_ref], [[straight_ref, across_ref]], sum_ref, left_wide, right_wide
-        )
+        triangle(left_ref, [straight_ref], sum_ref, right_wide)
+        triangle(given_ref, [across_ref], sum_ref, right_wide, more=True)
 
 
 def finished(flags_ref, own, partner, at, gain_ref, proj_ref, gating_ref):
@@ -295,7 +287,7 @@
     out_ref,
 ):
     keeps_near, odd = flags_ref[3], flags_ref[4]
-    total = lambda a, b: a[...].astype(jnp.float32) + b[...].astype(jnp.float32)
+    total = lambda a, b: unpaired(a[...].astype(jnp.float32) + b[...].astype(jnp.float32))
     at = jnp.where(keeps_near == 1, 1 - odd, odd)
     out_ref[...] = finished(
         flags_ref,
@@ -322,11 +314,10 @@
     gating_ref,
     out_ref,
     other_ref,
-    left_wide,
     right_wide,
 ):
     last_kernel(
-        flags_ref, left_ref, given_ref, straight_ref, across_ref, other_ref, left_wide, right_wide
+        flags_ref, left_ref, given_ref, straight_ref, across_ref, other_ref, right_wide
     )
     rows = out_ref.shape[0]
     keeps_near, odd = flags_ref[3] == 1, flags_ref[4]
@@ -341,22 +332,23 @@
     ).astype(jnp.bfloat16)
 
 
-def call(kernel, micros, out_shape, in_specs, out_specs, grid, scratch=()):
-    return pl.pallas_call(
-        kernel,
-        out_shape=out_shape,
-        grid_spec=pltpu.PrefetchScalarGridSpec(
-            num_scalar_prefetch=1,
-            grid=grid,
-            in_specs=in_specs,
-            out_specs=out_specs,
+def call(kernel, micros, out_shape, scratch=()):
+    vmem = pl.BlockSpec(memory_space=pltpu.VMEM)
+
+    def run(flags, *arrays):
+        return pl.pallas_call(
+            kernel,
+            out_shape=out_shape,
+            in_specs=[pl.BlockSpec(memory_space=pltpu.SMEM)] + [vmem] * len(arrays),
+            out_specs=jax.tree.map(lambda _: vmem, out_shape),
             scratch_shapes=list(scratch),
-        ),
-        compiler_params=pltpu.CompilerParams(vmem_limit_bytes=VMEM_LIMIT),
-        cost_estimate=pl.CostEstimate(
-            flops=int(micros * 1.1e9), bytes_accessed=int(micros * 3e6), transcendentals=0
-        ),
-    )
+            compiler_params=pltpu.CompilerParams(vmem_limit_bytes=VMEM_LIMIT),
+            cost_estimate=pl.CostEstimate(
+                flops=int(micros * 1.1e9), bytes_accessed=int(micros * 3e6), transcendentals=0
+            ),
+        )(flags, *arrays)
+
+    return run
 
 
 def exchanged(
@@ -394,44 +386,31 @@
     across = [(p, p ^ 5) for p in places if keeps_far(p ^ 5)]
     send = lambda value, pairs: lax.ppermute(value, LINE, pairs)
 
-    steps = 4
-    block = rows // steps
-    pair_spec = pl.BlockSpec((block, cols, width), lambda s, _: (s, 0, 0))
-    square = whole((width, width))
-    vector = whole((1, width))
-    right = call(
-        right_kernel,
-        2.2,
-        jax.ShapeDtypeStruct((rows, cols, width), jnp.bfloat16),
-        [pair_spec, whole(mask.shape), vector, square, square],
-        pair_spec,
-        (steps,),
-    )(flags, pair_rep, mask, ln_gain, right_proj, right_gate)
+    bf16 = lambda *shape: jax.ShapeDtypeStruct(shape, jnp.bfloat16)
+    f32 = lambda *shape: jax.ShapeDtypeStruct(shape, jnp.float32)
+    two, one = (rows, 2 * rows, width), (rows, rows, width)
+    wide = lambda tiles: [pltpu.VMEM((tiles * VECTOR_ROWS, cols // 8, 8, width), jnp.float32)]
+    right = call(right_kernel, 2.2, bf16(rows, cols, width))(
+        flags, pair_rep, mask, ln_gain, right_proj, right_gate
+    )
 
     from_pair = send(right, over_pair)
     from_next = send(right, over_next)
     from_core = send(right, over_core)
 
     after = lambda value, *last: lax.optimization_barrier((value, *last))[0]
-    bf16 = lambda *shape: jax.ShapeDtypeStruct(shape, jnp.bfloat16)
-    f32 = lambda *shape: jax.ShapeDtypeStruct(shape, jnp.float32)
-    tile_spec = whole((rows, cols, width))
-    flat_spec = whole((tile, width))
-    two, one = (rows, 2 * rows, width), (rows, rows, width)
-    held = VECTOR_ROWS * cols
-    wide = lambda lefts, blocks: [
-        pltpu.VMEM((lefts * tile, width), jnp.float32),
-        pltpu.VMEM((blocks * held, width), jnp.float32),
-    ]
-    left, gating, near, swap = call(
+    left, gating, near, swap, hidden_gain = call(
         left_kernel,
         4.0,
-        (bf16(rows, cols, width), f32(tile, width), bf16(*two), bf16(rows, cols, width)),
-        [tile_spec, whole(mask.shape), vector, square, square, square, tile_spec, tile_spec],
-        (tile_spec, flat_spec, whole(two), tile_spec),
-        (1,),
-        wide(1, 2),
-    )(flags, pair_rep, mask, ln_gain, left_proj, left_gate, out_gate, right, from_core)
+        (
+            bf16(rows, cols, width),
+            f32(tile, width),
+            bf16(*two),
+            bf16(rows, cols, width),
+            f32(1, width),
+        ),
+        wide(2),
+    )(flags, pair_rep, mask, ln_gain, left_proj, left_gate, out_gate, right, from_core, hidden_gain)
     given = send(swap, over_col)
     left_other = send(left, over_core)
 
@@ -441,11 +420,8 @@
     kept_own, kept_other, sent_own, sent_other = call(
         middle_kernel,
         5.7,
-        (bf16(*one),) * 4,
-        [tile_spec] * 4,
-        (whole(one),) * 4,
-        (1,),
-        [pltpu.VMEM(two, jnp.float32)] + wide(1, 2),
+        (bf16(rows // 2, 2 * rows, width),) * 4,
+        [pltpu.VMEM(two, jnp.float32)] + wide(2),
     )(flags, left, after(left_other, from_pair), from_next, from_pair)
     kept_given = send(sent_own, over_col)
     partner_given = send(sent_other, over_both)
@@ -454,26 +430,20 @@
     far_straight, far_across = after(far_straight, kept_own), after(far_across, kept_own)
     other_straight, other_across = send(far_straight, over_core), send(far_across, over_core)
     mine = call(
-        last_kernel, 0.1, f32(*one), [tile_spec] * 4, whole(one), (1,), wide(2, 2)
+        last_kernel, 0.1, f32(*one), wide(1)
     )(flags, left, given, far_straight, far_across)
     gating = gating.reshape(rows, cols, width)
     done = call(
         swapped_kernel,
         8.0,
         bf16(*two),
-        [whole(one)] * 4 + [vector, square, tile_spec],
-        whole(two),
-        (1,),
     )(flags, kept_own, kept_given, partner, partner_given, hidden_gain, out_proj, gating)
     other_straight, other_across = after(other_straight, done), after(other_across, done)
     return call(
         finish_kernel,
         4.0,
         bf16(rows, cols, width),
-        [tile_spec] * 4 + [whole(one), whole(two), whole(two), vector, square, tile_spec],
-        tile_spec,
-        (1,),
-        [pltpu.VMEM(one, jnp.float32)] + wide(2, 2),
+        [pltpu.VMEM(one, jnp.float32)] + wide(1),
     )(
         flags,
         left,

time: 51.7 us -> 48.9 us (0.946)
  Pallas kernels: 20 us -> 18.2 us
  local copies, waits for them, and re-layouts: 2.43 us -> 1.78 us
    pallas_call x6, Pallas kernels: 20 us -> 18.2 us  [run(): pl.pallas_call(kernel, out_shape=out_shape, in_specs=[pl.BlockSpec(memory...]
    unnamed x20, local copies, waits for them, and re-layouts: 2.34 us -> 1.7 us
where the time goes in v4:
time: 48.9 us; the launch traced here: 48.6 us
  waiting for transfers between devices  19.1 us (39%)
  Pallas kernels  18.2 us (37%)
  starting transfers between devices  9.44 us (19%)
  local copies, waits for them, and re-layouts  1.78 us (4%)
    ppermute x12, waiting for transfers between devices, exchanged(): send = lambda value, pairs: lax.ppermute(value, LINE, pairs)  19.1 us
    pallas_call x6, Pallas kernels, run(): pl.pallas_call(kernel, out_shape=out_shape, in_specs=[pl.BlockSpec(memory...  18.2 us
    ppermute x12, starting transfers between devices, exchanged(): send = lambda value, pairs: lax.ppermute(value, LINE, pairs)  9.44 us
    unnamed x20, local copies, waits for them, and re-layouts  1.7 us
  transfers between devices with their start and end apart: 12, of which 5 were waited for; matrix products, arithmetic and copies ran while one was open for 0% of the time, Pallas kernels for 26%

profile of v4, /device:TPU:25, one launch (start us, length us, event | category | flops | bytes accessed | tf_op | source)
XLA Modules:
  0.0 48.6 jit_solution(16856608161887637662)
XLA Ops:
  0.0 0.0 copy-start.7
  0.0 0.0 copy-start.1
  0.0 0.0 copy-start.2
  0.1 0.1 stack.27.flags_ref
  0.1 0.5 %copy-done.7 = s32[160]{0:T(256)S(1)} copy-done((s32[160]{0:T(256)S(1)}, s32[160]{0:T(256)}, u32[]{:S(2)}) %copy-start.7) | copy-done | bytes 664
  0.7 0.0 copy-done.8
  0.7 0.1 copy-done.1
  0.8 0.0 copy-done.2
  0.8 0.0 copy-start
  0.8 1.0 %copy-done = bf16[20,80,128]{2,1,0:T(8,128)(2,1)S(1)} copy-done((bf16[20,80,128]{2,1,0:T(8,128)(2,1)S(1)}, bf16[20,80,128]{2,1,0:T(8,128)(2,1)}, u32[]{:S(2)}) %copy-start) | copy-done | bytes 409624
  1.8 0.0 copy-start.3
  1.8 0.0 copy-start.4
  1.8 1.5 %shard_map.100.mine_ref = bf16[20,80,128]{2,1,0:T(8,128)(2,1)S(1)} custom-call(s32[5]{0:T(128)S(1)} %stack.27.flags_ref, bf16[20,80,128]{2,1,0:T(8,128)(2,1)S(1)} %copy-done, s32[1,160]{1,0:T(1,128)S(1)} %bitcast.9, f32[1,128]{1,0:T(1,128)S(1)} %bitcast.11, bf16[128,128]{1,0:T(8,128)(2,1)S(1)} %copy-done.1, bf16[128,128]{1,0:T(8,128)(2,1)S(1)} %copy-done.2), custom_call_target="tpu_custom_call" | custom-call | flops 2420000000 | bytes 6600000 | tf_op jit(solution)/shard_map/pallas_call | solution.py:339
  3.3 0.0 copy-start.9
  3.3 0.7 %collective-permute-start = (bf16[20,80,128]{2,1,0:T(8,128)(2,1)S(1)}, bf16[20,80,128]{2,1,0:T(8,128)(2,1)S(1)}, u32[]{:S(2)}, u32[]{:S(2)}) collective-permute-start(bf16[20,80,128]{2,1,0:T(8,128)(2,1)S(1)} %shard_map.100.mine_ref), channel_id=1, source_target_pairs={{0,2},{1,3},{2,0},{3,1},{4,6},{5,7},{6,4},{7,5},{8,10},{9,11},{10,... | collective-permute-start | bytes 1228808 | tf_op jit(solution)/shard_map/ppermute | solution.py:387
  4.0 0.1 collective-permute-start.2
  4.1 0.1 collective-permute-start.5
  4.2 1.2 %collective-permute-done.other_ref = bf16[20,80,128]{2,1,0:T(8,128)(2,1)S(1)} collective-permute-done((bf16[20,80,128]{2,1,0:T(8,128)(2,1)S(1)}, bf16[20,80,128]{2,1,0:T(8,128)(2,1)S(1)}, u32[]{:S(2)}, u32[]{:S(2)}) %collective-permute-start) | collective-permute-done | bytes 409632 | tf_op jit(solution)/shard_map/ppermute | solution.py:387
  5.4 0.0 copy-done.3
  5.4 0.0 copy-done.4
  5.4 0.0 copy-done.5
  5.4 0.0 copy-done.9
  5.4 3.7 %shard_map.101 = (bf16[20,80,128]{2,1,0:T(8,128)(2,1)S(1)}, f32[1600,128]{1,0:T(8,128)S(1)}, bf16[20,40,128]{2,1,0:T(8,128)(2,1)S(1)}, bf16[20,80,128]{2,1,0:T(8,128)(2,1)S(1)}, f32[1,128]{1,0:T(1,128)S(1)}) custom-call(s32[5]{0:T(128)S(1)} %stack.27.flags_ref, bf16[20,80,128]{2,1,0:T(8,128)(2,1)S(1)} %copy-done, s32[1,160]{1,0:T(1,128)S(1)} %bitcast.10, ...), custom_call_target="tpu_custom_call" | custom-call | flops 4400000000 | bytes 12000000 | tf_op jit(solution)/shard_map/pallas_call | solution.py:339
  9.2 1.2 %collective-permute-start.1 = (bf16[20,80,128]{2,1,0:T(8,128)(2,1)S(1)}, bf16[20,80,128]{2,1,0:T(8,128)(2,1)S(1)}, u32[]{:S(2)}, u32[]{:S(2)}) collective-permute-start(bf16[20,80,128]{2,1,0:T(8,128)(2,1)S(1)} %get-tuple-element.22), channel_id=1, source_target_pairs={{0,1},{1,0},{2,3},{3,2},{4,5},{5,4},{6,7},{7,6},{8,9},{9,8},{10,11... | collective-permute-start | bytes 1228808 | tf_op jit(solution)/shard_map/ppermute | solution.py:387
  10.4 0.7 %collective-permute-start.4 = (bf16[20,80,128]{2,1,0:T(8,128)(2,1)S(1)}, bf16[20,80,128]{2,1,0:T(8,128)(2,1)S(1)}, u32[]{:S(2)}, u32[]{:S(2)}) collective-permute-start(bf16[20,80,128]{2,1,0:T(8,128)(2,1)S(1)} %get-tuple-element.21.left_ref), channel_id=1, source_target_pairs={{0,2},{1,3},{2,0},{3,1},{4,6},{5,7},{6,4},{7,5},{8,10},{9,11},{10,... | collective-permute-start | bytes 1228808 | tf_op jit(solution)/shard_map/ppermute | solution.py:387
  11.1 14.0 %collective-permute-done.2.pair_ref = bf16[20,80,128]{2,1,0:T(8,128)(2,1)S(1)} collective-permute-done((bf16[20,80,128]{2,1,0:T(8,128)(2,1)S(1)}, bf16[20,80,128]{2,1,0:T(8,128)(2,1)S(1)}, u32[]{:S(2)}, u32[]{:S(2)}) %collective-permute-start.2) | collective-permute-done | bytes 409632 | tf_op jit(solution)/shard_map/ppermute | solution.py:387
  25.0 1.3 %collective-permute-start.10 = (bf16[20,80,128]{2,1,0:T(8,128)(2,1)S(1)}, bf16[20,80,128]{2,1,0:T(8,128)(2,1)S(1)}, u32[]{:S(2)}, u32[]{:S(2)}) collective-permute-start(bf16[20,80,128]{2,1,0:T(8,128)(2,1)S(1)} %collective-permute-done.2.pair_ref), channel_id=1, source_target_pairs={{0,5},{2,7},{4,1},{6,3},{9,12},{11,14},{13,8},{15,10},{16,21},{18,... | collective-permute-start | bytes 1228808 | tf_op jit(solution)/shard_map/ppermute | solution.py:387
  26.3 1.9 %collective-permute-start.3 = (bf16[20,80,128]{2,1,0:T(8,128)(2,1)S(1)}, bf16[20,80,128]{2,1,0:T(8,128)(2,1)S(1)}, u32[]{:S(2)}, u32[]{:S(2)}) collective-permute-start(bf16[20,80,128]{2,1,0:T(8,128)(2,1)S(1)} %collective-permute-done.2.pair_ref), channel_id=1, source_target_pairs={{1,5},{3,7},{5,1},{7,3},{8,12},{10,14},{12,8},{14,10},{17,21},{19,... | collective-permute-start | bytes 1228808 | tf_op jit(solution)/shard_map/ppermute | solution.py:387
  28.3 0.0 collective-permute-done.5.next_ref
  28.3 0.0 collective-permute-done.1.given_ref
  28.3 0.0 collective-permute-done.4.left_other
  28.3 5.1 %shard_map.102 = (bf16[10,40,128]{2,1,0:T(8,128)(2,1)S(1)}, bf16[10,40,128]{2,1,0:T(8,128)(2,1)S(1)}, bf16[10,40,128]{2,1,0:T(8,128)(2,1)S(1)}, bf16[10,40,128]{2,1,0:T(8,128)(2,1)S(1)}) custom-call(s32[5]{0:T(128)S(1)} %stack.27.flags_ref, bf16[20,80,128]{2,1,0:T(8,128)(2,1)S(1)} %get-tuple-element.21.left_ref, ...), custom_call_target="tpu_custom_call" | custom-call | flops 6270000128 | bytes 17100000 | tf_op jit(solution)/shard_map/pallas_call | solution.py:339
  33.4 0.1 collective-permute-start.7
  33.4 0.7 %collective-permute-start.8 = (bf16[10,40,128]{2,1,0:T(8,128)(2,1)S(1)}, bf16[10,40,128]{2,1,0:T(8,128)(2,1)S(1)}, u32[]{:S(2)}, u32[]{:S(2)}) collective-permute-start(bf16[10,40,128]{2,1,0:T(8,128)(2,1)S(1)} %get-tuple-element.29), channel_id=1, source_target_pairs={{0,2},{1,3},{2,0},{3,1},{4,6},{5,7},{6,4},{7,5},{8,10},{9,11},{10,... | collective-permute-start | bytes 307208 | tf_op jit(solution)/shard_map/ppermute | solution.py:387
  34.1 1.4 %collective-permute-start.9 = (bf16[10,40,128]{2,1,0:T(8,128)(2,1)S(1)}, bf16[10,40,128]{2,1,0:T(8,128)(2,1)S(1)}, u32[]{:S(2)}, u32[]{:S(2)}) collective-permute-start(bf16[10,40,128]{2,1,0:T(8,128)(2,1)S(1)} %get-tuple-element.30), channel_id=1, source_target_pairs={{0,3},{1,2},{2,1},{3,0},{4,7},{5,6},{6,5},{7,4},{8,11},{9,10},{10,... | collective-permute-start | bytes 307208 | tf_op jit(solution)/shard_map/ppermute | solution.py:387
  35.5 3.0 %collective-permute-done.10.across_ref = bf16[20,80,128]{2,1,0:T(8,128)(2,1)S(1)} collective-permute-done((bf16[20,80,128]{2,1,0:T(8,128)(2,1)S(1)}, bf16[20,80,128]{2,1,0:T(8,128)(2,1)S(1)}, u32[]{:S(2)}, u32[]{:S(2)}) %collective-permute-start.10) | collective-permute-done | bytes 409632 | tf_op jit(solution)/shard_map/ppermute | solution.py:387
  38.5 0.4 collective-permute-done.3.straight_ref
  38.8 1.3 %collective-permute-start.11 = (bf16[20,80,128]{2,1,0:T(8,128)(2,1)S(1)}, bf16[20,80,128]{2,1,0:T(8,128)(2,1)S(1)}, u32[]{:S(2)}, u32[]{:S(2)}) collective-permute-start(bf16[20,80,128]{2,1,0:T(8,128)(2,1)S(1)} %collective-permute-done.10.across_ref), channel_id=1, source_target_pairs={{0,2},{1,3},{2,0},{3,1},{4,6},{5,7},{6,4},{7,5},{8,10},{9,11},{10,... | collective-permute-start | bytes 1228808 | tf_op jit(solution)/shard_map/ppermute | solution.py:387
  40.1 0.0 collective-permute-start.6
  40.1 2.9 %shard_map.104.mine_ref = f32[20,20,128]{2,1,0:T(8,128)S(1)} custom-call(s32[5]{0:T(128)S(1)} %stack.27.flags_ref, bf16[20,80,128]{2,1,0:T(8,128)(2,1)S(1)} %get-tuple-element.21.left_ref, bf16[20,80,128]{2,1,0:T(8,128)(2,1)S(1)} %collective-permute-done.1.given_ref, bf16[20,80,128]{2,1,0:T(8,128)(2,1)S(1)} %collective-permute-done.3.straight_ref, ...), custom_call_target="tpu_custom_call" | custom-call | flops 110000000 | bytes 300000 | tf_op jit(solution)/shard_map/pallas_call | solution.py:339
  43.0 0.0 collective-permute-done.7.own_given
  43.1 0.0 collective-permute-done.8.partner_ref
  43.1 0.6 %collective-permute-done.9.partner_given = bf16[10,40,128]{2,1,0:T(8,128)(2,1)S(1)} collective-permute-done((bf16[10,40,128]{2,1,0:T(8,128)(2,1)S(1)}, bf16[10,40,128]{2,1,0:T(8,128)(2,1)S(1)}, u32[]{:S(2)}, u32[]{:S(2)}) %collective-permute-start.9) | collective-permute-done | bytes 102432 | tf_op jit(solution)/shard_map/ppermute | solution.py:387
  43.6 0.0 copy-done.6
  43.6 1.0 %shard_map.103.done_ref = bf16[20,40,128]{2,1,0:T(8,128)(2,1)S(1)} custom-call(s32[5]{0:T(128)S(1)} %stack.27.flags_ref, bf16[10,40,128]{2,1,0:T(8,128)(2,1)S(1)} %get-tuple-element.26.own_ref, bf16[10,40,128]{2,1,0:T(8,128)(2,1)S(1)} %collective-permute-done.7.own_given, bf16[10,40,128]{2,1,0:T(8,128)(2,1)S(1)} %collective-permute-done.8.partner_ref, ...), custom_call_target="tpu_custom_call" | custom-call | flops 8800000000 | bytes 24000000 | tf_op jit(solution)/shard_map/pallas_call | solution.py:339
  44.6 0.0 collective-permute-done.11.across_ref
  44.6 0.0 collective-permute-done.6.straight_ref
  44.6 4.0 %shard_map.105 = bf16[20,80,128]{2,1,0:T(8,128)(2,1)} custom-call(s32[5]{0:T(128)S(1)} %stack.27.flags_ref, bf16[20,80,128]{2,1,0:T(8,128)(2,1)S(1)} %get-tuple-element.21.left_ref, bf16[20,80,128]{2,1,0:T(8,128)(2,1)S(1)} %collective-permute-done.1.given_ref, bf16[20,80,128]{2,1,0:T(8,128)(2,1)S(1)} %collective-permute-done.6.straight_ref, ...), custom_call_target="tpu_custom_call" | custom-call | flops 4400000000 | bytes 12000000 | tf_op jit(solution)/shard_map/pallas_call | solution.py:339
  (3 shorter events, 0.0 us)
Async XLA Ops:
  0.0 0.7 %copy-start.7 = (s32[160]{0:T(256)S(1)}, s32[160]{0:T(256)}, u32[]{:S(2)}) copy-start(s32[160]{0:T(256)} %param.11) | copy-start | bytes 1924
  0.0 0.7 %copy-start.8 = (f32[128]{0:T(128)S(1)}, f32[128]{0:T(128)}, u32[]{:S(2)}) copy-start(f32[128]{0:T(128)} %param.12) | copy-start | bytes 1540
  0.0 0.8 %copy-start.1 = (bf16[128,128]{1,0:T(8,128)(2,1)S(1)}, bf16[128,128]{1,0:T(8,128)(2,1)}, u32[]{:S(2)}) copy-start(bf16[128,128]{1,0:T(8,128)(2,1)} %proj_ref.4) | copy-start | bytes 98308
  0.0 0.8 %copy-start.2 = (bf16[128,128]{1,0:T(8,128)(2,1)S(1)}, bf16[128,128]{1,0:T(8,128)(2,1)}, u32[]{:S(2)}) copy-start(bf16[128,128]{1,0:T(8,128)(2,1)} %gate_ref.2) | copy-start | bytes 98308
  0.8 1.0 %copy-start = (bf16[20,80,128]{2,1,0:T(8,128)(2,1)S(1)}, bf16[20,80,128]{2,1,0:T(8,128)(2,1)}, u32[]{:S(2)}) copy-start(bf16[20,80,128]{2,1,0:T(8,128)(2,1)} %pair_ref.3) | copy-start | bytes 1228804
  1.8 3.6 %copy-start.3 = (bf16[128,128]{1,0:T(8,128)(2,1)S(1)}, bf16[128,128]{1,0:T(8,128)(2,1)}, u32[]{:S(2)}) copy-start(bf16[128,128]{1,0:T(8,128)(2,1)} %proj_ref.5) | copy-start | bytes 98308
  1.8 3.6 %copy-start.4 = (bf16[128,128]{1,0:T(8,128)(2,1)S(1)}, bf16[128,128]{1,0:T(8,128)(2,1)}, u32[]{:S(2)}) copy-start(bf16[128,128]{1,0:T(8,128)(2,1)} %gate_ref.3) | copy-start | bytes 98308
  1.8 3.6 %copy-start.5 = (bf16[128,128]{1,0:T(8,128)(2,1)S(1)}, bf16[128,128]{1,0:T(8,128)(2,1)}, u32[]{:S(2)}) copy-start(bf16[128,128]{1,0:T(8,128)(2,1)} %out_gate_ref.1) | copy-start | bytes 98308
  3.3 2.1 %copy-start.9 = (f32[128]{0:T(128)S(1)}, f32[128]{0:T(128)}, u32[]{:S(2)}) copy-start(f32[128]{0:T(128)} %param.17) | copy-start | bytes 1540
  3.3 2.1 %collective-permute-start = (bf16[20,80,128]{2,1,0:T(8,128)(2,1)S(1)}, bf16[20,80,128]{2,1,0:T(8,128)(2,1)S(1)}, u32[]{:S(2)}, u32[]{:S(2)}) collective-permute-start(bf16[20,80,128]{2,1,0:T(8,128)(2,1)S(1)} %shard_map.100.mine_ref), channel_id=1, source_target_pairs={{0,2},{1,3},{2,0},{3,1},{4,6},{5,7},{6,4},{7,5},{8,10},{9,11},{10,... | collective-permute-start | bytes 1228808 | tf_op jit(solution)/shard_map/ppermute | solution.py:387
  4.0 21.0 %collective-permute-start.2 = (bf16[20,80,128]{2,1,0:T(8,128)(2,1)S(1)}, bf16[20,80,128]{2,1,0:T(8,128)(2,1)S(1)}, u32[]{:S(2)}, u32[]{:S(2)}) collective-permute-start(bf16[20,80,128]{2,1,0:T(8,128)(2,1)S(1)} %shard_map.100.mine_ref), channel_id=1, source_target_pairs={{0,8},{1,9},{2,10},{3,11},{4,12},{5,13},{6,14},{7,15},{8,0},{9,1},... | collective-permute-start | bytes 1228808 | tf_op jit(solution)/shard_map/ppermute | solution.py:387
  4.1 24.2 %collective-permute-start.5 = (bf16[20,80,128]{2,1,0:T(8,128)(2,1)S(1)}, bf16[20,80,128]{2,1,0:T(8,128)(2,1)S(1)}, u32[]{:S(2)}, u32[]{:S(2)}) collective-permute-start(bf16[20,80,128]{2,1,0:T(8,128)(2,1)S(1)} %shard_map.100.mine_ref), channel_id=1, source_target_pairs={{0,4},{1,5},{2,6},{3,7},{4,0},{5,1},{6,2},{7,3},{8,12},{9,13},{10,... | collective-permute-start | bytes 1228808 | tf_op jit(solution)/shard_map/ppermute | solution.py:387
  9.2 19.1 %collective-permute-start.1 = (bf16[20,80,128]{2,1,0:T(8,128)(2,1)S(1)}, bf16[20,80,128]{2,1,0:T(8,128)(2,1)S(1)}, u32[]{:S(2)}, u32[]{:S(2)}) collective-permute-start(bf16[20,80,128]{2,1,0:T(8,128)(2,1)S(1)} %get-tuple-element.22), channel_id=1, source_target_pairs={{0,1},{1,0},{2,3},{3,2},{4,5},{5,4},{6,7},{7,6},{8,9},{9,8},{10,11... | collective-permute-start | bytes 1228808 | tf_op jit(solution)/shard_map/ppermute | solution.py:387
  10.4 17.9 %collective-permute-start.4 = (bf16[20,80,128]{2,1,0:T(8,128)(2,1)S(1)}, bf16[20,80,128]{2,1,0:T(8,128)(2,1)S(1)}, u32[]{:S(2)}, u32[]{:S(2)}) collective-permute-start(bf16[20,80,128]{2,1,0:T(8,128)(2,1)S(1)} %get-tuple-element.21.left_ref), channel_id=1, source_target_pairs={{0,2},{1,3},{2,0},{3,1},{4,6},{5,7},{6,4},{7,5},{8,10},{9,11},{10,... | collective-permute-start | bytes 1228808 | tf_op jit(solution)/shard_map/ppermute | solution.py:387
  25.0 13.4 %collective-permute-start.10 = (bf16[20,80,128]{2,1,0:T(8,128)(2,1)S(1)}, bf16[20,80,128]{2,1,0:T(8,128)(2,1)S(1)}, u32[]{:S(2)}, u32[]{:S(2)}) collective-permute-start(bf16[20,80,128]{2,1,0:T(8,128)(2,1)S(1)} %collective-permute-done.2.pair_ref), channel_id=1, source_target_pairs={{0,5},{2,7},{4,1},{6,3},{9,12},{11,14},{13,8},{15,10},{16,21},{18,... | collective-permute-start | bytes 1228808 | tf_op jit(solution)/shard_map/ppermute | solution.py:387
  26.3 12.5 %collective-permute-start.3 = (bf16[20,80,128]{2,1,0:T(8,128)(2,1)S(1)}, bf16[20,80,128]{2,1,0:T(8,128)(2,1)S(1)}, u32[]{:S(2)}, u32[]{:S(2)}) collective-permute-start(bf16[20,80,128]{2,1,0:T(8,128)(2,1)S(1)} %collective-permute-done.2.pair_ref), channel_id=1, source_target_pairs={{1,5},{3,7},{5,1},{7,3},{8,12},{10,14},{12,8},{14,10},{17,21},{19,... | collective-permute-start | bytes 1228808 | tf_op jit(solution)/shard_map/ppermute | solution.py:387
  33.4 9.7 %collective-permute-start.7 = (bf16[10,40,128]{2,1,0:T(8,128)(2,1)S(1)}, bf16[10,40,128]{2,1,0:T(8,128)(2,1)S(1)}, u32[]{:S(2)}, u32[]{:S(2)}) collective-permute-start(bf16[10,40,128]{2,1,0:T(8,128)(2,1)S(1)} %get-tuple-element.28), channel_id=1, source_target_pairs={{0,1},{1,0},{2,3},{3,2},{4,5},{5,4},{6,7},{7,6},{8,9},{9,8},{10,11... | collective-permute-start | bytes 307208 | tf_op jit(solution)/shard_map/ppermute | solution.py:387
  33.4 9.6 %collective-permute-start.8 = (bf16[10,40,128]{2,1,0:T(8,128)(2,1)S(1)}, bf16[10,40,128]{2,1,0:T(8,128)(2,1)S(1)}, u32[]{:S(2)}, u32[]{:S(2)}) collective-permute-start(bf16[10,40,128]{2,1,0:T(8,128)(2,1)S(1)} %get-tuple-element.29), channel_id=1, source_target_pairs={{0,2},{1,3},{2,0},{3,1},{4,6},{5,7},{6,4},{7,5},{8,10},{9,11},{10,... | collective-permute-start | bytes 307208 | tf_op jit(solution)/shard_map/ppermute | solution.py:387
  34.1 9.5 %collective-permute-start.9 = (bf16[10,40,128]{2,1,0:T(8,128)(2,1)S(1)}, bf16[10,40,128]{2,1,0:T(8,128)(2,1)S(1)}, u32[]{:S(2)}, u32[]{:S(2)}) collective-permute-start(bf16[10,40,128]{2,1,0:T(8,128)(2,1)S(1)} %get-tuple-element.30), channel_id=1, source_target_pairs={{0,3},{1,2},{2,1},{3,0},{4,7},{5,6},{6,5},{7,4},{8,11},{9,10},{10,... | collective-permute-start | bytes 307208 | tf_op jit(solution)/shard_map/ppermute | solution.py:387
  38.5 5.1 %copy-start.6 = (bf16[128,128]{1,0:T(8,128)(2,1)S(1)}, bf16[128,128]{1,0:T(8,128)(2,1)}, u32[]{:S(2)}) copy-start(bf16[128,128]{1,0:T(8,128)(2,1)} %proj_ref.7) | copy-start | bytes 98308
  38.8 5.8 %collective-permute-start.11 = (bf16[20,80,128]{2,1,0:T(8,128)(2,1)S(1)}, bf16[20,80,128]{2,1,0:T(8,128)(2,1)S(1)}, u32[]{:S(2)}, u32[]{:S(2)}) collective-permute-start(bf16[20,80,128]{2,1,0:T(8,128)(2,1)S(1)} %collective-permute-done.10.across_ref), channel_id=1, source_target_pairs={{0,2},{1,3},{2,0},{3,1},{4,6},{5,7},{6,4},{7,5},{8,10},{9,11},{10,... | collective-permute-start | bytes 1228808 | tf_op jit(solution)/shard_map/ppermute | solution.py:387
  40.1 4.5 %collective-permute-start.6 = (bf16[20,80,128]{2,1,0:T(8,128)(2,1)S(1)}, bf16[20,80,128]{2,1,0:T(8,128)(2,1)S(1)}, u32[]{:S(2)}, u32[]{:S(2)}) collective-permute-start(bf16[20,80,128]{2,1,0:T(8,128)(2,1)S(1)} %collective-permute-done.3.straight_ref), channel_id=1, source_target_pairs={{0,2},{1,3},{2,0},{3,1},{4,6},{5,7},{6,4},{7,5},{8,10},{9,11},{10,... | collective-permute-start | bytes 1228808 | tf_op jit(solution)/shard_map/ppermute | solution.py:387

commit v5 on v4

--- a/solution.py
+++ b/solution.py
@@ -382,8 +382,8 @@
     over_col = [(p, p ^ 1) for p in places]
     over_both = [(p, p ^ 3) for p in places]
     keeps_far = lambda p: p // 8 != p % 2
-    straight = [(p, p ^ 4) for p in places if keeps_far(p ^ 4)]
-    across = [(p, p ^ 5) for p in places if keeps_far(p ^ 5)]
+    straight = [(p, p ^ 4 if keeps_far(p ^ 4) else p ^ 2) for p in places]
+    across = [(p, p ^ 5 if keeps_far(p ^ 5) else p ^ 1) for p in places]
     send = lambda value, pairs: lax.ppermute(value, LINE, pairs)
 
     bf16 = lambda *shape: jax.ShapeDtypeStruct(shape, jnp.bfloat16)
@@ -414,8 +414,8 @@
     given = send(swap, over_col)
     left_other = send(left, over_core)
 
-    from_pair = after(from_pair, left)
-    from_next = after(from_next, from_pair, given)
+    from_next = after(from_next, left)
+    from_pair = after(from_pair, from_next, given)
     far_straight, far_across = send(from_pair, straight), send(from_pair, across)
     kept_own, kept_other, sent_own, sent_other = call(
         middle_kernel,
@@ -437,7 +437,7 @@
         swapped_kernel,
         8.0,
         bf16(*two),
-    )(flags, kept_own, kept_given, partner, partner_given, hidden_gain, out_proj, gating)
+    )(flags, after(kept_own, mine), kept_given, partner, partner_given, hidden_gain, out_proj, gating)
     other_straight, other_across = after(other_straight, done), after(other_across, done)
     return call(
         finish_kernel,

time: 48.9 us -> 46.9 us (0.959)
  waiting for transfers between devices: 19.1 us -> 17 us
    ppermute x12, waiting for transfers between devices: 19.1 us -> 17 us  [exchanged(): send = lambda value, pairs: lax.ppermute(value, LINE, pairs)]
  transfers between devices with their start and end apart: 12 -> 12, of which waited for: 5 -> 5; matrix products, arithmetic and copies ran while one was open for 0% -> 0% of each run, Pallas kernels for 26% -> 27%
where the time goes in v5:
time: 46.9 us; the launch traced here: 46.4 us
  Pallas kernels  18.2 us (39%)
  waiting for transfers between devices  17 us (36%)
  starting transfers between devices  9.29 us (20%)
  local copies, waits for them, and re-layouts  1.78 us (4%)
    pallas_call x6, Pallas kernels, run(): pl.pallas_call(kernel, out_shape=out_shape, in_specs=[pl.BlockSpec(memory...  18.2 us
    ppermute x12, waiting for transfers between devices, exchanged(): send = lambda value, pairs: lax.ppermute(value, LINE, pairs)  17 us
    ppermute x12, starting transfers between devices, exchanged(): send = lambda value, pairs: lax.ppermute(value, LINE, pairs)  9.29 us
    unnamed x20, local copies, waits for them, and re-layouts  1.7 us
  transfers between devices with their start and end apart: 12, of which 5 were waited for; matrix products, arithmetic and copies ran while one was open for 0% of the time, Pallas kernels for 27%

profile of v5, /device:TPU:25, one launch (start us, length us, event | category | flops | bytes accessed | tf_op | source)
XLA Modules:
  0.0 46.4 jit_solution(14098174958258980755)
XLA Ops:
  0.0 0.0 copy-start.7
  0.0 0.0 copy-start.8
  0.0 0.0 copy-start.1
  0.0 0.0 copy-start.2
  0.1 0.1 stack.27.flags_ref
  0.1 0.5 %copy-done.7 = s32[160]{0:T(256)S(1)} copy-done((s32[160]{0:T(256)S(1)}, s32[160]{0:T(256)}, u32[]{:S(2)}) %copy-start.7) | copy-done | bytes 664
  0.7 0.0 copy-done.8
  0.7 0.1 copy-done.1
  0.8 0.0 copy-done.2
  0.8 0.0 copy-start
  0.8 1.0 %copy-done = bf16[20,80,128]{2,1,0:T(8,128)(2,1)S(1)} copy-done((bf16[20,80,128]{2,1,0:T(8,128)(2,1)S(1)}, bf16[20,80,128]{2,1,0:T(8,128)(2,1)}, u32[]{:S(2)}) %copy-start) | copy-done | bytes 409624
  1.8 0.0 copy-start.3
  1.8 1.5 %shard_map.100.mine_ref = bf16[20,80,128]{2,1,0:T(8,128)(2,1)S(1)} custom-call(s32[5]{0:T(128)S(1)} %stack.27.flags_ref, bf16[20,80,128]{2,1,0:T(8,128)(2,1)S(1)} %copy-done, s32[1,160]{1,0:T(1,128)S(1)} %bitcast.9, f32[1,128]{1,0:T(1,128)S(1)} %bitcast.11, bf16[128,128]{1,0:T(8,128)(2,1)S(1)} %copy-done.1, bf16[128,128]{1,0:T(8,128)(2,1)S(1)} %copy-done.2), custom_call_target="tpu_custom_call" | custom-call | flops 2420000000 | bytes 6600000 | tf_op jit(solution)/shard_map/pallas_call | solution.py:339
  3.3 0.0 copy-start.9
  3.3 0.7 %collective-permute-start = (bf16[20,80,128]{2,1,0:T(8,128)(2,1)S(1)}, bf16[20,80,128]{2,1,0:T(8,128)(2,1)S(1)}, u32[]{:S(2)}, u32[]{:S(2)}) collective-permute-start(bf16[20,80,128]{2,1,0:T(8,128)(2,1)S(1)} %shard_map.100.mine_ref), channel_id=1, source_target_pairs={{0,2},{1,3},{2,0},{3,1},{4,6},{5,7},{6,4},{7,5},{8,10},{9,11},{10,... | collective-permute-start | bytes 1228808 | tf_op jit(solution)/shard_map/ppermute | solution.py:387
  4.0 0.2 collective-permute-start.3
  4.2 0.0 collective-permute-start.2
  4.2 1.2 %collective-permute-done.other_ref = bf16[20,80,128]{2,1,0:T(8,128)(2,1)S(1)} collective-permute-done((bf16[20,80,128]{2,1,0:T(8,128)(2,1)S(1)}, bf16[20,80,128]{2,1,0:T(8,128)(2,1)S(1)}, u32[]{:S(2)}, u32[]{:S(2)}) %collective-permute-start) | collective-permute-done | bytes 409632 | tf_op jit(solution)/shard_map/ppermute | solution.py:387
  5.4 0.0 copy-done.3
  5.4 0.0 copy-done.4
  5.4 0.0 copy-done.5
  5.4 0.0 copy-done.9
  5.4 3.7 %shard_map.101 = (bf16[20,80,128]{2,1,0:T(8,128)(2,1)S(1)}, f32[1600,128]{1,0:T(8,128)S(1)}, bf16[20,40,128]{2,1,0:T(8,128)(2,1)S(1)}, bf16[20,80,128]{2,1,0:T(8,128)(2,1)S(1)}, f32[1,128]{1,0:T(1,128)S(1)}) custom-call(s32[5]{0:T(128)S(1)} %stack.27.flags_ref, bf16[20,80,128]{2,1,0:T(8,128)(2,1)S(1)} %copy-done, s32[1,160]{1,0:T(1,128)S(1)} %bitcast.10, ...), custom_call_target="tpu_custom_call" | custom-call | flops 4400000000 | bytes 12000000 | tf_op jit(solution)/shard_map/pallas_call | solution.py:339
  9.2 1.2 %collective-permute-start.1 = (bf16[20,80,128]{2,1,0:T(8,128)(2,1)S(1)}, bf16[20,80,128]{2,1,0:T(8,128)(2,1)S(1)}, u32[]{:S(2)}, u32[]{:S(2)}) collective-permute-start(bf16[20,80,128]{2,1,0:T(8,128)(2,1)S(1)} %get-tuple-element.23), channel_id=1, source_target_pairs={{0,1},{1,0},{2,3},{3,2},{4,5},{5,4},{6,7},{7,6},{8,9},{9,8},{10,11... | collective-permute-start | bytes 1228808 | tf_op jit(solution)/shard_map/ppermute | solution.py:387
  10.4 0.7 %collective-permute-start.5 = (bf16[20,80,128]{2,1,0:T(8,128)(2,1)S(1)}, bf16[20,80,128]{2,1,0:T(8,128)(2,1)S(1)}, u32[]{:S(2)}, u32[]{:S(2)}) collective-permute-start(bf16[20,80,128]{2,1,0:T(8,128)(2,1)S(1)} %get-tuple-element.22.left_ref), channel_id=1, source_target_pairs={{0,2},{1,3},{2,0},{3,1},{4,6},{5,7},{6,4},{7,5},{8,10},{9,11},{10,... | collective-permute-start | bytes 1228808 | tf_op jit(solution)/shard_map/ppermute | solution.py:387
  11.1 11.6 %collective-permute-done.3.next_ref = bf16[20,80,128]{2,1,0:T(8,128)(2,1)S(1)} collective-permute-done((bf16[20,80,128]{2,1,0:T(8,128)(2,1)S(1)}, bf16[20,80,128]{2,1,0:T(8,128)(2,1)S(1)}, u32[]{:S(2)}, u32[]{:S(2)}) %collective-permute-start.3) | collective-permute-done | bytes 409632 | tf_op jit(solution)/shard_map/ppermute | solution.py:387
  22.6 2.0 %collective-permute-done.2.pair_ref = bf16[20,80,128]{2,1,0:T(8,128)(2,1)S(1)} collective-permute-done((bf16[20,80,128]{2,1,0:T(8,128)(2,1)S(1)}, bf16[20,80,128]{2,1,0:T(8,128)(2,1)S(1)}, u32[]{:S(2)}, u32[]{:S(2)}) %collective-permute-start.2) | collective-permute-done | bytes 409632 | tf_op jit(solution)/shard_map/ppermute | solution.py:387
  24.6 0.0 collective-permute-done.1.given_ref
  24.6 1.2 %collective-permute-start.7 = (bf16[20,80,128]{2,1,0:T(8,128)(2,1)S(1)}, bf16[20,80,128]{2,1,0:T(8,128)(2,1)S(1)}, u32[]{:S(2)}, u32[]{:S(2)}) collective-permute-start(bf16[20,80,128]{2,1,0:T(8,128)(2,1)S(1)} %collective-permute-done.2.pair_ref), channel_id=1, source_target_pairs={{0,5},{1,0},{2,7},{3,2},{4,1},{5,4},{6,3},{7,6},{8,9},{9,12},{10,1... | collective-permute-start | bytes 1228808 | tf_op jit(solution)/shard_map/ppermute | solution.py:387
  25.9 0.0 collective-permute-start.4
  25.9 0.0 collective-permute-done.5.left_other
  25.9 5.1 %shard_map.102 = (bf16[10,40,128]{2,1,0:T(8,128)(2,1)S(1)}, bf16[10,40,128]{2,1,0:T(8,128)(2,1)S(1)}, bf16[10,40,128]{2,1,0:T(8,128)(2,1)S(1)}, bf16[10,40,128]{2,1,0:T(8,128)(2,1)S(1)}) custom-call(s32[5]{0:T(128)S(1)} %stack.27.flags_ref, bf16[20,80,128]{2,1,0:T(8,128)(2,1)S(1)} %get-tuple-element.22.left_ref, ...), custom_call_target="tpu_custom_call" | custom-call | flops 6270000128 | bytes 17100000 | tf_op jit(solution)/shard_map/pallas_call | solution.py:339
  30.9 1.1 %collective-permute-start.10 = (bf16[10,40,128]{2,1,0:T(8,128)(2,1)S(1)}, bf16[10,40,128]{2,1,0:T(8,128)(2,1)S(1)}, u32[]{:S(2)}, u32[]{:S(2)}) collective-permute-start(bf16[10,40,128]{2,1,0:T(8,128)(2,1)S(1)} %get-tuple-element.33), channel_id=1, source_target_pairs={{0,3},{1,2},{2,1},{3,0},{4,7},{5,6},{6,5},{7,4},{8,11},{9,10},{10,... | collective-permute-start | bytes 307208 | tf_op jit(solution)/shard_map/ppermute | solution.py:387
  32.1 1.7 %collective-permute-start.8 = (bf16[10,40,128]{2,1,0:T(8,128)(2,1)S(1)}, bf16[10,40,128]{2,1,0:T(8,128)(2,1)S(1)}, u32[]{:S(2)}, u32[]{:S(2)}) collective-permute-start(bf16[10,40,128]{2,1,0:T(8,128)(2,1)S(1)} %get-tuple-element.31), channel_id=1, source_target_pairs={{0,1},{1,0},{2,3},{3,2},{4,5},{5,4},{6,7},{7,6},{8,9},{9,8},{10,11... | collective-permute-start | bytes 307208 | tf_op jit(solution)/shard_map/ppermute | solution.py:387
  33.8 0.0 collective-permute-start.9
  33.8 1.5 %collective-permute-done.7.across_ref = bf16[20,80,128]{2,1,0:T(8,128)(2,1)S(1)} collective-permute-done((bf16[20,80,128]{2,1,0:T(8,128)(2,1)S(1)}, bf16[20,80,128]{2,1,0:T(8,128)(2,1)S(1)}, u32[]{:S(2)}, u32[]{:S(2)}) %collective-permute-start.7) | collective-permute-done | bytes 409632 | tf_op jit(solution)/shard_map/ppermute | solution.py:387
  35.3 0.0 collective-permute-done.4.straight_ref
  35.4 2.4 %collective-permute-start.11 = (bf16[20,80,128]{2,1,0:T(8,128)(2,1)S(1)}, bf16[20,80,128]{2,1,0:T(8,128)(2,1)S(1)}, u32[]{:S(2)}, u32[]{:S(2)}) collective-permute-start(bf16[20,80,128]{2,1,0:T(8,128)(2,1)S(1)} %collective-permute-done.7.across_ref), channel_id=1, source_target_pairs={{0,2},{1,3},{2,0},{3,1},{4,6},{5,7},{6,4},{7,5},{8,10},{9,11},{10,... | collective-permute-start | bytes 1228808 | tf_op jit(solution)/shard_map/ppermute | solution.py:387
  37.7 0.0 collective-permute-start.6
  37.8 2.9 %shard_map.103.mine_ref = f32[20,20,128]{2,1,0:T(8,128)S(1)} custom-call(s32[5]{0:T(128)S(1)} %stack.27.flags_ref, bf16[20,80,128]{2,1,0:T(8,128)(2,1)S(1)} %get-tuple-element.22.left_ref, bf16[20,80,128]{2,1,0:T(8,128)(2,1)S(1)} %collective-permute-done.1.given_ref, bf16[20,80,128]{2,1,0:T(8,128)(2,1)S(1)} %collective-permute-done.4.straight_ref, ...), custom_call_target="tpu_custom_call" | custom-call | flops 110000000 | bytes 300000 | tf_op jit(solution)/shard_map/pallas_call | solution.py:339
  40.7 0.0 collective-permute-done.10.partner_given
  40.7 0.7 %collective-permute-done.8.own_given = bf16[10,40,128]{2,1,0:T(8,128)(2,1)S(1)} collective-permute-done((bf16[10,40,128]{2,1,0:T(8,128)(2,1)S(1)}, bf16[10,40,128]{2,1,0:T(8,128)(2,1)S(1)}, u32[]{:S(2)}, u32[]{:S(2)}) %collective-permute-start.8) | collective-permute-done | bytes 102432 | tf_op jit(solution)/shard_map/ppermute | solution.py:387
  41.4 0.0 collective-permute-done.9.partner_ref
  41.4 0.0 copy-done.6
  41.4 1.0 %shard_map.104.done_ref = bf16[20,40,128]{2,1,0:T(8,128)(2,1)S(1)} custom-call(s32[5]{0:T(128)S(1)} %stack.27.flags_ref, bf16[10,40,128]{2,1,0:T(8,128)(2,1)S(1)} %get-tuple-element.30.own_ref, bf16[10,40,128]{2,1,0:T(8,128)(2,1)S(1)} %collective-permute-done.8.own_given, bf16[10,40,128]{2,1,0:T(8,128)(2,1)S(1)} %collective-permute-done.9.partner_ref, ...), custom_call_target="tpu_custom_call" | custom-call | flops 8800000000 | bytes 24000000 | tf_op jit(solution)/shard_map/pallas_call | solution.py:339
  42.3 0.0 collective-permute-done.11.across_ref
  42.3 0.0 collective-permute-done.6.straight_ref
  42.3 4.0 %shard_map.105 = bf16[20,80,128]{2,1,0:T(8,128)(2,1)} custom-call(s32[5]{0:T(128)S(1)} %stack.27.flags_ref, bf16[20,80,128]{2,1,0:T(8,128)(2,1)S(1)} %get-tuple-element.22.left_ref, bf16[20,80,128]{2,1,0:T(8,128)(2,1)S(1)} %collective-permute-done.1.given_ref, bf16[20,80,128]{2,1,0:T(8,128)(2,1)S(1)} %collective-permute-done.6.straight_ref, ...), custom_call_target="tpu_custom_call" | custom-call | flops 4400000000 | bytes 12000000 | tf_op jit(solution)/shard_map/pallas_call | solution.py:339
  (3 shorter events, 0.0 us)
Async XLA Ops:
  0.0 0.7 %copy-start.7 = (s32[160]{0:T(256)S(1)}, s32[160]{0:T(256)}, u32[]{:S(2)}) copy-start(s32[160]{0:T(256)} %param.11) | copy-start | bytes 1924
  0.0 0.7 %copy-start.8 = (f32[128]{0:T(128)S(1)}, f32[128]{0:T(128)}, u32[]{:S(2)}) copy-start(f32[128]{0:T(128)} %param.12) | copy-start | bytes 1540
  0.0 0.8 %copy-start.1 = (bf16[128,128]{1,0:T(8,128)(2,1)S(1)}, bf16[128,128]{1,0:T(8,128)(2,1)}, u32[]{:S(2)}) copy-start(bf16[128,128]{1,0:T(8,128)(2,1)} %proj_ref.4) | copy-start | bytes 98308
  0.0 0.8 %copy-start.2 = (bf16[128,128]{1,0:T(8,128)(2,1)S(1)}, bf16[128,128]{1,0:T(8,128)(2,1)}, u32[]{:S(2)}) copy-start(bf16[128,128]{1,0:T(8,128)(2,1)} %gate_ref.2) | copy-start | bytes 98308
  0.8 1.0 %copy-start = (bf16[20,80,128]{2,1,0:T(8,128)(2,1)S(1)}, bf16[20,80,128]{2,1,0:T(8,128)(2,1)}, u32[]{:S(2)}) copy-start(bf16[20,80,128]{2,1,0:T(8,128)(2,1)} %pair_ref.3) | copy-start | bytes 1228804
  1.8 3.6 %copy-start.3 = (bf16[128,128]{1,0:T(8,128)(2,1)S(1)}, bf16[128,128]{1,0:T(8,128)(2,1)}, u32[]{:S(2)}) copy-start(bf16[128,128]{1,0:T(8,128)(2,1)} %proj_ref.5) | copy-start | bytes 98308
  1.8 3.6 %copy-start.4 = (bf16[128,128]{1,0:T(8,128)(2,1)S(1)}, bf16[128,128]{1,0:T(8,128)(2,1)}, u32[]{:S(2)}) copy-start(bf16[128,128]{1,0:T(8,128)(2,1)} %gate_ref.3) | copy-start | bytes 98308
  1.8 3.6 %copy-start.5 = (bf16[128,128]{1,0:T(8,128)(2,1)S(1)}, bf16[128,128]{1,0:T(8,128)(2,1)}, u32[]{:S(2)}) copy-start(bf16[128,128]{1,0:T(8,128)(2,1)} %out_gate_ref.1) | copy-start | bytes 98308
  3.3 2.1 %copy-start.9 = (f32[128]{0:T(128)S(1)}, f32[128]{0:T(128)}, u32[]{:S(2)}) copy-start(f32[128]{0:T(128)} %param.17) | copy-start | bytes 1540
  3.3 2.1 %collective-permute-start = (bf16[20,80,128]{2,1,0:T(8,128)(2,1)S(1)}, bf16[20,80,128]{2,1,0:T(8,128)(2,1)S(1)}, u32[]{:S(2)}, u32[]{:S(2)}) collective-permute-start(bf16[20,80,128]{2,1,0:T(8,128)(2,1)S(1)} %shard_map.100.mine_ref), channel_id=1, source_target_pairs={{0,2},{1,3},{2,0},{3,1},{4,6},{5,7},{6,4},{7,5},{8,10},{9,11},{10,... | collective-permute-start | bytes 1228808 | tf_op jit(solution)/shard_map/ppermute | solution.py:387
  4.0 18.6 %collective-permute-start.3 = (bf16[20,80,128]{2,1,0:T(8,128)(2,1)S(1)}, bf16[20,80,128]{2,1,0:T(8,128)(2,1)S(1)}, u32[]{:S(2)}, u32[]{:S(2)}) collective-permute-start(bf16[20,80,128]{2,1,0:T(8,128)(2,1)S(1)} %shard_map.100.mine_ref), channel_id=1, source_target_pairs={{0,4},{1,5},{2,6},{3,7},{4,0},{5,1},{6,2},{7,3},{8,12},{9,13},{10,... | collective-permute-start | bytes 1228808 | tf_op jit(solution)/shard_map/ppermute | solution.py:387
  4.2 20.4 %collective-permute-start.2 = (bf16[20,80,128]{2,1,0:T(8,128)(2,1)S(1)}, bf16[20,80,128]{2,1,0:T(8,128)(2,1)S(1)}, u32[]{:S(2)}, u32[]{:S(2)}) collective-permute-start(bf16[20,80,128]{2,1,0:T(8,128)(2,1)S(1)} %shard_map.100.mine_ref), channel_id=1, source_target_pairs={{0,8},{1,9},{2,10},{3,11},{4,12},{5,13},{6,14},{7,15},{8,0},{9,1},... | collective-permute-start | bytes 1228808 | tf_op jit(solution)/shard_map/ppermute | solution.py:387
  9.2 15.5 %collective-permute-start.1 = (bf16[20,80,128]{2,1,0:T(8,128)(2,1)S(1)}, bf16[20,80,128]{2,1,0:T(8,128)(2,1)S(1)}, u32[]{:S(2)}, u32[]{:S(2)}) collective-permute-start(bf16[20,80,128]{2,1,0:T(8,128)(2,1)S(1)} %get-tuple-element.23), channel_id=1, source_target_pairs={{0,1},{1,0},{2,3},{3,2},{4,5},{5,4},{6,7},{7,6},{8,9},{9,8},{10,11... | collective-permute-start | bytes 1228808 | tf_op jit(solution)/shard_map/ppermute | solution.py:387
  10.4 15.5 %collective-permute-start.5 = (bf16[20,80,128]{2,1,0:T(8,128)(2,1)S(1)}, bf16[20,80,128]{2,1,0:T(8,128)(2,1)S(1)}, u32[]{:S(2)}, u32[]{:S(2)}) collective-permute-start(bf16[20,80,128]{2,1,0:T(8,128)(2,1)S(1)} %get-tuple-element.22.left_ref), channel_id=1, source_target_pairs={{0,2},{1,3},{2,0},{3,1},{4,6},{5,7},{6,4},{7,5},{8,10},{9,11},{10,... | collective-permute-start | bytes 1228808 | tf_op jit(solution)/shard_map/ppermute | solution.py:387
  24.6 10.7 %collective-permute-start.7 = (bf16[20,80,128]{2,1,0:T(8,128)(2,1)S(1)}, bf16[20,80,128]{2,1,0:T(8,128)(2,1)S(1)}, u32[]{:S(2)}, u32[]{:S(2)}) collective-permute-start(bf16[20,80,128]{2,1,0:T(8,128)(2,1)S(1)} %collective-permute-done.2.pair_ref), channel_id=1, source_target_pairs={{0,5},{1,0},{2,7},{3,2},{4,1},{5,4},{6,3},{7,6},{8,9},{9,12},{10,1... | collective-permute-start | bytes 1228808 | tf_op jit(solution)/shard_map/ppermute | solution.py:387
  25.9 9.5 %collective-permute-start.4 = (bf16[20,80,128]{2,1,0:T(8,128)(2,1)S(1)}, bf16[20,80,128]{2,1,0:T(8,128)(2,1)S(1)}, u32[]{:S(2)}, u32[]{:S(2)}) collective-permute-start(bf16[20,80,128]{2,1,0:T(8,128)(2,1)S(1)} %collective-permute-done.2.pair_ref), channel_id=1, source_target_pairs={{0,2},{1,5},{2,0},{3,7},{4,6},{5,1},{6,4},{7,3},{8,12},{9,11},{10,... | collective-permute-start | bytes 1228808 | tf_op jit(solution)/shard_map/ppermute | solution.py:387
  30.9 9.8 %collective-permute-start.10 = (bf16[10,40,128]{2,1,0:T(8,128)(2,1)S(1)}, bf16[10,40,128]{2,1,0:T(8,128)(2,1)S(1)}, u32[]{:S(2)}, u32[]{:S(2)}) collective-permute-start(bf16[10,40,128]{2,1,0:T(8,128)(2,1)S(1)} %get-tuple-element.33), channel_id=1, source_target_pairs={{0,3},{1,2},{2,1},{3,0},{4,7},{5,6},{6,5},{7,4},{8,11},{9,10},{10,... | collective-permute-start | bytes 307208 | tf_op jit(solution)/shard_map/ppermute | solution.py:387
  32.1 9.3 %collective-permute-start.8 = (bf16[10,40,128]{2,1,0:T(8,128)(2,1)S(1)}, bf16[10,40,128]{2,1,0:T(8,128)(2,1)S(1)}, u32[]{:S(2)}, u32[]{:S(2)}) collective-permute-start(bf16[10,40,128]{2,1,0:T(8,128)(2,1)S(1)} %get-tuple-element.31), channel_id=1, source_target_pairs={{0,1},{1,0},{2,3},{3,2},{4,5},{5,4},{6,7},{7,6},{8,9},{9,8},{10,11... | collective-permute-start | bytes 307208 | tf_op jit(solution)/shard_map/ppermute | solution.py:387
  33.8 7.6 %collective-permute-start.9 = (bf16[10,40,128]{2,1,0:T(8,128)(2,1)S(1)}, bf16[10,40,128]{2,1,0:T(8,128)(2,1)S(1)}, u32[]{:S(2)}, u32[]{:S(2)}) collective-permute-start(bf16[10,40,128]{2,1,0:T(8,128)(2,1)S(1)} %get-tuple-element.32), channel_id=1, source_target_pairs={{0,2},{1,3},{2,0},{3,1},{4,6},{5,7},{6,4},{7,5},{8,10},{9,11},{10,... | collective-permute-start | bytes 307208 | tf_op jit(solution)/shard_map/ppermute | solution.py:387
  35.3 6.0 %copy-start.6 = (bf16[128,128]{1,0:T(8,128)(2,1)S(1)}, bf16[128,128]{1,0:T(8,128)(2,1)}, u32[]{:S(2)}) copy-start(bf16[128,128]{1,0:T(8,128)(2,1)} %proj_ref.7) | copy-start | bytes 98308
  35.4 7.0 %collective-permute-start.11 = (bf16[20,80,128]{2,1,0:T(8,128)(2,1)S(1)}, bf16[20,80,128]{2,1,0:T(8,128)(2,1)S(1)}, u32[]{:S(2)}, u32[]{:S(2)}) collective-permute-start(bf16[20,80,128]{2,1,0:T(8,128)(2,1)S(1)} %collective-permute-done.7.across_ref), channel_id=1, source_target_pairs={{0,2},{1,3},{2,0},{3,1},{4,6},{5,7},{6,4},{7,5},{8,10},{9,11},{10,... | collective-permute-start | bytes 1228808 | tf_op jit(solution)/shard_map/ppermute | solution.py:387
  37.7 4.6 %collective-permute-start.6 = (bf16[20,80,128]{2,1,0:T(8,128)(2,1)S(1)}, bf16[20,80,128]{2,1,0:T(8,128)(2,1)S(1)}, u32[]{:S(2)}, u32[]{:S(2)}) collective-permute-start(bf16[20,80,128]{2,1,0:T(8,128)(2,1)S(1)} %collective-permute-done.4.straight_ref), channel_id=1, source_target_pairs={{0,2},{1,3},{2,0},{3,1},{4,6},{5,7},{6,4},{7,5},{8,10},{9,11},{10,... | collective-permute-start | bytes 1228808 | tf_op jit(solution)/shard_map/ppermute | solution.py:387

commit v6 on v5

--- a/solution.py
+++ b/solution.py
@@ -147,6 +147,7 @@
     sum_ref,
     swap_ref,
     held_gain_ref,
+    wide_sums,
     right_wide,
 ):
     rows, cols, width = pair_ref.shape
@@ -159,7 +160,8 @@
     gating_ref[...] = jax.nn.sigmoid(
         jnp.dot(normed, out_gate_ref[...], preferred_element_type=jnp.float32)
     )
-    triangle(left_ref, [mine_ref, other_ref], sum_ref, right_wide)
+    triangle(left_ref, [mine_ref, other_ref], wide_sums, right_wide)
+    sum_ref[...] = wide_sums[...].astype(jnp.bfloat16)
     held_gain_ref[...] = hidden_gain_ref[...]
     keeps_near = flags_ref[3] == 1
 
@@ -169,8 +171,8 @@
 
     @pl.when(jnp.logical_not(keeps_near))
     def _():
-        swap_ref[:, : 2 * rows] = sum_ref[...]
-        swap_ref[:, 2 * rows :] = jnp.zeros((rows, cols - 2 * rows, width), jnp.bfloat16)
+        rest = jnp.zeros((rows, cols - 2 * rows, width), jnp.float32)
+        swap_ref[...] = jnp.concatenate([wide_sums[...], rest], axis=1).astype(jnp.bfloat16)
 
 
 def run_sums(count, length):
@@ -321,7 +323,7 @@
     )
     rows = out_ref.shape[0]
     keeps_near, odd = flags_ref[3] == 1, flags_ref[4]
-    near = near_ref[...].astype(jnp.float32) + given_ref[:, : 2 * rows].astype(jnp.float32)
+    near = near_ref[...].astype(jnp.float32) + given_ref[...].astype(jnp.float32)[:, : 2 * rows]
     own = jnp.where(keeps_near, near[:, :rows], mine_ref[...])
     partner = jnp.where(keeps_near, near[:, rows:], other_ref[...])
     at = jnp.where(keeps_near, odd, 1 - odd)
@@ -409,7 +411,7 @@
             bf16(rows, cols, width),
             f32(1, width),
         ),
-        wide(2),
+        [pltpu.VMEM(two, jnp.float32)] + wide(2),
     )(flags, pair_rep, mask, ln_gain, left_proj, left_gate, out_gate, right, from_core, hidden_gain)
     given = send(swap, over_col)
     left_other = send(left, over_core)

time: 46.9 us -> 46.9 us (level)
  no operation moved by 1% of the time
where the time goes in v6:
time: 46.9 us; the launch traced here: 46.4 us
  Pallas kernels  18.1 us (39%)
  waiting for transfers between devices  17.1 us (36%)
  starting transfers between devices  9.29 us (20%)
  local copies, waits for them, and re-layouts  1.78 us (4%)
    pallas_call x6, Pallas kernels, run(): pl.pallas_call(kernel, out_shape=out_shape, in_specs=[pl.BlockSpec(memory...  18.1 us
    ppermute x12, waiting for transfers between devices, exchanged(): send = lambda value, pairs: lax.ppermute(value, LINE, pairs)  17.1 us
    ppermute x12, starting transfers between devices, exchanged(): send = lambda value, pairs: lax.ppermute(value, LINE, pairs)  9.29 us
    unnamed x20, local copies, waits for them, and re-layouts  1.7 us
  transfers between devices with their start and end apart: 12, of which 5 were waited for; matrix products, arithmetic and copies ran while one was open for 0% of the time, Pallas kernels for 27%

profile of v6, /device:TPU:25, one launch (start us, length us, event | category | flops | bytes accessed | tf_op | source)
XLA Modules:
  0.0 46.4 jit_solution(11424619605729771537)
XLA Ops:
  0.0 0.0 copy-start.7
  0.0 0.0 copy-start.8
  0.0 0.0 copy-start.1
  0.0 0.0 copy-start.2
  0.1 0.1 stack.27.flags_ref
  0.1 0.5 %copy-done.7 = s32[160]{0:T(256)S(1)} copy-done((s32[160]{0:T(256)S(1)}, s32[160]{0:T(256)}, u32[]{:S(2)}) %copy-start.7) | copy-done | bytes 664
  0.7 0.0 copy-done.8
  0.7 0.1 copy-done.1
  0.8 0.0 copy-done.2
  0.8 0.0 copy-start
  0.8 1.0 %copy-done = bf16[20,80,128]{2,1,0:T(8,128)(2,1)S(1)} copy-done((bf16[20,80,128]{2,1,0:T(8,128)(2,1)S(1)}, bf16[20,80,128]{2,1,0:T(8,128)(2,1)}, u32[]{:S(2)}) %copy-start) | copy-done | bytes 409624
  1.8 0.0 copy-start.3
  1.8 1.5 %shard_map.100.mine_ref = bf16[20,80,128]{2,1,0:T(8,128)(2,1)S(1)} custom-call(s32[5]{0:T(128)S(1)} %stack.27.flags_ref, bf16[20,80,128]{2,1,0:T(8,128)(2,1)S(1)} %copy-done, s32[1,160]{1,0:T(1,128)S(1)} %bitcast.9, f32[1,128]{1,0:T(1,128)S(1)} %bitcast.11, bf16[128,128]{1,0:T(8,128)(2,1)S(1)} %copy-done.1, bf16[128,128]{1,0:T(8,128)(2,1)S(1)} %copy-done.2), custom_call_target="tpu_custom_call" | custom-call | flops 2420000000 | bytes 6600000 | tf_op jit(solution)/shard_map/pallas_call | solution.py:341
  3.3 0.0 copy-start.9
  3.3 0.7 %collective-permute-start = (bf16[20,80,128]{2,1,0:T(8,128)(2,1)S(1)}, bf16[20,80,128]{2,1,0:T(8,128)(2,1)S(1)}, u32[]{:S(2)}, u32[]{:S(2)}) collective-permute-start(bf16[20,80,128]{2,1,0:T(8,128)(2,1)S(1)} %shard_map.100.mine_ref), channel_id=1, source_target_pairs={{0,2},{1,3},{2,0},{3,1},{4,6},{5,7},{6,4},{7,5},{8,10},{9,11},{10,... | collective-permute-start | bytes 1228808 | tf_op jit(solution)/shard_map/ppermute | solution.py:389
  4.0 0.2 collective-permute-start.3
  4.2 0.0 collective-permute-start.2
  4.2 1.2 %collective-permute-done.other_ref = bf16[20,80,128]{2,1,0:T(8,128)(2,1)S(1)} collective-permute-done((bf16[20,80,128]{2,1,0:T(8,128)(2,1)S(1)}, bf16[20,80,128]{2,1,0:T(8,128)(2,1)S(1)}, u32[]{:S(2)}, u32[]{:S(2)}) %collective-permute-start) | collective-permute-done | bytes 409632 | tf_op jit(solution)/shard_map/ppermute | solution.py:389
  5.4 0.0 copy-done.3
  5.4 0.0 copy-done.4
  5.4 0.0 copy-done.5
  5.4 0.0 copy-done.9
  5.4 3.7 %shard_map.101 = (bf16[20,80,128]{2,1,0:T(8,128)(2,1)S(1)}, f32[1600,128]{1,0:T(8,128)S(1)}, bf16[20,40,128]{2,1,0:T(8,128)(2,1)S(1)}, bf16[20,80,128]{2,1,0:T(8,128)(2,1)S(1)}, f32[1,128]{1,0:T(1,128)S(1)}) custom-call(s32[5]{0:T(128)S(1)} %stack.27.flags_ref, bf16[20,80,128]{2,1,0:T(8,128)(2,1)S(1)} %copy-done, s32[1,160]{1,0:T(1,128)S(1)} %bitcast.10, ...), custom_call_target="tpu_custom_call" | custom-call | flops 4400000000 | bytes 12000000 | tf_op jit(solution)/shard_map/pallas_call | solution.py:341
  9.1 1.2 %collective-permute-start.1 = (bf16[20,80,128]{2,1,0:T(8,128)(2,1)S(1)}, bf16[20,80,128]{2,1,0:T(8,128)(2,1)S(1)}, u32[]{:S(2)}, u32[]{:S(2)}) collective-permute-start(bf16[20,80,128]{2,1,0:T(8,128)(2,1)S(1)} %get-tuple-element.23), channel_id=1, source_target_pairs={{0,1},{1,0},{2,3},{3,2},{4,5},{5,4},{6,7},{7,6},{8,9},{9,8},{10,11... | collective-permute-start | bytes 1228808 | tf_op jit(solution)/shard_map/ppermute | solution.py:389
  10.4 0.7 %collective-permute-start.5 = (bf16[20,80,128]{2,1,0:T(8,128)(2,1)S(1)}, bf16[20,80,128]{2,1,0:T(8,128)(2,1)S(1)}, u32[]{:S(2)}, u32[]{:S(2)}) collective-permute-start(bf16[20,80,128]{2,1,0:T(8,128)(2,1)S(1)} %get-tuple-element.22.left_ref), channel_id=1, source_target_pairs={{0,2},{1,3},{2,0},{3,1},{4,6},{5,7},{6,4},{7,5},{8,10},{9,11},{10,... | collective-permute-start | bytes 1228808 | tf_op jit(solution)/shard_map/ppermute | solution.py:389
  11.0 11.6 %collective-permute-done.3.next_ref = bf16[20,80,128]{2,1,0:T(8,128)(2,1)S(1)} collective-permute-done((bf16[20,80,128]{2,1,0:T(8,128)(2,1)S(1)}, bf16[20,80,128]{2,1,0:T(8,128)(2,1)S(1)}, u32[]{:S(2)}, u32[]{:S(2)}) %collective-permute-start.3) | collective-permute-done | bytes 409632 | tf_op jit(solution)/shard_map/ppermute | solution.py:389
  22.6 2.0 %collective-permute-done.2.pair_ref = bf16[20,80,128]{2,1,0:T(8,128)(2,1)S(1)} collective-permute-done((bf16[20,80,128]{2,1,0:T(8,128)(2,1)S(1)}, bf16[20,80,128]{2,1,0:T(8,128)(2,1)S(1)}, u32[]{:S(2)}, u32[]{:S(2)}) %collective-permute-start.2) | collective-permute-done | bytes 409632 | tf_op jit(solution)/shard_map/ppermute | solution.py:389
  24.6 0.0 collective-permute-done.1.given_ref
  24.6 1.2 %collective-permute-start.7 = (bf16[20,80,128]{2,1,0:T(8,128)(2,1)S(1)}, bf16[20,80,128]{2,1,0:T(8,128)(2,1)S(1)}, u32[]{:S(2)}, u32[]{:S(2)}) collective-permute-start(bf16[20,80,128]{2,1,0:T(8,128)(2,1)S(1)} %collective-permute-done.2.pair_ref), channel_id=1, source_target_pairs={{0,5},{1,0},{2,7},{3,2},{4,1},{5,4},{6,3},{7,6},{8,9},{9,12},{10,1... | collective-permute-start | bytes 1228808 | tf_op jit(solution)/shard_map/ppermute | solution.py:389
  25.9 0.0 collective-permute-start.4
  25.9 0.0 collective-permute-done.5.left_other
  25.9 5.1 %shard_map.102 = (bf16[10,40,128]{2,1,0:T(8,128)(2,1)S(1)}, bf16[10,40,128]{2,1,0:T(8,128)(2,1)S(1)}, bf16[10,40,128]{2,1,0:T(8,128)(2,1)S(1)}, bf16[10,40,128]{2,1,0:T(8,128)(2,1)S(1)}) custom-call(s32[5]{0:T(128)S(1)} %stack.27.flags_ref, bf16[20,80,128]{2,1,0:T(8,128)(2,1)S(1)} %get-tuple-element.22.left_ref, ...), custom_call_target="tpu_custom_call" | custom-call | flops 6270000128 | bytes 17100000 | tf_op jit(solution)/shard_map/pallas_call | solution.py:341
  30.9 1.1 %collective-permute-start.10 = (bf16[10,40,128]{2,1,0:T(8,128)(2,1)S(1)}, bf16[10,40,128]{2,1,0:T(8,128)(2,1)S(1)}, u32[]{:S(2)}, u32[]{:S(2)}) collective-permute-start(bf16[10,40,128]{2,1,0:T(8,128)(2,1)S(1)} %get-tuple-element.33), channel_id=1, source_target_pairs={{0,3},{1,2},{2,1},{3,0},{4,7},{5,6},{6,5},{7,4},{8,11},{9,10},{10,... | collective-permute-start | bytes 307208 | tf_op jit(solution)/shard_map/ppermute | solution.py:389
  32.1 1.7 %collective-permute-start.8 = (bf16[10,40,128]{2,1,0:T(8,128)(2,1)S(1)}, bf16[10,40,128]{2,1,0:T(8,128)(2,1)S(1)}, u32[]{:S(2)}, u32[]{:S(2)}) collective-permute-start(bf16[10,40,128]{2,1,0:T(8,128)(2,1)S(1)} %get-tuple-element.31), channel_id=1, source_target_pairs={{0,1},{1,0},{2,3},{3,2},{4,5},{5,4},{6,7},{7,6},{8,9},{9,8},{10,11... | collective-permute-start | bytes 307208 | tf_op jit(solution)/shard_map/ppermute | solution.py:389
  33.8 0.0 collective-permute-start.9
  33.8 1.5 %collective-permute-done.7.across_ref = bf16[20,80,128]{2,1,0:T(8,128)(2,1)S(1)} collective-permute-done((bf16[20,80,128]{2,1,0:T(8,128)(2,1)S(1)}, bf16[20,80,128]{2,1,0:T(8,128)(2,1)S(1)}, u32[]{:S(2)}, u32[]{:S(2)}) %collective-permute-start.7) | collective-permute-done | bytes 409632 | tf_op jit(solution)/shard_map/ppermute | solution.py:389
  35.3 0.0 collective-permute-done.4.straight_ref
  35.4 2.4 %collective-permute-start.11 = (bf16[20,80,128]{2,1,0:T(8,128)(2,1)S(1)}, bf16[20,80,128]{2,1,0:T(8,128)(2,1)S(1)}, u32[]{:S(2)}, u32[]{:S(2)}) collective-permute-start(bf16[20,80,128]{2,1,0:T(8,128)(2,1)S(1)} %collective-permute-done.7.across_ref), channel_id=1, source_target_pairs={{0,2},{1,3},{2,0},{3,1},{4,6},{5,7},{6,4},{7,5},{8,10},{9,11},{10,... | collective-permute-start | bytes 1228808 | tf_op jit(solution)/shard_map/ppermute | solution.py:389
  37.7 0.0 collective-permute-start.6
  37.8 2.9 %shard_map.103.mine_ref = f32[20,20,128]{2,1,0:T(8,128)S(1)} custom-call(s32[5]{0:T(128)S(1)} %stack.27.flags_ref, bf16[20,80,128]{2,1,0:T(8,128)(2,1)S(1)} %get-tuple-element.22.left_ref, bf16[20,80,128]{2,1,0:T(8,128)(2,1)S(1)} %collective-permute-done.1.given_ref, bf16[20,80,128]{2,1,0:T(8,128)(2,1)S(1)} %collective-permute-done.4.straight_ref, ...), custom_call_target="tpu_custom_call" | custom-call | flops 110000000 | bytes 300000 | tf_op jit(solution)/shard_map/pallas_call | solution.py:341
  40.7 0.0 collective-permute-done.10.partner_given
  40.7 0.7 %collective-permute-done.8.own_given = bf16[10,40,128]{2,1,0:T(8,128)(2,1)S(1)} collective-permute-done((bf16[10,40,128]{2,1,0:T(8,128)(2,1)S(1)}, bf16[10,40,128]{2,1,0:T(8,128)(2,1)S(1)}, u32[]{:S(2)}, u32[]{:S(2)}) %collective-permute-start.8) | collective-permute-done | bytes 102432 | tf_op jit(solution)/shard_map/ppermute | solution.py:389
  41.4 0.0 collective-permute-done.9.partner_ref
  41.4 0.0 copy-done.6
  41.4 1.0 %shard_map.104.done_ref = bf16[20,40,128]{2,1,0:T(8,128)(2,1)S(1)} custom-call(s32[5]{0:T(128)S(1)} %stack.27.flags_ref, bf16[10,40,128]{2,1,0:T(8,128)(2,1)S(1)} %get-tuple-element.30.own_ref, bf16[10,40,128]{2,1,0:T(8,128)(2,1)S(1)} %collective-permute-done.8.own_given, bf16[10,40,128]{2,1,0:T(8,128)(2,1)S(1)} %collective-permute-done.9.partner_ref, ...), custom_call_target="tpu_custom_call" | custom-call | flops 8800000000 | bytes 24000000 | tf_op jit(solution)/shard_map/pallas_call | solution.py:341
  42.3 0.0 collective-permute-done.11.across_ref
  42.3 0.0 collective-permute-done.6.straight_ref
  42.3 4.0 %shard_map.105 = bf16[20,80,128]{2,1,0:T(8,128)(2,1)} custom-call(s32[5]{0:T(128)S(1)} %stack.27.flags_ref, bf16[20,80,128]{2,1,0:T(8,128)(2,1)S(1)} %get-tuple-element.22.left_ref, bf16[20,80,128]{2,1,0:T(8,128)(2,1)S(1)} %collective-permute-done.1.given_ref, bf16[20,80,128]{2,1,0:T(8,128)(2,1)S(1)} %collective-permute-done.6.straight_ref, ...), custom_call_target="tpu_custom_call" | custom-call | flops 4400000000 | bytes 12000000 | tf_op jit(solution)/shard_map/pallas_call | solution.py:341
  (3 shorter events, 0.0 us)
Async XLA Ops:
  0.0 0.7 %copy-start.7 = (s32[160]{0:T(256)S(1)}, s32[160]{0:T(256)}, u32[]{:S(2)}) copy-start(s32[160]{0:T(256)} %param.11) | copy-start | bytes 1924
  0.0 0.7 %copy-start.8 = (f32[128]{0:T(128)S(1)}, f32[128]{0:T(128)}, u32[]{:S(2)}) copy-start(f32[128]{0:T(128)} %param.12) | copy-start | bytes 1540
  0.0 0.8 %copy-start.1 = (bf16[128,128]{1,0:T(8,128)(2,1)S(1)}, bf16[128,128]{1,0:T(8,128)(2,1)}, u32[]{:S(2)}) copy-start(bf16[128,128]{1,0:T(8,128)(2,1)} %proj_ref.4) | copy-start | bytes 98308
  0.0 0.8 %copy-start.2 = (bf16[128,128]{1,0:T(8,128)(2,1)S(1)}, bf16[128,128]{1,0:T(8,128)(2,1)}, u32[]{:S(2)}) copy-start(bf16[128,128]{1,0:T(8,128)(2,1)} %gate_ref.2) | copy-start | bytes 98308
  0.8 1.0 %copy-start = (bf16[20,80,128]{2,1,0:T(8,128)(2,1)S(1)}, bf16[20,80,128]{2,1,0:T(8,128)(2,1)}, u32[]{:S(2)}) copy-start(bf16[20,80,128]{2,1,0:T(8,128)(2,1)} %pair_ref.3) | copy-start | bytes 1228804
  1.8 3.6 %copy-start.3 = (bf16[128,128]{1,0:T(8,128)(2,1)S(1)}, bf16[128,128]{1,0:T(8,128)(2,1)}, u32[]{:S(2)}) copy-start(bf16[128,128]{1,0:T(8,128)(2,1)} %proj_ref.5) | copy-start | bytes 98308
  1.8 3.6 %copy-start.4 = (bf16[128,128]{1,0:T(8,128)(2,1)S(1)}, bf16[128,128]{1,0:T(8,128)(2,1)}, u32[]{:S(2)}) copy-start(bf16[128,128]{1,0:T(8,128)(2,1)} %gate_ref.3) | copy-start | bytes 98308
  1.8 3.6 %copy-start.5 = (bf16[128,128]{1,0:T(8,128)(2,1)S(1)}, bf16[128,128]{1,0:T(8,128)(2,1)}, u32[]{:S(2)}) copy-start(bf16[128,128]{1,0:T(8,128)(2,1)} %out_gate_ref.1) | copy-start | bytes 98308
  3.3 2.1 %copy-start.9 = (f32[128]{0:T(128)S(1)}, f32[128]{0:T(128)}, u32[]{:S(2)}) copy-start(f32[128]{0:T(128)} %param.17) | copy-start | bytes 1540
  3.3 2.1 %collective-permute-start = (bf16[20,80,128]{2,1,0:T(8,128)(2,1)S(1)}, bf16[20,80,128]{2,1,0:T(8,128)(2,1)S(1)}, u32[]{:S(2)}, u32[]{:S(2)}) collective-permute-start(bf16[20,80,128]{2,1,0:T(8,128)(2,1)S(1)} %shard_map.100.mine_ref), channel_id=1, source_target_pairs={{0,2},{1,3},{2,0},{3,1},{4,6},{5,7},{6,4},{7,5},{8,10},{9,11},{10,... | collective-permute-start | bytes 1228808 | tf_op jit(solution)/shard_map/ppermute | solution.py:389
  4.0 18.6 %collective-permute-start.3 = (bf16[20,80,128]{2,1,0:T(8,128)(2,1)S(1)}, bf16[20,80,128]{2,1,0:T(8,128)(2,1)S(1)}, u32[]{:S(2)}, u32[]{:S(2)}) collective-permute-start(bf16[20,80,128]{2,1,0:T(8,128)(2,1)S(1)} %shard_map.100.mine_ref), channel_id=1, source_target_pairs={{0,4},{1,5},{2,6},{3,7},{4,0},{5,1},{6,2},{7,3},{8,12},{9,13},{10,... | collective-permute-start | bytes 1228808 | tf_op jit(solution)/shard_map/ppermute | solution.py:389
  4.2 20.4 %collective-permute-start.2 = (bf16[20,80,128]{2,1,0:T(8,128)(2,1)S(1)}, bf16[20,80,128]{2,1,0:T(8,128)(2,1)S(1)}, u32[]{:S(2)}, u32[]{:S(2)}) collective-permute-start(bf16[20,80,128]{2,1,0:T(8,128)(2,1)S(1)} %shard_map.100.mine_ref), channel_id=1, source_target_pairs={{0,8},{1,9},{2,10},{3,11},{4,12},{5,13},{6,14},{7,15},{8,0},{9,1},... | collective-permute-start | bytes 1228808 | tf_op jit(solution)/shard_map/ppermute | solution.py:389
  9.1 15.5 %collective-permute-start.1 = (bf16[20,80,128]{2,1,0:T(8,128)(2,1)S(1)}, bf16[20,80,128]{2,1,0:T(8,128)(2,1)S(1)}, u32[]{:S(2)}, u32[]{:S(2)}) collective-permute-start(bf16[20,80,128]{2,1,0:T(8,128)(2,1)S(1)} %get-tuple-element.23), channel_id=1, source_target_pairs={{0,1},{1,0},{2,3},{3,2},{4,5},{5,4},{6,7},{7,6},{8,9},{9,8},{10,11... | collective-permute-start | bytes 1228808 | tf_op jit(solution)/shard_map/ppermute | solution.py:389
  10.4 15.5 %collective-permute-start.5 = (bf16[20,80,128]{2,1,0:T(8,128)(2,1)S(1)}, bf16[20,80,128]{2,1,0:T(8,128)(2,1)S(1)}, u32[]{:S(2)}, u32[]{:S(2)}) collective-permute-start(bf16[20,80,128]{2,1,0:T(8,128)(2,1)S(1)} %get-tuple-element.22.left_ref), channel_id=1, source_target_pairs={{0,2},{1,3},{2,0},{3,1},{4,6},{5,7},{6,4},{7,5},{8,10},{9,11},{10,... | collective-permute-start | bytes 1228808 | tf_op jit(solution)/shard_map/ppermute | solution.py:389
  24.6 10.7 %collective-permute-start.7 = (bf16[20,80,128]{2,1,0:T(8,128)(2,1)S(1)}, bf16[20,80,128]{2,1,0:T(8,128)(2,1)S(1)}, u32[]{:S(2)}, u32[]{:S(2)}) collective-permute-start(bf16[20,80,128]{2,1,0:T(8,128)(2,1)S(1)} %collective-permute-done.2.pair_ref), channel_id=1, source_target_pairs={{0,5},{1,0},{2,7},{3,2},{4,1},{5,4},{6,3},{7,6},{8,9},{9,12},{10,1... | collective-permute-start | bytes 1228808 | tf_op jit(solution)/shard_map/ppermute | solution.py:389
  25.9 9.5 %collective-permute-start.4 = (bf16[20,80,128]{2,1,0:T(8,128)(2,1)S(1)}, bf16[20,80,128]{2,1,0:T(8,128)(2,1)S(1)}, u32[]{:S(2)}, u32[]{:S(2)}) collective-permute-start(bf16[20,80,128]{2,1,0:T(8,128)(2,1)S(1)} %collective-permute-done.2.pair_ref), channel_id=1, source_target_pairs={{0,2},{1,5},{2,0},{3,7},{4,6},{5,1},{6,4},{7,3},{8,12},{9,11},{10,... | collective-permute-start | bytes 1228808 | tf_op jit(solution)/shard_map/ppermute | solution.py:389
  30.9 9.8 %collective-permute-start.10 = (bf16[10,40,128]{2,1,0:T(8,128)(2,1)S(1)}, bf16[10,40,128]{2,1,0:T(8,128)(2,1)S(1)}, u32[]{:S(2)}, u32[]{:S(2)}) collective-permute-start(bf16[10,40,128]{2,1,0:T(8,128)(2,1)S(1)} %get-tuple-element.33), channel_id=1, source_target_pairs={{0,3},{1,2},{2,1},{3,0},{4,7},{5,6},{6,5},{7,4},{8,11},{9,10},{10,... | collective-permute-start | bytes 307208 | tf_op jit(solution)/shard_map/ppermute | solution.py:389
  32.1 9.3 %collective-permute-start.8 = (bf16[10,40,128]{2,1,0:T(8,128)(2,1)S(1)}, bf16[10,40,128]{2,1,0:T(8,128)(2,1)S(1)}, u32[]{:S(2)}, u32[]{:S(2)}) collective-permute-start(bf16[10,40,128]{2,1,0:T(8,128)(2,1)S(1)} %get-tuple-element.31), channel_id=1, source_target_pairs={{0,1},{1,0},{2,3},{3,2},{4,5},{5,4},{6,7},{7,6},{8,9},{9,8},{10,11... | collective-permute-start | bytes 307208 | tf_op jit(solution)/shard_map/ppermute | solution.py:389
  33.8 7.6 %collective-permute-start.9 = (bf16[10,40,128]{2,1,0:T(8,128)(2,1)S(1)}, bf16[10,40,128]{2,1,0:T(8,128)(2,1)S(1)}, u32[]{:S(2)}, u32[]{:S(2)}) collective-permute-start(bf16[10,40,128]{2,1,0:T(8,128)(2,1)S(1)} %get-tuple-element.32), channel_id=1, source_target_pairs={{0,2},{1,3},{2,0},{3,1},{4,6},{5,7},{6,4},{7,5},{8,10},{9,11},{10,... | collective-permute-start | bytes 307208 | tf_op jit(solution)/shard_map/ppermute | solution.py:389
  35.3 6.0 %copy-start.6 = (bf16[128,128]{1,0:T(8,128)(2,1)S(1)}, bf16[128,128]{1,0:T(8,128)(2,1)}, u32[]{:S(2)}) copy-start(bf16[128,128]{1,0:T(8,128)(2,1)} %proj_ref.7) | copy-start | bytes 98308
  35.4 7.0 %collective-permute-start.11 = (bf16[20,80,128]{2,1,0:T(8,128)(2,1)S(1)}, bf16[20,80,128]{2,1,0:T(8,128)(2,1)S(1)}, u32[]{:S(2)}, u32[]{:S(2)}) collective-permute-start(bf16[20,80,128]{2,1,0:T(8,128)(2,1)S(1)} %collective-permute-done.7.across_ref), channel_id=1, source_target_pairs={{0,2},{1,3},{2,0},{3,1},{4,6},{5,7},{6,4},{7,5},{8,10},{9,11},{10,... | collective-permute-start | bytes 1228808 | tf_op jit(solution)/shard_map/ppermute | solution.py:389
  37.7 4.6 %collective-permute-start.6 = (bf16[20,80,128]{2,1,0:T(8,128)(2,1)S(1)}, bf16[20,80,128]{2,1,0:T(8,128)(2,1)S(1)}, u32[]{:S(2)}, u32[]{:S(2)}) collective-permute-start(bf16[20,80,128]{2,1,0:T(8,128)(2,1)S(1)} %collective-permute-done.4.straight_ref), channel_id=1, source_target_pairs={{0,2},{1,3},{2,0},{3,1},{4,6},{5,7},{6,4},{7,5},{8,10},{9,11},{10,... | collective-permute-start | bytes 1228808 | tf_op jit(solution)/shard_map/ppermute | solution.py:389

commit v7 on v6

--- a/solution.py
+++ b/solution.py
@@ -9,7 +9,7 @@
 
 LINE = ("row", "col")
 VMEM_LIMIT = 48 * 1024 * 1024
-VECTOR_ROWS = 16
+VECTOR_ROWS = 12
 PAIR = 2
 UNROLL = 10
 

time: 46.9 us -> 46.9 us (level)
  no operation moved by 1% of the time
where the time goes in v7:
time: 46.9 us; the launch traced here: 46.4 us
  Pallas kernels  18.2 us (39%)
  waiting for transfers between devices  17 us (36%)
  starting transfers between devices  9.3 us (20%)
  local copies, waits for them, and re-layouts  1.78 us (4%)
    pallas_call x6, Pallas kernels, run(): pl.pallas_call(kernel, out_shape=out_shape, in_specs=[pl.BlockSpec(memory...  18.2 us
    ppermute x12, waiting for transfers between devices, exchanged(): send = lambda value, pairs: lax.ppermute(value, LINE, pairs)  17 us
    ppermute x12, starting transfers between devices, exchanged(): send = lambda value, pairs: lax.ppermute(value, LINE, pairs)  9.3 us
    unnamed x20, local copies, waits for them, and re-layouts  1.7 us
  transfers between devices with their start and end apart: 12, of which 5 were waited for; matrix products, arithmetic and copies ran while one was open for 0% of the time, Pallas kernels for 27%

profile of v7, /device:TPU:25, one launch (start us, length us, event | category | flops | bytes accessed | tf_op | source)
XLA Modules:
  0.0 46.4 jit_solution(2598450079547068643)
XLA Ops:
  0.0 0.0 copy-start.7
  0.0 0.0 copy-start.8
  0.0 0.0 copy-start.1
  0.0 0.0 copy-start.2
  0.1 0.1 stack.27.flags_ref
  0.1 0.5 %copy-done.7 = s32[160]{0:T(256)S(1)} copy-done((s32[160]{0:T(256)S(1)}, s32[160]{0:T(256)}, u32[]{:S(2)}) %copy-start.7) | copy-done | bytes 664
  0.7 0.0 copy-done.8
  0.7 0.1 copy-done.1
  0.8 0.0 copy-done.2
  0.8 0.0 copy-start
  0.8 1.0 %copy-done = bf16[20,80,128]{2,1,0:T(8,128)(2,1)S(1)} copy-done((bf16[20,80,128]{2,1,0:T(8,128)(2,1)S(1)}, bf16[20,80,128]{2,1,0:T(8,128)(2,1)}, u32[]{:S(2)}) %copy-start) | copy-done | bytes 409624
  1.8 0.0 copy-start.3
  1.8 1.5 %shard_map.100.mine_ref = bf16[20,80,128]{2,1,0:T(8,128)(2,1)S(1)} custom-call(s32[5]{0:T(128)S(1)} %stack.27.flags_ref, bf16[20,80,128]{2,1,0:T(8,128)(2,1)S(1)} %copy-done, s32[1,160]{1,0:T(1,128)S(1)} %bitcast.9, f32[1,128]{1,0:T(1,128)S(1)} %bitcast.11, bf16[128,128]{1,0:T(8,128)(2,1)S(1)} %copy-done.1, bf16[128,128]{1,0:T(8,128)(2,1)S(1)} %copy-done.2), custom_call_target="tpu_custom_call" | custom-call | flops 2420000000 | bytes 6600000 | tf_op jit(solution)/shard_map/pallas_call | solution.py:341
  3.3 0.0 copy-start.9
  3.3 0.7 %collective-permute-start = (bf16[20,80,128]{2,1,0:T(8,128)(2,1)S(1)}, bf16[20,80,128]{2,1,0:T(8,128)(2,1)S(1)}, u32[]{:S(2)}, u32[]{:S(2)}) collective-permute-start(bf16[20,80,128]{2,1,0:T(8,128)(2,1)S(1)} %shard_map.100.mine_ref), channel_id=1, source_target_pairs={{0,2},{1,3},{2,0},{3,1},{4,6},{5,7},{6,4},{7,5},{8,10},{9,11},{10,... | collective-permute-start | bytes 1228808 | tf_op jit(solution)/shard_map/ppermute | solution.py:389
  4.0 0.2 collective-permute-start.3
  4.2 0.0 collective-permute-start.2
  4.2 1.2 %collective-permute-done.other_ref = bf16[20,80,128]{2,1,0:T(8,128)(2,1)S(1)} collective-permute-done((bf16[20,80,128]{2,1,0:T(8,128)(2,1)S(1)}, bf16[20,80,128]{2,1,0:T(8,128)(2,1)S(1)}, u32[]{:S(2)}, u32[]{:S(2)}) %collective-permute-start) | collective-permute-done | bytes 409632 | tf_op jit(solution)/shard_map/ppermute | solution.py:389
  5.4 0.0 copy-done.3
  5.4 0.0 copy-done.4
  5.4 0.0 copy-done.5
  5.4 0.0 copy-done.9
  5.4 3.8 %shard_map.101 = (bf16[20,80,128]{2,1,0:T(8,128)(2,1)S(1)}, f32[1600,128]{1,0:T(8,128)S(1)}, bf16[20,40,128]{2,1,0:T(8,128)(2,1)S(1)}, bf16[20,80,128]{2,1,0:T(8,128)(2,1)S(1)}, f32[1,128]{1,0:T(1,128)S(1)}) custom-call(s32[5]{0:T(128)S(1)} %stack.27.flags_ref, bf16[20,80,128]{2,1,0:T(8,128)(2,1)S(1)} %copy-done, s32[1,160]{1,0:T(1,128)S(1)} %bitcast.10, ...), custom_call_target="tpu_custom_call" | custom-call | flops 4400000000 | bytes 12000000 | tf_op jit(solution)/shard_map/pallas_call | solution.py:341
  9.2 1.2 %collective-permute-start.1 = (bf16[20,80,128]{2,1,0:T(8,128)(2,1)S(1)}, bf16[20,80,128]{2,1,0:T(8,128)(2,1)S(1)}, u32[]{:S(2)}, u32[]{:S(2)}) collective-permute-start(bf16[20,80,128]{2,1,0:T(8,128)(2,1)S(1)} %get-tuple-element.23), channel_id=1, source_target_pairs={{0,1},{1,0},{2,3},{3,2},{4,5},{5,4},{6,7},{7,6},{8,9},{9,8},{10,11... | collective-permute-start | bytes 1228808 | tf_op jit(solution)/shard_map/ppermute | solution.py:389
  10.4 0.7 %collective-permute-start.5 = (bf16[20,80,128]{2,1,0:T(8,128)(2,1)S(1)}, bf16[20,80,128]{2,1,0:T(8,128)(2,1)S(1)}, u32[]{:S(2)}, u32[]{:S(2)}) collective-permute-start(bf16[20,80,128]{2,1,0:T(8,128)(2,1)S(1)} %get-tuple-element.22.left_ref), channel_id=1, source_target_pairs={{0,2},{1,3},{2,0},{3,1},{4,6},{5,7},{6,4},{7,5},{8,10},{9,11},{10,... | collective-permute-start | bytes 1228808 | tf_op jit(solution)/shard_map/ppermute | solution.py:389
  11.1 11.5 %collective-permute-done.3.next_ref = bf16[20,80,128]{2,1,0:T(8,128)(2,1)S(1)} collective-permute-done((bf16[20,80,128]{2,1,0:T(8,128)(2,1)S(1)}, bf16[20,80,128]{2,1,0:T(8,128)(2,1)S(1)}, u32[]{:S(2)}, u32[]{:S(2)}) %collective-permute-start.3) | collective-permute-done | bytes 409632 | tf_op jit(solution)/shard_map/ppermute | solution.py:389
  22.6 2.0 %collective-permute-done.2.pair_ref = bf16[20,80,128]{2,1,0:T(8,128)(2,1)S(1)} collective-permute-done((bf16[20,80,128]{2,1,0:T(8,128)(2,1)S(1)}, bf16[20,80,128]{2,1,0:T(8,128)(2,1)S(1)}, u32[]{:S(2)}, u32[]{:S(2)}) %collective-permute-start.2) | collective-permute-done | bytes 409632 | tf_op jit(solution)/shard_map/ppermute | solution.py:389
  24.6 0.0 collective-permute-done.1.given_ref
  24.6 1.2 %collective-permute-start.7 = (bf16[20,80,128]{2,1,0:T(8,128)(2,1)S(1)}, bf16[20,80,128]{2,1,0:T(8,128)(2,1)S(1)}, u32[]{:S(2)}, u32[]{:S(2)}) collective-permute-start(bf16[20,80,128]{2,1,0:T(8,128)(2,1)S(1)} %collective-permute-done.2.pair_ref), channel_id=1, source_target_pairs={{0,5},{1,0},{2,7},{3,2},{4,1},{5,4},{6,3},{7,6},{8,9},{9,12},{10,1... | collective-permute-start | bytes 1228808 | tf_op jit(solution)/shard_map/ppermute | solution.py:389
  25.9 0.0 collective-permute-start.4
  25.9 0.0 collective-permute-done.5.left_other
  25.9 4.9 %shard_map.102 = (bf16[10,40,128]{2,1,0:T(8,128)(2,1)S(1)}, bf16[10,40,128]{2,1,0:T(8,128)(2,1)S(1)}, bf16[10,40,128]{2,1,0:T(8,128)(2,1)S(1)}, bf16[10,40,128]{2,1,0:T(8,128)(2,1)S(1)}) custom-call(s32[5]{0:T(128)S(1)} %stack.27.flags_ref, bf16[20,80,128]{2,1,0:T(8,128)(2,1)S(1)} %get-tuple-element.22.left_ref, ...), custom_call_target="tpu_custom_call" | custom-call | flops 6270000128 | bytes 17100000 | tf_op jit(solution)/shard_map/pallas_call | solution.py:341
  30.8 1.1 %collective-permute-start.10 = (bf16[10,40,128]{2,1,0:T(8,128)(2,1)S(1)}, bf16[10,40,128]{2,1,0:T(8,128)(2,1)S(1)}, u32[]{:S(2)}, u32[]{:S(2)}) collective-permute-start(bf16[10,40,128]{2,1,0:T(8,128)(2,1)S(1)} %get-tuple-element.33), channel_id=1, source_target_pairs={{0,3},{1,2},{2,1},{3,0},{4,7},{5,6},{6,5},{7,4},{8,11},{9,10},{10,... | collective-permute-start | bytes 307208 | tf_op jit(solution)/shard_map/ppermute | solution.py:389
  31.9 1.7 %collective-permute-start.8 = (bf16[10,40,128]{2,1,0:T(8,128)(2,1)S(1)}, bf16[10,40,128]{2,1,0:T(8,128)(2,1)S(1)}, u32[]{:S(2)}, u32[]{:S(2)}) collective-permute-start(bf16[10,40,128]{2,1,0:T(8,128)(2,1)S(1)} %get-tuple-element.31), channel_id=1, source_target_pairs={{0,1},{1,0},{2,3},{3,2},{4,5},{5,4},{6,7},{7,6},{8,9},{9,8},{10,11... | collective-permute-start | bytes 307208 | tf_op jit(solution)/shard_map/ppermute | solution.py:389
  33.7 0.0 collective-permute-start.9
  33.7 1.7 %collective-permute-done.7.across_ref = bf16[20,80,128]{2,1,0:T(8,128)(2,1)S(1)} collective-permute-done((bf16[20,80,128]{2,1,0:T(8,128)(2,1)S(1)}, bf16[20,80,128]{2,1,0:T(8,128)(2,1)S(1)}, u32[]{:S(2)}, u32[]{:S(2)}) %collective-permute-start.7) | collective-permute-done | bytes 409632 | tf_op jit(solution)/shard_map/ppermute | solution.py:389
  35.3 0.0 collective-permute-done.4.straight_ref
  35.4 2.4 %collective-permute-start.11 = (bf16[20,80,128]{2,1,0:T(8,128)(2,1)S(1)}, bf16[20,80,128]{2,1,0:T(8,128)(2,1)S(1)}, u32[]{:S(2)}, u32[]{:S(2)}) collective-permute-start(bf16[20,80,128]{2,1,0:T(8,128)(2,1)S(1)} %collective-permute-done.7.across_ref), channel_id=1, source_target_pairs={{0,2},{1,3},{2,0},{3,1},{4,6},{5,7},{6,4},{7,5},{8,10},{9,11},{10,... | collective-permute-start | bytes 1228808 | tf_op jit(solution)/shard_map/ppermute | solution.py:389
  37.7 0.0 collective-permute-start.6
  37.8 3.0 %shard_map.103.mine_ref = f32[20,20,128]{2,1,0:T(8,128)S(1)} custom-call(s32[5]{0:T(128)S(1)} %stack.27.flags_ref, bf16[20,80,128]{2,1,0:T(8,128)(2,1)S(1)} %get-tuple-element.22.left_ref, bf16[20,80,128]{2,1,0:T(8,128)(2,1)S(1)} %collective-permute-done.1.given_ref, bf16[20,80,128]{2,1,0:T(8,128)(2,1)S(1)} %collective-permute-done.4.straight_ref, ...), custom_call_target="tpu_custom_call" | custom-call | flops 110000000 | bytes 300000 | tf_op jit(solution)/shard_map/pallas_call | solution.py:341
  40.8 0.0 collective-permute-done.10.partner_given
  40.8 0.6 %collective-permute-done.8.own_given = bf16[10,40,128]{2,1,0:T(8,128)(2,1)S(1)} collective-permute-done((bf16[10,40,128]{2,1,0:T(8,128)(2,1)S(1)}, bf16[10,40,128]{2,1,0:T(8,128)(2,1)S(1)}, u32[]{:S(2)}, u32[]{:S(2)}) %collective-permute-start.8) | collective-permute-done | bytes 102432 | tf_op jit(solution)/shard_map/ppermute | solution.py:389
  41.4 0.0 collective-permute-done.9.partner_ref
  41.4 0.0 copy-done.6
  41.4 1.0 %shard_map.104.done_ref = bf16[20,40,128]{2,1,0:T(8,128)(2,1)S(1)} custom-call(s32[5]{0:T(128)S(1)} %stack.27.flags_ref, bf16[10,40,128]{2,1,0:T(8,128)(2,1)S(1)} %get-tuple-element.30.own_ref, bf16[10,40,128]{2,1,0:T(8,128)(2,1)S(1)} %collective-permute-done.8.own_given, bf16[10,40,128]{2,1,0:T(8,128)(2,1)S(1)} %collective-permute-done.9.partner_ref, ...), custom_call_target="tpu_custom_call" | custom-call | flops 8800000000 | bytes 24000000 | tf_op jit(solution)/shard_map/pallas_call | solution.py:341
  42.3 0.0 collective-permute-done.11.across_ref
  42.3 0.0 collective-permute-done.6.straight_ref
  42.3 4.1 %shard_map.105 = bf16[20,80,128]{2,1,0:T(8,128)(2,1)} custom-call(s32[5]{0:T(128)S(1)} %stack.27.flags_ref, bf16[20,80,128]{2,1,0:T(8,128)(2,1)S(1)} %get-tuple-element.22.left_ref, bf16[20,80,128]{2,1,0:T(8,128)(2,1)S(1)} %collective-permute-done.1.given_ref, bf16[20,80,128]{2,1,0:T(8,128)(2,1)S(1)} %collective-permute-done.6.straight_ref, ...), custom_call_target="tpu_custom_call" | custom-call | flops 4400000000 | bytes 12000000 | tf_op jit(solution)/shard_map/pallas_call | solution.py:341
  (3 shorter events, 0.0 us)
Async XLA Ops:
  0.0 0.7 %copy-start.7 = (s32[160]{0:T(256)S(1)}, s32[160]{0:T(256)}, u32[]{:S(2)}) copy-start(s32[160]{0:T(256)} %param.11) | copy-start | bytes 1924
  0.0 0.7 %copy-start.8 = (f32[128]{0:T(128)S(1)}, f32[128]{0:T(128)}, u32[]{:S(2)}) copy-start(f32[128]{0:T(128)} %param.12) | copy-start | bytes 1540
  0.0 0.8 %copy-start.1 = (bf16[128,128]{1,0:T(8,128)(2,1)S(1)}, bf16[128,128]{1,0:T(8,128)(2,1)}, u32[]{:S(2)}) copy-start(bf16[128,128]{1,0:T(8,128)(2,1)} %proj_ref.4) | copy-start | bytes 98308
  0.0 0.8 %copy-start.2 = (bf16[128,128]{1,0:T(8,128)(2,1)S(1)}, bf16[128,128]{1,0:T(8,128)(2,1)}, u32[]{:S(2)}) copy-start(bf16[128,128]{1,0:T(8,128)(2,1)} %gate_ref.2) | copy-start | bytes 98308
  0.8 1.0 %copy-start = (bf16[20,80,128]{2,1,0:T(8,128)(2,1)S(1)}, bf16[20,80,128]{2,1,0:T(8,128)(2,1)}, u32[]{:S(2)}) copy-start(bf16[20,80,128]{2,1,0:T(8,128)(2,1)} %pair_ref.3) | copy-start | bytes 1228804
  1.8 3.6 %copy-start.3 = (bf16[128,128]{1,0:T(8,128)(2,1)S(1)}, bf16[128,128]{1,0:T(8,128)(2,1)}, u32[]{:S(2)}) copy-start(bf16[128,128]{1,0:T(8,128)(2,1)} %proj_ref.5) | copy-start | bytes 98308
  1.8 3.6 %copy-start.4 = (bf16[128,128]{1,0:T(8,128)(2,1)S(1)}, bf16[128,128]{1,0:T(8,128)(2,1)}, u32[]{:S(2)}) copy-start(bf16[128,128]{1,0:T(8,128)(2,1)} %gate_ref.3) | copy-start | bytes 98308
  1.8 3.6 %copy-start.5 = (bf16[128,128]{1,0:T(8,128)(2,1)S(1)}, bf16[128,128]{1,0:T(8,128)(2,1)}, u32[]{:S(2)}) copy-start(bf16[128,128]{1,0:T(8,128)(2,1)} %out_gate_ref.1) | copy-start | bytes 98308
  3.3 2.1 %copy-start.9 = (f32[128]{0:T(128)S(1)}, f32[128]{0:T(128)}, u32[]{:S(2)}) copy-start(f32[128]{0:T(128)} %param.17) | copy-start | bytes 1540
  3.3 2.1 %collective-permute-start = (bf16[20,80,128]{2,1,0:T(8,128)(2,1)S(1)}, bf16[20,80,128]{2,1,0:T(8,128)(2,1)S(1)}, u32[]{:S(2)}, u32[]{:S(2)}) collective-permute-start(bf16[20,80,128]{2,1,0:T(8,128)(2,1)S(1)} %shard_map.100.mine_ref), channel_id=1, source_target_pairs={{0,2},{1,3},{2,0},{3,1},{4,6},{5,7},{6,4},{7,5},{8,10},{9,11},{10,... | collective-permute-start | bytes 1228808 | tf_op jit(solution)/shard_map/ppermute | solution.py:389
  4.0 18.6 %collective-permute-start.3 = (bf16[20,80,128]{2,1,0:T(8,128)(2,1)S(1)}, bf16[20,80,128]{2,1,0:T(8,128)(2,1)S(1)}, u32[]{:S(2)}, u32[]{:S(2)}) collective-permute-start(bf16[20,80,128]{2,1,0:T(8,128)(2,1)S(1)} %shard_map.100.mine_ref), channel_id=1, source_target_pairs={{0,4},{1,5},{2,6},{3,7},{4,0},{5,1},{6,2},{7,3},{8,12},{9,13},{10,... | collective-permute-start | bytes 1228808 | tf_op jit(solution)/shard_map/ppermute | solution.py:389
  4.2 20.4 %collective-permute-start.2 = (bf16[20,80,128]{2,1,0:T(8,128)(2,1)S(1)}, bf16[20,80,128]{2,1,0:T(8,128)(2,1)S(1)}, u32[]{:S(2)}, u32[]{:S(2)}) collective-permute-start(bf16[20,80,128]{2,1,0:T(8,128)(2,1)S(1)} %shard_map.100.mine_ref), channel_id=1, source_target_pairs={{0,8},{1,9},{2,10},{3,11},{4,12},{5,13},{6,14},{7,15},{8,0},{9,1},... | collective-permute-start | bytes 1228808 | tf_op jit(solution)/shard_map/ppermute | solution.py:389
  9.2 15.5 %collective-permute-start.1 = (bf16[20,80,128]{2,1,0:T(8,128)(2,1)S(1)}, bf16[20,80,128]{2,1,0:T(8,128)(2,1)S(1)}, u32[]{:S(2)}, u32[]{:S(2)}) collective-permute-start(bf16[20,80,128]{2,1,0:T(8,128)(2,1)S(1)} %get-tuple-element.23), channel_id=1, source_target_pairs={{0,1},{1,0},{2,3},{3,2},{4,5},{5,4},{6,7},{7,6},{8,9},{9,8},{10,11... | collective-permute-start | bytes 1228808 | tf_op jit(solution)/shard_map/ppermute | solution.py:389
  10.4 15.4 %collective-permute-start.5 = (bf16[20,80,128]{2,1,0:T(8,128)(2,1)S(1)}, bf16[20,80,128]{2,1,0:T(8,128)(2,1)S(1)}, u32[]{:S(2)}, u32[]{:S(2)}) collective-permute-start(bf16[20,80,128]{2,1,0:T(8,128)(2,1)S(1)} %get-tuple-element.22.left_ref), channel_id=1, source_target_pairs={{0,2},{1,3},{2,0},{3,1},{4,6},{5,7},{6,4},{7,5},{8,10},{9,11},{10,... | collective-permute-start | bytes 1228808 | tf_op jit(solution)/shard_map/ppermute | solution.py:389
  24.6 10.7 %collective-permute-start.7 = (bf16[20,80,128]{2,1,0:T(8,128)(2,1)S(1)}, bf16[20,80,128]{2,1,0:T(8,128)(2,1)S(1)}, u32[]{:S(2)}, u32[]{:S(2)}) collective-permute-start(bf16[20,80,128]{2,1,0:T(8,128)(2,1)S(1)} %collective-permute-done.2.pair_ref), channel_id=1, source_target_pairs={{0,5},{1,0},{2,7},{3,2},{4,1},{5,4},{6,3},{7,6},{8,9},{9,12},{10,1... | collective-permute-start | bytes 1228808 | tf_op jit(solution)/shard_map/ppermute | solution.py:389
  25.9 9.5 %collective-permute-start.4 = (bf16[20,80,128]{2,1,0:T(8,128)(2,1)S(1)}, bf16[20,80,128]{2,1,0:T(8,128)(2,1)S(1)}, u32[]{:S(2)}, u32[]{:S(2)}) collective-permute-start(bf16[20,80,128]{2,1,0:T(8,128)(2,1)S(1)} %collective-permute-done.2.pair_ref), channel_id=1, source_target_pairs={{0,2},{1,5},{2,0},{3,7},{4,6},{5,1},{6,4},{7,3},{8,12},{9,11},{10,... | collective-permute-start | bytes 1228808 | tf_op jit(solution)/shard_map/ppermute | solution.py:389
  30.8 10.0 %collective-permute-start.10 = (bf16[10,40,128]{2,1,0:T(8,128)(2,1)S(1)}, bf16[10,40,128]{2,1,0:T(8,128)(2,1)S(1)}, u32[]{:S(2)}, u32[]{:S(2)}) collective-permute-start(bf16[10,40,128]{2,1,0:T(8,128)(2,1)S(1)} %get-tuple-element.33), channel_id=1, source_target_pairs={{0,3},{1,2},{2,1},{3,0},{4,7},{5,6},{6,5},{7,4},{8,11},{9,10},{10,... | collective-permute-start | bytes 307208 | tf_op jit(solution)/shard_map/ppermute | solution.py:389
  31.9 9.4 %collective-permute-start.8 = (bf16[10,40,128]{2,1,0:T(8,128)(2,1)S(1)}, bf16[10,40,128]{2,1,0:T(8,128)(2,1)S(1)}, u32[]{:S(2)}, u32[]{:S(2)}) collective-permute-start(bf16[10,40,128]{2,1,0:T(8,128)(2,1)S(1)} %get-tuple-element.31), channel_id=1, source_target_pairs={{0,1},{1,0},{2,3},{3,2},{4,5},{5,4},{6,7},{7,6},{8,9},{9,8},{10,11... | collective-permute-start | bytes 307208 | tf_op jit(solution)/shard_map/ppermute | solution.py:389
  33.7 7.7 %collective-permute-start.9 = (bf16[10,40,128]{2,1,0:T(8,128)(2,1)S(1)}, bf16[10,40,128]{2,1,0:T(8,128)(2,1)S(1)}, u32[]{:S(2)}, u32[]{:S(2)}) collective-permute-start(bf16[10,40,128]{2,1,0:T(8,128)(2,1)S(1)} %get-tuple-element.32), channel_id=1, source_target_pairs={{0,2},{1,3},{2,0},{3,1},{4,6},{5,7},{6,4},{7,5},{8,10},{9,11},{10,... | collective-permute-start | bytes 307208 | tf_op jit(solution)/shard_map/ppermute | solution.py:389
  35.3 6.0 %copy-start.6 = (bf16[128,128]{1,0:T(8,128)(2,1)S(1)}, bf16[128,128]{1,0:T(8,128)(2,1)}, u32[]{:S(2)}) copy-start(bf16[128,128]{1,0:T(8,128)(2,1)} %proj_ref.7) | copy-start | bytes 98308
  35.4 7.0 %collective-permute-start.11 = (bf16[20,80,128]{2,1,0:T(8,128)(2,1)S(1)}, bf16[20,80,128]{2,1,0:T(8,128)(2,1)S(1)}, u32[]{:S(2)}, u32[]{:S(2)}) collective-permute-start(bf16[20,80,128]{2,1,0:T(8,128)(2,1)S(1)} %collective-permute-done.7.across_ref), channel_id=1, source_target_pairs={{0,2},{1,3},{2,0},{3,1},{4,6},{5,7},{6,4},{7,5},{8,10},{9,11},{10,... | collective-permute-start | bytes 1228808 | tf_op jit(solution)/shard_map/ppermute | solution.py:389
  37.7 4.6 %collective-permute-start.6 = (bf16[20,80,128]{2,1,0:T(8,128)(2,1)S(1)}, bf16[20,80,128]{2,1,0:T(8,128)(2,1)S(1)}, u32[]{:S(2)}, u32[]{:S(2)}) collective-permute-start(bf16[20,80,128]{2,1,0:T(8,128)(2,1)S(1)} %collective-permute-done.4.straight_ref), channel_id=1, source_target_pairs={{0,2},{1,3},{2,0},{3,1},{4,6},{5,7},{6,4},{7,5},{8,10},{9,11},{10,... | collective-permute-start | bytes 1228808 | tf_op jit(solution)/shard_map/ppermute | solution.py:389
